TPU v7x, 32 devices: a whole 2x2x4 slice. The times are simulated.
32 devices in a mesh: groups: 2 (over y), member: 4 (over x, core), band: 4 (over z).
Axes of the slice: x: 2, y: 2, z: 4, core: 2. Of those that a mesh axis runs over, the one named last changes fastest.
Arguments:
- latent: bfloat16 [8, 256, 1024], P(('groups', 'member'), 'band'), parts along dimension 0, may hold values from -6 to 6
- coef_table: bfloat16 [16, 1024], replicated, may hold values from 0.25 to 2
- out_proj: bfloat16 [25, 1024], replicated, may hold values from -0.1875 to 0.1875
- target: float32 [25, 2048], P(None, ('groups', 'band')), parts along dimension 1, may hold values from -12 to 12
- cell_area: float32 [1024], P('band'), may hold values from 0.2 to 2
- var_weight: float32 [25], replicated, may hold values from 0.5 to 4
- edge_source: int32 [4, 4, 384], replicated, may hold values from 0 to 63
- edge_target: int32 [4, 4, 384], P(None, 'band'), may hold values from 0 to 256, as said below
- edge_weight: int32 [4, 4, 384], replicated, may hold values from 0 to 15
Outputs:
- latent_grad: bfloat16 [8, 256, 1024], P(('groups', 'member'), 'band'), parts along dimension 0
- proj_grad: float32 [50, 1024], P('groups'), parts along dimension 0
- coef_grad: float32 [32, 1024], P('groups'), parts along dimension 0
- mean_loss: float32 [2], P('groups'), parts along dimension 0
There are 2 independent parts, one for each index of `groups`. A program takes and returns all parts, laid end to end along the dimension named above; an argument that names none is the same for every part. Nothing has to cross between parts.
Inputs may be any that keep to these rules, and one draw needn't show every extreme that they name: `edge_target`: A value of 256 marks an unused slot; in each block (s, d) the used slots come first. Every cell of a band is the target of exactly 4 used slots over all source bands. A target band receives at most 384 used slots from one source band, and exactly 384 from some source band.
All inputs are finite; a program needn't handle non-finite values.
Results may differ from a plain program's by a relative error of at most 0.012.
The roundings to bfloat16 on the way count: a program that leaves them out, or rounds other values in their place, can miss the bound.
Values may be sent and summed in bfloat16 or wider, within the bound.
No kernel may reach another device: no remote copies, remote signals or barrier semaphores. Data moves between devices by JAX's collectives and lax.ppermute only.
A program may use at most 64 MiB of HBM per device.

v0:
```python
import math

import jax
import jax.numpy as jnp
from jax import lax
from jax.sharding import PartitionSpec as P

K = 4


FAIR_ALPHA = 0.95
SOFTNESS = 0.1
EXACT = lax.Precision.HIGHEST


def from_behind(shard, axis, by):
    peers = lax.axis_size(axis)
    return lax.ppermute(shard, axis, [(i, (i + by) % peers) for i in range(peers)])


def soft_abs(values):
    return jnp.sqrt(values * values + SOFTNESS * SOFTNESS) - SOFTNESS


def soft_slope(values):
    return values / jnp.sqrt(values * values + SOFTNESS * SOFTNESS)


def contract(left, right, left_dim, right_dim):
    return lax.dot_general(
        left,
        right,
        (((left_dim,), (right_dim,)), ((), ())),
        precision=EXACT,
        preferred_element_type=jnp.float32,
    )


def local(
    latent,
    coef_table,
    out_proj,
    target,
    cell_area,
    var_weight,
    edge_source,
    edge_target,
    edge_weight,
):
    latent_rows = latent[0]
    row_count = latent_rows.shape[0]
    hidden = latent_rows.shape[1]
    bands = lax.axis_size("band")
    members = lax.axis_size("member")
    band_here = lax.axis_index("band")
    variables = target.shape[0]
    cells_dev = target.shape[1]
    cells_all = cells_dev * bands
    target_ids = edge_target[:, 0, :].reshape(-1)
    table_rows = coef_table.shape[0]
    source_ids = lax.dynamic_index_in_dim(edge_source, band_here, 0, keepdims=False).reshape(-1)
    weight_ids = lax.dynamic_index_in_dim(edge_weight, band_here, 0, keepdims=False).reshape(-1)
    pick_weight = jnp.arange(table_rows)[:, None] == weight_ids[None, :]
    edge_scale = lax.dot_general(
        pick_weight.astype(jnp.bfloat16),
        coef_table,
        (((0,), (0,)), ((), ())),
        preferred_element_type=jnp.float32,
    ).astype(jnp.bfloat16)
    scale_wide = edge_scale.astype(jnp.float32)
    gathered_rows = latent_rows[source_ids]
    messages = (gathered_rows.astype(jnp.float32) * scale_wide).astype(jnp.bfloat16)
    proj_wide = out_proj.astype(jnp.float32)
    cell_iota = jnp.arange(cells_dev)
    into_cell = (cell_iota[:, None] == target_ids[None, :]).astype(jnp.bfloat16)
    arrived = lax.all_to_all(
        messages.reshape(bands, -1, hidden), "band", split_axis=0, concat_axis=0, tiled=True
    ).reshape(-1, hidden)
    aggregate = jnp.dot(into_cell, arrived, preferred_element_type=jnp.float32)
    predicted = contract(proj_wide, aggregate, 1, 1)
    weights = var_weight[:, None] * cell_area[None, :]
    error = predicted - target
    pair_coef = FAIR_ALPHA / (members - 1) + (1.0 - FAIR_ALPHA) / members
    own_slopes = jnp.zeros_like(predicted)
    spread = jnp.zeros_like(predicted)
    moving = predicted
    owed = jnp.zeros_like(predicted)
    for offset in range(1, members // 2 + 1):
        moving, owed = from_behind((moving, owed), "member", 1)
        gap_value = predicted - moving
        gap_slope = soft_slope(gap_value)
        own_slopes = own_slopes + gap_slope
        if 2 * offset == members:
            spread = spread + 0.5 * soft_abs(gap_value)
        else:
            spread = spread + soft_abs(gap_value)
            owed = owed - gap_slope
    returned = from_behind(owed, "member", members // 2)
    slope_total = own_slopes + returned
    loss_part = jnp.sum(weights * (soft_abs(error) - pair_coef * spread))
    grad_pred = weights * (soft_slope(error) - pair_coef * slope_total)
    cell_grad = contract(grad_pred, proj_wide, 0, 0).astype(jnp.bfloat16)
    slot_grad = lax.dot_general(
        into_cell, cell_grad, (((0,), (0,)), ((), ())), preferred_element_type=jnp.float32
    ).astype(jnp.bfloat16)
    returned_grad = lax.all_to_all(
        slot_grad.reshape(bands, -1, hidden), "band", split_axis=0, concat_axis=0, tiled=True
    ).reshape(-1, hidden)
    proj_part = jnp.dot(grad_pred, aggregate, precision=EXACT)
    grad_wide = returned_grad.astype(jnp.float32)
    weighted = grad_wide * scale_wide
    into_row = (jnp.arange(row_count)[:, None] == source_ids[None, :]).astype(jnp.float32)
    latent_grad = jnp.dot(into_row, weighted, precision=EXACT).astype(jnp.bfloat16)
    coef_part = jnp.dot(
        pick_weight.astype(jnp.float32),
        grad_wide * gathered_rows.astype(jnp.float32),
        precision=EXACT,
    )
    scale_proj = 1.0 / math.sqrt(members * cells_all)
    scale_coef = 1.0 / math.sqrt(members * cells_all * K)
    loss_total, proj_total, coef_total = lax.psum(
        (loss_part, proj_part * scale_proj, coef_part * scale_coef), ("member", "band")
    )
    mean_loss = (loss_total / (members * variables * cells_all)).reshape(1)
    return (latent_grad[None], proj_total, coef_total, mean_loss)


def solution(mesh):
    placed = (
        P(("groups", "member"), "band", None),
        P(),
        P(),
        P(None, ("groups", "band")),
        P("band"),
        P(),
        P(),
        P(None, "band", None),
        P(),
    )
    return jax.shard_map(
        local,
        mesh=mesh,
        in_specs=placed,
        out_specs=(
            P(("groups", "member"), "band", None),
            P("groups", None),
            P("groups", None),
            P("groups"),
        ),
        check_vma=False,
    )
```

profile of v0, /device:TPU:0, one launch (start us, length us, event | category | flops | bytes accessed | tf_op | source)
XLA Modules:
  0.0 315.4 jit_solution(11185289565549401622)
XLA Ops:
  7.2 0.0 copy-start
  7.2 0.7 constant_dynamic-slice_fusion
  8.0 0.1 copy-done
  8.1 0.0 copy-start.4
  8.1 5.1 %gather_fusion = bf16[1536,1024]{1,0:T(8,128)(2,1)S(1)} fusion(bf16[64,1024]{1,0:T(8,128)(2,1)S(1)} %bitcast.23, s32[2048]{0:T(1024)S(1)} %pad_clamp_fusion), kind=kCustom, calls=%fused_computation | custom fusion | bytes 6297600 | tf_op jit(solution)/shard_map/gather | solution.py:71
  13.2 0.0 copy-done.4
  13.2 0.0 copy-start.1
  13.2 3.7 %fusion = (bf16[1536,1024]{1,0:T(8,128)(2,1)}, bf16[1536,1024]{1,0:T(8,128)(2,1)}) fusion(bf16[1536,1024]{1,0:T(8,128)(2,1)S(1)} %gather_fusion, bf16[16,1024]{1,0:T(8,128)(2,1)S(1)} %copy-done.4, s32[1536]{0:T(1024)S(1)} %eq.54), kind=kOutput, calls=%fused_computation.4 | convolution fusion | flops 58220544 | bytes 9476096 | tf_op jit(solution)/shard_map/dot_general | solution.py:64
  16.9 0.0 copy-done.1
  16.9 0.0 copy-start.6
  16.9 6.4 %all-to-all-start = ((bf16[4,384,1024]{2,1,0:T(8,128)(2,1)}), bf16[4,384,1024]{2,1,0:T(8,128)(2,1)S(1)}, u32[]{:S(2)}, u32[]{:S(2)}) async-start(bf16[4,384,1024]{2,1,0:T(8,128)(2,1)} %bitcast.27), calls=%async_computation | async-start | bytes 6291456 | tf_op jit(solution)/shard_map/all_to_all | solution.py:76
  23.3 0.0 copy-start.3
  23.4 0.1 collective-permute-start.2
  23.4 0.0 copy-done.6
  23.5 70.5 %all-to-all-done = bf16[4,384,1024]{2,1,0:T(8,128)(2,1)S(1)} async-done(((bf16[4,384,1024]{2,1,0:T(8,128)(2,1)}), bf16[4,384,1024]{2,1,0:T(8,128)(2,1)S(1)}, u32[]{:S(2)}, u32[]{:S(2)}) %all-to-all-start) | async-done | bytes 3145760 | tf_op jit(solution)/shard_map/all_to_all | solution.py:76
  94.0 0.0 copy-start.5
  94.0 0.0 copy-start.7
  94.0 0.0 copy-start.8
  94.0 1.0 fusion.3
  95.0 0.0 copy-start.2
  95.0 0.9 copy-done.2
  96.0 0.0 copy-done.3
  96.0 0.6 convolution_bitcast_fusion
  96.6 0.1 collective-permute-start
  96.7 0.0 collective-permute-done.2
  96.7 3.3 %collective-permute-done = f32[25,256]{1,0:T(8,128)S(1)} collective-permute-done((f32[25,256]{1,0:T(8,128)S(1)}, f32[25,256]{1,0:T(8,128)S(1)}, u32[]{:S(2)}, u32[]{:S(2)}) %collective-permute-start) | collective-permute-done | bytes 25632 | tf_op jit(solution)/shard_map/ppermute | solution.py:18
  100.0 0.1 collective-permute-start.3
  100.1 1.6 collective-permute-start.1
  101.7 1.7 collective-permute-done.3
  103.4 1.5 collective-permute-start.4
  104.9 0.0 collective-permute-done.1
  104.9 2.4 collective-permute-done.4
  107.3 0.0 copy-done.5
  107.3 0.0 copy-done.7
  107.3 0.0 copy-done.8
  107.3 0.7 fusion.12
  108.0 0.6 convolution_convert_fusion.2
  108.6 2.7 convolution_convert_fusion
  111.4 3.7 %all-to-all-start.1 = ((bf16[4,384,1024]{2,1,0:T(8,128)(2,1)}), bf16[4,384,1024]{2,1,0:T(8,128)(2,1)S(1)}, u32[]{:S(2)}, u32[]{:S(2)}) async-start(bf16[4,384,1024]{2,1,0:T(8,128)(2,1)} %bitcast.26), calls=%async_computation.1 | async-start | bytes 6291456 | tf_op jit(solution)/shard_map/all_to_all | solution.py:106
  115.1 0.0 all-reduce.3.cloned.1.call-start
  115.2 93.4 %psum.23 = f32[]{:T(128)} all-reduce(f32[]{:T(128)} %get-tuple-element.6), channel_id=1, replica_groups=mesh['groups'=2,'member'=4,'band'=4] {'member','band'}, use_global_device_ids=true, to_apply=%region_3.4 | all-reduce | flops 1 | bytes 8 | tf_op jit(solution)/shard_map/psum | solution.py:121
  209.2 2.6 convolution_multiply_fusion
  211.8 0.0 all-to-all-done.1
  211.8 5.2 %fusion.6 = f32[16,1024]{1,0:T(8,128)} fusion(bf16[1536,1024]{1,0:T(8,128)(2,1)S(1)} %bitcast.24, bf16[1536,1024]{1,0:T(8,128)(2,1)} %copy-done.1, s32[1536]{0:T(1024)S(1)} %eq.54), kind=kOutput, calls=%fused_computation.15 | convolution fusion | flops 306749440 | bytes 6363136 | tf_op jit(solution)/shard_map/dot_general | solution.py:114
  217.0 0.0 all-reduce.3.cloned.1.call-update
  217.0 5.6 %fusion.5 = bf16[1,64,1024]{2,1,0:T(8,128)(2,1)} fusion(bf16[1536,1024]{1,0:T(8,128)(2,1)S(1)} %bitcast.25, bf16[1536,1024]{1,0:T(8,128)(2,1)} %get-tuple-element.9, s32[1536]{0:T(1024)S(1)} %eq.46), kind=kOutput, calls=%fused_computation.14 | convolution fusion | flops 1212841984 | bytes 6428672 | tf_op jit(solution)/shard_map/dot_general | solution.py:113
  222.6 81.7 %all-reduce.3.cloned.1.call-done = (f32[25,1024]{1,0:T(8,128)}, f32[16,1024]{1,0:T(8,128)}) async-done(((f32[25,1024]{1,0:T(8,128)}, f32[16,1024]{1,0:T(8,128)}), (f32[25,1024]{1,0:T(8,128)}, f32[16,1024]{1,0:T(8,128)})) %all-reduce.3.cloned.1.call-update) | async-done | bytes 167952 | tf_op jit(solution)/shard_map/psum | solution.py:121
  304.4 1.6 copy.16
  305.9 1.5 copy.17
  (9 shorter events, 0.1 us)
Async XLA Ops:
  7.2 0.9 copy-start
  8.1 5.1 %copy-start.4 = (bf16[16,1024]{1,0:T(8,128)(2,1)S(1)}, bf16[16,1024]{1,0:T(8,128)(2,1)}, u32[]{:S(2)}) copy-start(bf16[16,1024]{1,0:T(8,128)(2,1)} %param.10) | copy-start | bytes 98308
  13.2 3.7 %copy-start.1 = (bf16[1536,1024]{1,0:T(8,128)(2,1)}, bf16[1536,1024]{1,0:T(8,128)(2,1)S(1)}, u32[]{:S(2)}) copy-start(bf16[1536,1024]{1,0:T(8,128)(2,1)S(1)} %gather_fusion) | copy-start | bytes 9437188
  16.9 6.5 %copy-start.6 = (s32[4,1,384]{2,1,0:T(1,128)S(1)}, s32[4,1,384]{2,1,0:T(1,128)}, u32[]{:S(2)}) copy-start(s32[4,1,384]{2,1,0:T(1,128)} %param.16) | copy-start | bytes 18436
  16.9 77.1 %all-to-all-start = ((bf16[4,384,1024]{2,1,0:T(8,128)(2,1)}), bf16[4,384,1024]{2,1,0:T(8,128)(2,1)S(1)}, u32[]{:S(2)}, u32[]{:S(2)}) async-start(bf16[4,384,1024]{2,1,0:T(8,128)(2,1)} %bitcast.27), calls=%async_computation | async-start | bytes 6291456 | tf_op jit(solution)/shard_map/all_to_all | solution.py:76
  23.3 72.6 %copy-start.3 = (bf16[25,1024]{1,0:T(8,128)(2,1)S(1)}, bf16[25,1024]{1,0:T(8,128)(2,1)}, u32[]{:S(2)}) copy-start(bf16[25,1024]{1,0:T(8,128)(2,1)} %param.11) | copy-start | bytes 153604
  23.4 73.3 %collective-permute-start.2 = (f32[25,256]{1,0:T(8,128)S(1)}, f32[25,256]{1,0:T(8,128)S(1)}, u32[]{:S(2)}, u32[]{:S(2)}) collective-permute-start(f32[25,256]{1,0:T(8,128)S(1)} %broadcast_in_dim.4), channel_id=1, source_target_pairs={{0,4},{4,8},{8,12},{12,0},{1,5},{5,9},{9,13},{13,1},{2,6},{6,10},{... | collective-permute-start | bytes 76808 | tf_op jit(solution)/shard_map/ppermute | solution.py:18
  94.0 13.3 %copy-start.5 = (f32[25,256]{1,0:T(8,128)S(1)}, f32[25,256]{1,0:T(8,128)}, u32[]{:S(2)}) copy-start(f32[25,256]{1,0:T(8,128)} %param.12) | copy-start | bytes 76804
  94.0 13.3 %copy-start.7 = (f32[256]{0:T(256)S(1)}, f32[256]{0:T(256)}, u32[]{:S(2)}) copy-start(f32[256]{0:T(256)} %param.13) | copy-start | bytes 3076
  94.0 13.3 %copy-start.8 = (f32[25]{0:T(128)S(1)}, f32[25]{0:T(128)}, u32[]{:S(2)}) copy-start(f32[25]{0:T(128)} %param.14) | copy-start | bytes 304
  95.0 1.0 copy-start.2
  96.6 3.4 %collective-permute-start = (f32[25,256]{1,0:T(8,128)S(1)}, f32[25,256]{1,0:T(8,128)S(1)}, u32[]{:S(2)}, u32[]{:S(2)}) collective-permute-start(f32[25,256]{1,0:T(8,128)S(1)} %convolution_bitcast_fusion), channel_id=1, source_target_pairs={{0,4},{4,8},{8,12},{12,0},{1,5},{5,9},{9,13},{13,1},{2,6},{6,10},{... | collective-permute-start | bytes 76808 | tf_op jit(solution)/shard_map/ppermute | solution.py:18
  100.0 3.4 %collective-permute-start.3 = (f32[25,256]{1,0:T(8,128)S(1)}, f32[25,256]{1,0:T(8,128)S(1)}, u32[]{:S(2)}, u32[]{:S(2)}) collective-permute-start(f32[25,256]{1,0:T(8,128)S(1)} %fusion.15), channel_id=1, source_target_pairs={{0,4},{4,8},{8,12},{12,0},{1,5},{5,9},{9,13},{13,1},{2,6},{6,10},{... | collective-permute-start | bytes 76808 | tf_op jit(solution)/shard_map/ppermute | solution.py:18
  100.1 4.8 %collective-permute-start.1 = (f32[25,256]{1,0:T(8,128)S(1)}, f32[25,256]{1,0:T(8,128)S(1)}, u32[]{:S(2)}, u32[]{:S(2)}) collective-permute-start(f32[25,256]{1,0:T(8,128)S(1)} %collective-permute-done), channel_id=1, source_target_pairs={{0,4},{4,8},{8,12},{12,0},{1,5},{5,9},{9,13},{13,1},{2,6},{6,10},{... | collective-permute-start | bytes 76808 | tf_op jit(solution)/shard_map/ppermute | solution.py:18
  103.4 3.9 %collective-permute-start.4 = (f32[25,256]{1,0:T(8,128)S(1)}, f32[25,256]{1,0:T(8,128)S(1)}, u32[]{:S(2)}, u32[]{:S(2)}) collective-permute-start(f32[25,256]{1,0:T(8,128)S(1)} %collective-permute-done.3), channel_id=1, source_target_pairs={{0,8},{4,12},{8,0},{12,4},{1,9},{5,13},{9,1},{13,5},{2,10},{6,14},... | collective-permute-start | bytes 76808 | tf_op jit(solution)/shard_map/ppermute | solution.py:18
  111.4 100.4 %all-to-all-start.1 = ((bf16[4,384,1024]{2,1,0:T(8,128)(2,1)}), bf16[4,384,1024]{2,1,0:T(8,128)(2,1)S(1)}, u32[]{:S(2)}, u32[]{:S(2)}) async-start(bf16[4,384,1024]{2,1,0:T(8,128)(2,1)} %bitcast.26), calls=%async_computation.1 | async-start | bytes 6291456 | tf_op jit(solution)/shard_map/all_to_all | solution.py:106
  115.1 189.3 %all-reduce.3.cloned.1.call-start = ((), (), s32[]{:S(2)}) async-start(), calls=%async_computation.2 | async-start | bytes 393216 | tf_op jit(solution)/shard_map/psum | solution.py:121
Sparse Core Ops, SparseCore 0:
  217.1 87.1 all-reduce.2
where the time goes:
time: 316 us; the launch traced here: 315 us
  waiting for transfers between devices  160 us (51%)
  blocking collectives  93.4 us (30%)
  matrix products  22.1 us (7%)
  between operations  16 us (5%)
  starting transfers between devices  13.4 us (4%)
  local copies, waits for them, and re-layouts  9.98 us (3%)
    psum x1, blocking collectives, local(): lax.psum((loss_part, proj_part * scale_proj, coef_part * scale_coef), ('m...  93.4 us
    psum x1, waiting for transfers between devices, local(): lax.psum((loss_part, proj_part * scale_proj, coef_part * scale_coef), ('m...  81.7 us
    all_to_all x1, waiting for transfers between devices, local(): lax.all_to_all(messages.reshape(bands, -1, hidden), 'band', split_axis=0,...  70.5 us
    ppermute x5, waiting for transfers between devices, from_behind(): lax.ppermute(shard, axis, [(i, (i + by) % peers) for i in range(peers)])  7.47 us
    all_to_all x1, starting transfers between devices, local(): lax.all_to_all(messages.reshape(bands, -1, hidden), 'band', split_axis=0,...  6.45 us
  transfers between devices with their start and end apart: 8, of which 5 were waited for; matrix products, arithmetic and copies ran while one was open for 3% of the time, Pallas kernels for 0%

commit v1 on v0

v1 whole, which is shorter than its diff:
```python
import functools
import math

import jax
import jax.numpy as jnp
from jax import lax
from jax.experimental import pallas as pl
from jax.experimental.pallas import tpu as pltpu
from jax.sharding import PartitionSpec as P

K = 4
FAIR_ALPHA = 0.95
SOFTNESS = 0.1
F32 = jnp.float32
BF16 = jnp.bfloat16
VMEM = pl.BlockSpec(memory_space=pltpu.VMEM)
PARAMS = pltpu.CompilerParams(vmem_limit_bytes=48 * 1024 * 1024)


def swap(shard, axis, mask):
    peers = lax.axis_size(axis)
    return lax.ppermute(shard, axis, [(i, i ^ mask) for i in range(peers)])


def soft_abs(values):
    return jnp.sqrt(values * values + SOFTNESS * SOFTNESS) - SOFTNESS


def soft_slope(values):
    return values * lax.rsqrt(values * values + SOFTNESS * SOFTNESS)


def up(size, unit):
    return -(-size // unit) * unit


def dot(left, right, left_dim, right_dim):
    return lax.dot_general(
        left, right, (((left_dim,), (right_dim,)), ((), ())), preferred_element_type=F32
    )


def parts(values):
    high = values.astype(BF16)
    rest = values - high.astype(F32)
    mid = rest.astype(BF16)
    low = (rest - mid.astype(F32)).astype(BF16)
    return jnp.concatenate([high, mid, low], axis=0)


def whole(stacked):
    rows = stacked.shape[0] // 3
    return (stacked[:rows] + stacked[rows : 2 * rows]) + stacked[2 * rows :]


def hot(ids, size):
    rows = lax.broadcasted_iota(jnp.int32, (size, ids.shape[1]), 0)
    return jnp.where(rows == ids, 1.0, 0.0).astype(BF16)


def project_kernel(latent, coef, proj, source, weight, target, *out):
    *payloads, products, proj_pad = out
    bands = len(payloads)
    here = lax.axis_index("band")
    rows, hidden = latent.shape
    table = coef.shape[0]
    variables = proj.shape[0]
    proj_pad[...] = jnp.zeros_like(proj_pad)
    proj_pad[0:variables, :] = proj[...]
    wide = latent[...].astype(F32)
    scale = coef[...].astype(F32)
    for q in range(table):
        products[q * rows : (q + 1) * rows, :] = (wide * scale[q : q + 1, :]).astype(BF16)
    projected = dot(proj_pad[...], products[...], 1, 1)
    split = parts(projected)
    for i in range(bands):
        there = lax.bitwise_xor(here, i)
        ids = weight[here, pl.ds(there, 1), :] * rows + source[here, pl.ds(there, 1), :]
        at_slots = whole(dot(split, hot(ids, table * rows), 1, 0))
        cells = target[there, :, :].astype(F32)
        row = lax.broadcasted_iota(jnp.int32, at_slots.shape, 0)
        payloads[i][...] = jnp.where(row == variables, cells, at_slots)


def predict_kernel(variables, *refs):
    *payloads, target, predicted = refs
    bands = len(payloads)
    here = lax.axis_index("band")
    total = 0.0
    for i in range(bands):
        there = lax.bitwise_xor(here, i)
        arrived = payloads[i][...]
        row = lax.broadcasted_iota(jnp.int32, arrived.shape, 0)
        split = parts(jnp.where(row < variables, arrived, 0.0))
        total = total + dot(split, hot(target[there, :, :], predicted.shape[1]), 1, 1)
    predicted[...] = whole(total)


def count_kernel(variables, cells_dev, rows, table, source, weight, *refs):
    *payloads, counts = refs
    here = lax.axis_index("band")
    for i, payload in enumerate(payloads):
        there = lax.bitwise_xor(here, i)
        ids = weight[here, pl.ds(there, 1), :] * rows + source[here, pl.ds(there, 1), :]
        cells = payload[variables : variables + 1, :].astype(jnp.int32)
        block = dot(hot(ids, table * rows), hot(cells, cells_dev), 1, 1)
        counts[:, i * cells_dev : (i + 1) * cells_dev] = block.astype(BF16)


def grade_kernel(pair_coef, target, area, var_weight, *refs):
    *predicted, grad = refs
    members = len(predicted)
    here = lax.axis_index("member")
    variables = target.shape[0]
    wanted = target[...]
    spots = lax.broadcasted_iota(jnp.int32, (variables, variables), 0)
    same = spots == lax.broadcasted_iota(jnp.int32, (variables, variables), 1)
    column = jnp.sum(jnp.where(same, var_weight[...], 0.0), axis=1, keepdims=True)
    weights = column * area[...]
    values = [ref[0:variables, :] for ref in predicted]
    own = values[0]
    slopes = 0.0
    for other in values[1:]:
        slopes = slopes + soft_slope(own - other)
    grad_pred = weights * (soft_slope(own - wanted) - pair_coef * slopes)
    for bit in range(members.bit_length() - 1):
        flip = lax.bitwise_and(lax.shift_right_logical(here, bit), 1) == 1
        ordered = list(values)
        for i in range(members):
            if not i >> bit & 1:
                first, second = values[i], values[i ^ (1 << bit)]
                ordered[i] = jnp.where(flip, second, first)
                ordered[i ^ (1 << bit)] = jnp.where(flip, first, second)
        values = ordered
    loss = 0.0
    spread = 0.0
    for m in range(members):
        loss = loss + soft_abs(values[m] - wanted)
        for k in range(m + 1, members):
            spread = spread + soft_abs(values[m] - values[k])
    total = jnp.sum(weights * (loss - pair_coef * spread), axis=(0, 1), keepdims=True)
    grad[...] = jnp.broadcast_to(total, grad.shape)
    grad[0:variables, :] = grad_pred


def backward_kernel(scale_proj, scale_coef, scale_loss, latent, coef, proj, counts, products, *refs):
    *grads, latent_grad, keep, send, mean_loss, proj_pad, cell_grad, sums = refs
    bands = len(grads)
    band = lax.axis_index("band")
    side = lax.bitwise_and(lax.axis_index("member"), 1)
    variables = proj.shape[0]
    rows, hidden = latent.shape
    table = coef.shape[0]
    cells_dev = grads[0].shape[1]
    padded = grads[0].shape[0]
    proj_pad[...] = jnp.zeros_like(proj_pad)
    proj_pad[0:variables, :] = proj[...]
    lane = lax.broadcasted_iota(jnp.int32, (1, 128), 1)
    losses = jnp.zeros((1, 128), F32)
    pair_grad = jnp.zeros((3 * padded, table * rows), F32)
    for i in range(bands):
        arrived = grads[i][...]
        there = lax.bitwise_xor(band, i)
        losses = losses + jnp.where(lane == there, arrived[variables : variables + 1, 0:128], 0.0)
        row = lax.broadcasted_iota(jnp.int32, arrived.shape, 0)
        split = parts(jnp.where(row < variables, arrived, 0.0))
        pair_grad = pair_grad + dot(split, counts[:, i * cells_dev : (i + 1) * cells_dev], 1, 1)
        three = jnp.concatenate([proj_pad[...]] * 3, axis=0)
        cell_grad[i * cells_dev : (i + 1) * cells_dev, :] = dot(split, three, 0, 0).astype(BF16)
    mean_loss[...] = jnp.sum(losses, axis=1, keepdims=True) * scale_loss
    sums[0:padded, :] = whole(dot(parts(whole(pair_grad)), products[...], 1, 0)) * scale_proj
    step = 256
    for h in range(0, hidden, step):
        block = dot(counts[...], cell_grad[:, h : h + step], 1, 0)
        wide = latent[:, h : h + step].astype(F32)
        scale = coef[:, h : h + step].astype(F32)
        into_latent = 0.0
        for q in range(table):
            piece = block[q * rows : (q + 1) * rows, :]
            into_latent = into_latent + piece * scale[q : q + 1, :]
            sums[padded + q : padded + q + 1, h : h + step] = (
                jnp.sum(piece * wide, axis=0, keepdims=True) * scale_coef
            )
        latent_grad[:, h : h + step] = into_latent.astype(BF16)
    half = hidden // 2
    left, right = sums[:, 0:half], sums[:, half:hidden]
    keep[...] = jnp.where(side == 0, left, right)
    send[...] = jnp.where(side == 0, right, left)


def call(kernel, outs, operands, scratch=(), flops=0):
    return pl.pallas_call(
        kernel,
        out_shape=outs,
        in_specs=[VMEM] * len(operands),
        out_specs=[VMEM] * len(outs),
        scratch_shapes=list(scratch),
        compiler_params=PARAMS,
        cost_estimate=pl.CostEstimate(flops=flops, bytes_accessed=1 << 20, transcendentals=0),
    )(*operands)


def shape(*dims, dtype=F32):
    return jax.ShapeDtypeStruct(dims, dtype)


def local(
    latent,
    coef_table,
    out_proj,
    target,
    cell_area,
    var_weight,
    edge_source,
    edge_target,
    edge_weight,
):
    latent_rows = latent[0]
    rows, hidden = latent_rows.shape
    bands = lax.axis_size("band")
    members = lax.axis_size("member")
    variables, cells_dev = target.shape
    cells_all = cells_dev * bands
    table = coef_table.shape[0]
    slots = edge_source.shape[2]
    pairs = table * rows
    padded = up(variables + 1, 16)
    pair_coef = FAIR_ALPHA / (members - 1) + (1.0 - FAIR_ALPHA) / members

    *payloads, products = call(
        project_kernel,
        [shape(padded, slots)] * bands + [shape(pairs, hidden, dtype=BF16)],
        (latent_rows, coef_table, out_proj, edge_source, edge_weight, edge_target),
        [pltpu.VMEM((padded, hidden), BF16)],
    )
    arrived = [payloads[0]] + [swap(payloads[i], "band", i) for i in range(1, bands)]
    (predicted,) = call(
        functools.partial(predict_kernel, variables),
        [shape(padded, cells_dev)],
        (*arrived, edge_target),
    )
    (counts,) = call(
        functools.partial(count_kernel, variables, cells_dev, rows, table),
        [shape(pairs, cells_all, dtype=BF16)],
        (edge_source, edge_weight, *arrived),
        flops=2 * pairs * slots * cells_all,
    )
    others = [predicted] + [swap(predicted, "member", i) for i in range(1, members)]
    (grad,) = call(
        functools.partial(grade_kernel, pair_coef),
        [shape(padded, cells_dev)],
        (target, cell_area.reshape(1, -1), var_weight.reshape(1, -1), *others),
    )
    grads = [grad] + [swap(grad, "band", i) for i in range(1, bands)]
    latent_grad, keep, send, mean_loss = call(
        functools.partial(
            backward_kernel,
            1.0 / math.sqrt(members * cells_all),
            1.0 / math.sqrt(members * cells_all * K),
            1.0 / (members * variables * cells_all),
        ),
        [
            shape(rows, hidden, dtype=BF16),
            shape(padded + table, hidden // 2),
            shape(padded + table, hidden // 2),
            shape(1, 1),
        ],
        (latent_rows, coef_table, out_proj, counts, products, *grads),
        [
            pltpu.VMEM((padded, hidden), BF16),
            pltpu.VMEM((cells_all, hidden), BF16),
            pltpu.VMEM((padded + table, hidden), F32),
        ],
    )
    total = keep + swap(send, "member", 1)
    step = 2
    while step < members:
        total = total + swap(total, "member", step)
        step *= 2
    step = 1
    while step < bands:
        total = total + swap(total, "band", step)
        step *= 2
    other = swap(total, "member", 1)
    side = lax.bitwise_and(lax.axis_index("member"), 1)
    left = jnp.where(side == 0, total, other)
    right = jnp.where(side == 0, other, total)
    full = jnp.concatenate([left, right], axis=1)
    return (
        latent_grad[None],
        full[:variables],
        full[padded : padded + table],
        mean_loss.reshape(1),
    )


def solution(mesh):
    placed = (
        P(("groups", "member"), "band", None),
        P(),
        P(),
        P(None, ("groups", "band")),
        P("band"),
        P(),
        P(),
        P(None, "band", None),
        P(),
    )
    return jax.shard_map(
        local,
        mesh=mesh,
        in_specs=placed,
        out_specs=(
            P(("groups", "member"), "band", None),
            P("groups", None),
            P("groups", None),
            P("groups"),
        ),
        check_vma=False,
    )
```

time: 316 us -> 59 us (0.19)
  waiting for transfers between devices: 160 us -> 25.2 us
  blocking collectives: 93.4 us -> 0 us
  matrix products: 22.1 us -> 0 us
  between operations: 16 us -> 0.79 us
  Pallas kernels: 0 us -> 8.1 us
    psum x1 -> x0, blocking collectives: 93.4 us -> none  [local(): lax.psum((loss_part, proj_part * scale_proj, coef_part * scale_coef), ('m...]
    psum x1 -> x0, waiting for transfers between devices: 81.7 us -> none  [local(): lax.psum((loss_part, proj_part * scale_proj, coef_part * scale_coef), ('m...]
    all_to_all x2 -> x0, waiting for transfers between devices: 70.5 us -> none  [the longest x1 70.5 us: local(): lax.all_to_all(messages.reshape(bands, -1, hidden), 'band', split_axis=0,...]
    dot_general x8 -> x0, matrix products: 22.1 us -> none  [the longest x1 5.62 us: local(): jnp.dot(into_row, weighted, precision=EXACT).astype(jnp.bfloat16)]
    ppermute x5 -> x14, waiting for transfers between devices: 7.47 us -> 25.2 us  [swap(): return lax.ppermute(shard, axis, [(i, i ^ mask) for i in range(peers)])]
    ppermute x5 -> x14, starting transfers between devices: 3.25 us -> 14.6 us  [swap(): return lax.ppermute(shard, axis, [(i, i ^ mask) for i in range(peers)])]
    all_to_all x2 -> x0, starting transfers between devices: 10.1 us -> none  [the longest x1 6.45 us: local(): lax.all_to_all(messages.reshape(bands, -1, hidden), 'band', split_axis=0,...]
    pallas_call x0 -> x5, Pallas kernels: none -> 8.1 us  [call(): pl.pallas_call(kernel, out_shape=outs, in_specs=[VMEM] * len(operands), o...]
  transfers between devices with their start and end apart: 8 -> 14, of which waited for: 5 -> 9; matrix products, arithmetic and copies ran while one was open for 3% -> 0% of each run, Pallas kernels for 0% -> 2%
where the time goes in v1:
time: 59 us; the launch traced here: 58.3 us
  waiting for transfers between devices  25.2 us (43%)
  starting transfers between devices  14.6 us (25%)
  local copies, waits for them, and re-layouts  8.23 us (14%)
  Pallas kernels  8.1 us (14%)
  other arithmetic  1.38 us (2%)
  between operations  0.79 us (1%)
    ppermute x14, waiting for transfers between devices, swap(): return lax.ppermute(shard, axis, [(i, i ^ mask) for i in range(peers)])  25.2 us
    ppermute x14, starting transfers between devices, swap(): return lax.ppermute(shard, axis, [(i, i ^ mask) for i in range(peers)])  14.6 us
    unnamed x28, local copies, waits for them, and re-layouts  8.23 us
    pallas_call x5, Pallas kernels, call(): pl.pallas_call(kernel, out_shape=outs, in_specs=[VMEM] * len(operands), o...  8.1 us
    concatenate x2, other arithmetic, local(): full = jnp.concatenate([left, right], axis=1)  1.3 us
  transfers between devices with their start and end apart: 14, of which 9 were waited for; matrix products, arithmetic and copies ran while one was open for 0% of the time, Pallas kernels for 2%

profile of v1, /device:TPU:0, one launch (start us, length us, event | category | flops | bytes accessed | tf_op | source)
XLA Modules:
  0.0 58.3 jit_solution(1508570691139073459)
XLA Ops:
  0.6 0.0 copy-start
  0.6 0.9 %copy-done = bf16[1,64,1024]{2,1,0:T(8,128)(2,1)S(1)} copy-done((bf16[1,64,1024]{2,1,0:T(8,128)(2,1)S(1)}, bf16[1,64,1024]{2,1,0:T(8,128)(2,1)}, u32[]{:S(2)}) %copy-start) | copy-done | bytes 131096
  1.5 0.0 copy-start.2
  1.5 0.8 %copy-done.2 = bf16[25,1024]{1,0:T(8,128)(2,1)S(1)} copy-done((bf16[25,1024]{1,0:T(8,128)(2,1)S(1)}, bf16[25,1024]{1,0:T(8,128)(2,1)}, u32[]{:S(2)}) %copy-start.2) | copy-done | bytes 51224
  2.4 0.0 copy-start.4
  2.4 0.8 %copy-done.4 = bf16[16,1024]{1,0:T(8,128)(2,1)S(1)} copy-done((bf16[16,1024]{1,0:T(8,128)(2,1)S(1)}, bf16[16,1024]{1,0:T(8,128)(2,1)}, u32[]{:S(2)}) %copy-start.4) | copy-done | bytes 32792
  3.1 0.0 copy-start.7
  3.1 0.7 %copy-done.7 = s32[4,4,384]{2,1,0:T(4,128)S(1)} copy-done((s32[4,4,384]{2,1,0:T(4,128)S(1)}, s32[4,4,384]{2,1,0:T(4,128)}, u32[]{:S(2)}) %copy-start.7) | copy-done | bytes 24600
  3.9 0.0 copy-start.9
  3.9 0.7 %copy-done.9 = s32[4,4,384]{2,1,0:T(4,128)S(1)} copy-done((s32[4,4,384]{2,1,0:T(4,128)S(1)}, s32[4,4,384]{2,1,0:T(4,128)}, u32[]{:S(2)}) %copy-start.9) | copy-done | bytes 24600
  4.6 0.0 copy-start.11
  4.6 0.7 %copy-done.11 = s32[4,1,384]{2,1,0:T(1,128)S(1)} copy-done((s32[4,1,384]{2,1,0:T(1,128)S(1)}, s32[4,1,384]{2,1,0:T(1,128)}, u32[]{:S(2)}) %copy-start.11) | copy-done | bytes 6168
  5.3 0.0 copy-start.1
  5.3 0.0 copy-start.3
  5.3 0.0 copy-start.5
  5.3 1.4 %shard_map.120 = (f32[32,384]{1,0:T(8,128)S(1)}, f32[32,384]{1,0:T(8,128)S(1)}, f32[32,384]{1,0:T(8,128)S(1)}, f32[32,384]{1,0:T(8,128)S(1)}, bf16[1024,1024]{1,0:T(8,128)(2,1)S(1)}) custom-call(bf16[64,1024]{1,0:T(8,128)(2,1)S(1)} %bitcast.5, bf16[16,1024]{1,0:T(8,128)(2,1)S(1)} %copy-done.4, bf16[25,1024]{1,0:T(8,128)(2,1)S(1)} %copy-done.2, ...), custom_call_target="tpu_custom_call" | custom-call | bytes 1048576 | tf_op jit(solution)/shard_map/pallas_call | solution.py:192
  6.7 3.1 %collective-permute-start = (f32[32,384]{1,0:T(8,128)S(1)}, f32[32,384]{1,0:T(8,128)S(1)}, u32[]{:S(2)}, u32[]{:S(2)}) collective-permute-start(f32[32,384]{1,0:T(8,128)S(1)} %get-tuple-element.14), channel_id=1, source_target_pairs={{0,1},{1,0},{2,3},{3,2},{4,5},{5,4},{6,7},{7,6},{8,9},{9,8},{10,11... | collective-permute-start | bytes 147464 | tf_op jit(solution)/shard_map/ppermute | solution.py:22
  9.8 2.6 %collective-permute-start.1 = (f32[32,384]{1,0:T(8,128)S(1)}, f32[32,384]{1,0:T(8,128)S(1)}, u32[]{:S(2)}, u32[]{:S(2)}) collective-permute-start(f32[32,384]{1,0:T(8,128)S(1)} %get-tuple-element.15), channel_id=1, source_target_pairs={{0,2},{1,3},{2,0},{3,1},{4,6},{5,7},{6,4},{7,5},{8,10},{9,11},{10,... | collective-permute-start | bytes 147464 | tf_op jit(solution)/shard_map/ppermute | solution.py:22
  12.4 0.0 collective-permute-start.2
  12.4 0.0 collective-permute-done.refs_1_
  12.4 3.3 %collective-permute-done.1.refs_2_ = f32[32,384]{1,0:T(8,128)S(1)} collective-permute-done((f32[32,384]{1,0:T(8,128)S(1)}, f32[32,384]{1,0:T(8,128)S(1)}, u32[]{:S(2)}, u32[]{:S(2)}) %collective-permute-start.1) | collective-permute-done | bytes 49184 | tf_op jit(solution)/shard_map/ppermute | solution.py:22
  15.7 2.6 %collective-permute-done.2.refs_3_ = f32[32,384]{1,0:T(8,128)S(1)} collective-permute-done((f32[32,384]{1,0:T(8,128)S(1)}, f32[32,384]{1,0:T(8,128)S(1)}, u32[]{:S(2)}, u32[]{:S(2)}) %collective-permute-start.2) | collective-permute-done | bytes 49184 | tf_op jit(solution)/shard_map/ppermute | solution.py:22
  18.3 0.4 shard_map.122.refs_0_
  18.6 0.1 collective-permute-start.3
  18.7 1.6 %collective-permute-start.4 = (f32[32,256]{1,0:T(8,128)S(1)}, f32[32,256]{1,0:T(8,128)S(1)}, u32[]{:S(2)}, u32[]{:S(2)}) collective-permute-start(f32[32,256]{1,0:T(8,128)S(1)} %shard_map.122.refs_0_), channel_id=1, source_target_pairs={{0,8},{4,12},{8,0},{12,4},{1,9},{5,13},{9,1},{13,5},{2,10},{6,14},... | collective-permute-start | bytes 98312 | tf_op jit(solution)/shard_map/ppermute | solution.py:22
  20.3 0.3 collective-permute-start.5
  20.6 0.0 collective-permute-done.3.refs_1_
  20.6 2.1 %collective-permute-done.4.refs_2_ = f32[32,256]{1,0:T(8,128)S(1)} collective-permute-done((f32[32,256]{1,0:T(8,128)S(1)}, f32[32,256]{1,0:T(8,128)S(1)}, u32[]{:S(2)}, u32[]{:S(2)}) %collective-permute-start.4) | collective-permute-done | bytes 32800 | tf_op jit(solution)/shard_map/ppermute | solution.py:22
  22.7 0.9 %collective-permute-done.5.refs_3_ = f32[32,256]{1,0:T(8,128)S(1)} collective-permute-done((f32[32,256]{1,0:T(8,128)S(1)}, f32[32,256]{1,0:T(8,128)S(1)}, u32[]{:S(2)}, u32[]{:S(2)}) %collective-permute-start.5) | collective-permute-done | bytes 32800 | tf_op jit(solution)/shard_map/ppermute | solution.py:22
  23.6 0.0 copy-start.6
  23.6 0.8 %copy-done.6 = f32[25,256]{1,0:T(8,128)S(1)} copy-done((f32[25,256]{1,0:T(8,128)S(1)}, f32[25,256]{1,0:T(8,128)}, u32[]{:S(2)}) %copy-start.6) | copy-done | bytes 25624
  24.4 0.0 copy-start.12
  24.4 0.7 %copy-done.12 = f32[256]{0:T(256)S(1)} copy-done((f32[256]{0:T(256)S(1)}, f32[256]{0:T(256)}, u32[]{:S(2)}) %copy-start.12) | copy-done | bytes 1048
  25.1 0.0 copy-start.13
  25.1 0.7 %copy-done.13 = f32[25]{0:T(128)S(1)} copy-done((f32[25]{0:T(128)S(1)}, f32[25]{0:T(128)}, u32[]{:S(2)}) %copy-start.13) | copy-done | bytes 124
  25.7 0.3 shard_map.123.refs_0_
  26.0 0.1 collective-permute-start.6
  26.1 1.3 %collective-permute-start.7 = (f32[32,256]{1,0:T(8,128)S(1)}, f32[32,256]{1,0:T(8,128)S(1)}, u32[]{:S(2)}, u32[]{:S(2)}) collective-permute-start(f32[32,256]{1,0:T(8,128)S(1)} %shard_map.123.refs_0_), channel_id=1, source_target_pairs={{0,2},{1,3},{2,0},{3,1},{4,6},{5,7},{6,4},{7,5},{8,10},{9,11},{10,... | collective-permute-start | bytes 98312 | tf_op jit(solution)/shard_map/ppermute | solution.py:22
  27.4 3.1 %collective-permute-start.8 = (f32[32,256]{1,0:T(8,128)S(1)}, f32[32,256]{1,0:T(8,128)S(1)}, u32[]{:S(2)}, u32[]{:S(2)}) collective-permute-start(f32[32,256]{1,0:T(8,128)S(1)} %shard_map.123.refs_0_), channel_id=1, source_target_pairs={{0,3},{1,2},{2,1},{3,0},{4,7},{5,6},{6,5},{7,4},{8,11},{9,10},{10,... | collective-permute-start | bytes 98312 | tf_op jit(solution)/shard_map/ppermute | solution.py:22
  30.5 0.0 copy-start.8
  30.5 0.7 %copy-done.8 = s32[4,4,384]{2,1,0:T(4,128)S(1)} copy-done((s32[4,4,384]{2,1,0:T(4,128)S(1)}, s32[4,4,384]{2,1,0:T(4,128)}, u32[]{:S(2)}) %copy-start.8) | copy-done | bytes 24600
  31.2 0.0 copy-start.10
  31.2 0.7 %copy-done.10 = s32[4,4,384]{2,1,0:T(4,128)S(1)} copy-done((s32[4,4,384]{2,1,0:T(4,128)S(1)}, s32[4,4,384]{2,1,0:T(4,128)}, u32[]{:S(2)}) %copy-start.10) | copy-done | bytes 24600
  32.0 1.3 %shard_map.121.counts = bf16[1024,1024]{1,0:T(8,128)(2,1)S(1)} custom-call(s32[4,4,384]{2,1,0:T(4,128)S(1)} %copy-done.8, s32[4,4,384]{2,1,0:T(4,128)S(1)} %copy-done.10, f32[32,384]{1,0:T(8,128)S(1)} %get-tuple-element.13.refs_0_, f32[32,384]{1,0:T(8,128)S(1)} %collective-permute-done.refs_1_, f32[32,384]{1,0:T(8,128)S(1)} %collective-permute-done.1.refs_2_, ...), custom_call_target="tpu_custom_call" | custom-call | flops 805306368 | bytes 1048576 | tf_op jit(solution)/shard_map/pallas_call | solution.py:192
  33.3 0.0 collective-permute-done.6.refs_1_
  33.3 0.0 collective-permute-done.7.refs_2_
  33.3 0.0 collective-permute-done.8.refs_3_
  33.3 0.0 copy-done.1
  33.3 0.0 copy-done.3
  33.3 0.0 copy-done.5
  33.3 4.7 %shard_map.124 = (bf16[64,1024]{1,0:T(8,128)(2,1)}, f32[48,512]{1,0:T(8,128)S(1)}, f32[48,512]{1,0:T(8,128)S(1)}, f32[1,1]{1,0:T(1,128)}) custom-call(bf16[64,1024]{1,0:T(8,128)(2,1)S(1)} %bitcast.6, bf16[16,1024]{1,0:T(8,128)(2,1)S(1)} %copy-done.5, bf16[25,1024]{1,0:T(8,128)(2,1)S(1)} %copy-done.3, bf16[1024,1024]{1,0:T(8,128)(2,1)S(1)} %shard_map.121.counts, ...), custom_call_target="tpu_custom_call" | custom-call | bytes 1048576 | tf_op jit(solution)/shard_map/pallas_call | solution.py:192
  38.1 0.0 collective-permute-start.9
  38.1 1.3 %collective-permute-done.9 = f32[48,512]{1,0:T(8,128)S(1)} collective-permute-done((f32[48,512]{1,0:T(8,128)S(1)}, f32[48,512]{1,0:T(8,128)S(1)}, u32[]{:S(2)}, u32[]{:S(2)}) %collective-permute-start.9) | collective-permute-done | bytes 98336 | tf_op jit(solution)/shard_map/ppermute | solution.py:22
  39.4 0.9 %collective-permute-start.10 = (f32[48,512]{1,0:T(8,128)S(1)}, f32[48,512]{1,0:T(8,128)S(1)}, u32[]{:S(2)}, u32[]{:S(2)}) collective-permute-start(f32[48,512]{1,0:T(8,128)S(1)} %add.12), channel_id=1, source_target_pairs={{0,8},{4,12},{8,0},{12,4},{1,9},{5,13},{9,1},{13,5},{2,10},{6,14},... | collective-permute-start | bytes 294920 | tf_op jit(solution)/shard_map/ppermute | solution.py:22
  40.3 4.0 %collective-permute-done.10 = f32[48,512]{1,0:T(8,128)S(1)} collective-permute-done((f32[48,512]{1,0:T(8,128)S(1)}, f32[48,512]{1,0:T(8,128)S(1)}, u32[]{:S(2)}, u32[]{:S(2)}) %collective-permute-start.10) | collective-permute-done | bytes 98336 | tf_op jit(solution)/shard_map/ppermute | solution.py:22
  44.3 0.1 collective-permute-start.11
  44.4 4.6 %collective-permute-done.11 = f32[48,512]{1,0:T(8,128)S(1)} collective-permute-done((f32[48,512]{1,0:T(8,128)S(1)}, f32[48,512]{1,0:T(8,128)S(1)}, u32[]{:S(2)}, u32[]{:S(2)}) %collective-permute-start.11) | collective-permute-done | bytes 98336 | tf_op jit(solution)/shard_map/ppermute | solution.py:22
  49.0 1.5 %collective-permute-start.12 = (f32[48,512]{1,0:T(8,128)S(1)}, f32[48,512]{1,0:T(8,128)S(1)}, u32[]{:S(2)}, u32[]{:S(2)}) collective-permute-start(f32[48,512]{1,0:T(8,128)S(1)} %add.14), channel_id=1, source_target_pairs={{0,2},{1,3},{2,0},{3,1},{4,6},{5,7},{6,4},{7,5},{8,10},{9,11},{10,... | collective-permute-start | bytes 294920 | tf_op jit(solution)/shard_map/ppermute | solution.py:22
  50.5 5.1 %collective-permute-done.12 = f32[48,512]{1,0:T(8,128)S(1)} collective-permute-done((f32[48,512]{1,0:T(8,128)S(1)}, f32[48,512]{1,0:T(8,128)S(1)}, u32[]{:S(2)}, u32[]{:S(2)}) %collective-permute-start.12) | collective-permute-done | bytes 98336 | tf_op jit(solution)/shard_map/ppermute | solution.py:22
  55.6 0.1 collective-permute-start.13
  55.7 1.3 %collective-permute-done.13 = f32[48,512]{1,0:T(8,128)S(1)} collective-permute-done((f32[48,512]{1,0:T(8,128)S(1)}, f32[48,512]{1,0:T(8,128)S(1)}, u32[]{:S(2)}, u32[]{:S(2)}) %collective-permute-start.13) | collective-permute-done | bytes 98336 | tf_op jit(solution)/shard_map/ppermute | solution.py:22
  57.0 0.6 %pad_maximum_fusion = f32[16,1024]{1,0:T(8,128)} fusion(f32[48,512]{1,0:T(8,128)S(1)} %get-tuple-element.22, f32[48,512]{1,0:T(8,128)S(1)} %get-tuple-element.23), kind=kLoop, calls=%fused_computation.3 | loop fusion | flops 16384 | bytes 262144 | tf_op jit(solution)/shard_map/concatenate | solution.py:288
  57.7 0.7 %fusion = f32[25,1024]{1,0:T(8,128)} fusion(f32[48,512]{1,0:T(8,128)S(1)} %get-tuple-element.23, f32[48,512]{1,0:T(8,128)S(1)} %get-tuple-element.22), kind=kLoop, calls=%fused_computation.2 | loop fusion | flops 25600 | bytes 299008 | tf_op jit(solution)/shard_map/concatenate | solution.py:288
  (5 shorter events, 0.1 us)
Async XLA Ops:
  0.6 0.9 %copy-start = (bf16[1,64,1024]{2,1,0:T(8,128)(2,1)S(1)}, bf16[1,64,1024]{2,1,0:T(8,128)(2,1)}, u32[]{:S(2)}) copy-start(bf16[1,64,1024]{2,1,0:T(8,128)(2,1)} %param.9) | copy-start | bytes 393220
  1.5 0.8 %copy-start.2 = (bf16[25,1024]{1,0:T(8,128)(2,1)S(1)}, bf16[25,1024]{1,0:T(8,128)(2,1)}, u32[]{:S(2)}) copy-start(bf16[25,1024]{1,0:T(8,128)(2,1)} %proj.3) | copy-start | bytes 153604
  2.4 0.8 %copy-start.4 = (bf16[16,1024]{1,0:T(8,128)(2,1)S(1)}, bf16[16,1024]{1,0:T(8,128)(2,1)}, u32[]{:S(2)}) copy-start(bf16[16,1024]{1,0:T(8,128)(2,1)} %coef.3) | copy-start | bytes 98308
  3.1 0.7 %copy-start.7 = (s32[4,4,384]{2,1,0:T(4,128)S(1)}, s32[4,4,384]{2,1,0:T(4,128)}, u32[]{:S(2)}) copy-start(s32[4,4,384]{2,1,0:T(4,128)} %source.3) | copy-start | bytes 73732
  3.9 0.7 %copy-start.9 = (s32[4,4,384]{2,1,0:T(4,128)S(1)}, s32[4,4,384]{2,1,0:T(4,128)}, u32[]{:S(2)}) copy-start(s32[4,4,384]{2,1,0:T(4,128)} %weight.3) | copy-start | bytes 73732
  4.6 0.7 %copy-start.11 = (s32[4,1,384]{2,1,0:T(1,128)S(1)}, s32[4,1,384]{2,1,0:T(1,128)}, u32[]{:S(2)}) copy-start(s32[4,1,384]{2,1,0:T(1,128)} %refs_4_.1) | copy-start | bytes 18436
  5.3 28.0 %copy-start.1 = (bf16[1,64,1024]{2,1,0:T(8,128)(2,1)S(1)}, bf16[1,64,1024]{2,1,0:T(8,128)(2,1)}, u32[]{:S(2)}) copy-start(bf16[1,64,1024]{2,1,0:T(8,128)(2,1)} %param.9) | copy-start | bytes 393220
  5.3 28.0 %copy-start.3 = (bf16[25,1024]{1,0:T(8,128)(2,1)S(1)}, bf16[25,1024]{1,0:T(8,128)(2,1)}, u32[]{:S(2)}) copy-start(bf16[25,1024]{1,0:T(8,128)(2,1)} %proj.3) | copy-start | bytes 153604
  5.3 28.0 %copy-start.5 = (bf16[16,1024]{1,0:T(8,128)(2,1)S(1)}, bf16[16,1024]{1,0:T(8,128)(2,1)}, u32[]{:S(2)}) copy-start(bf16[16,1024]{1,0:T(8,128)(2,1)} %coef.3) | copy-start | bytes 98308
  6.7 5.7 %collective-permute-start = (f32[32,384]{1,0:T(8,128)S(1)}, f32[32,384]{1,0:T(8,128)S(1)}, u32[]{:S(2)}, u32[]{:S(2)}) collective-permute-start(f32[32,384]{1,0:T(8,128)S(1)} %get-tuple-element.14), channel_id=1, source_target_pairs={{0,1},{1,0},{2,3},{3,2},{4,5},{5,4},{6,7},{7,6},{8,9},{9,8},{10,11... | collective-permute-start | bytes 147464 | tf_op jit(solution)/shard_map/ppermute | solution.py:22
  9.8 5.9 %collective-permute-start.1 = (f32[32,384]{1,0:T(8,128)S(1)}, f32[32,384]{1,0:T(8,128)S(1)}, u32[]{:S(2)}, u32[]{:S(2)}) collective-permute-start(f32[32,384]{1,0:T(8,128)S(1)} %get-tuple-element.15), channel_id=1, source_target_pairs={{0,2},{1,3},{2,0},{3,1},{4,6},{5,7},{6,4},{7,5},{8,10},{9,11},{10,... | collective-permute-start | bytes 147464 | tf_op jit(solution)/shard_map/ppermute | solution.py:22
  12.4 5.9 %collective-permute-start.2 = (f32[32,384]{1,0:T(8,128)S(1)}, f32[32,384]{1,0:T(8,128)S(1)}, u32[]{:S(2)}, u32[]{:S(2)}) collective-permute-start(f32[32,384]{1,0:T(8,128)S(1)} %get-tuple-element.16), channel_id=1, source_target_pairs={{0,3},{1,2},{2,1},{3,0},{4,7},{5,6},{6,5},{7,4},{8,11},{9,10},{10,... | collective-permute-start | bytes 147464 | tf_op jit(solution)/shard_map/ppermute | solution.py:22
  18.6 1.9 %collective-permute-start.3 = (f32[32,256]{1,0:T(8,128)S(1)}, f32[32,256]{1,0:T(8,128)S(1)}, u32[]{:S(2)}, u32[]{:S(2)}) collective-permute-start(f32[32,256]{1,0:T(8,128)S(1)} %shard_map.122.refs_0_), channel_id=1, source_target_pairs={{0,4},{4,0},{8,12},{12,8},{1,5},{5,1},{9,13},{13,9},{2,6},{6,2},{1... | collective-permute-start | bytes 98312 | tf_op jit(solution)/shard_map/ppermute | solution.py:22
  18.7 4.0 %collective-permute-start.4 = (f32[32,256]{1,0:T(8,128)S(1)}, f32[32,256]{1,0:T(8,128)S(1)}, u32[]{:S(2)}, u32[]{:S(2)}) collective-permute-start(f32[32,256]{1,0:T(8,128)S(1)} %shard_map.122.refs_0_), channel_id=1, source_target_pairs={{0,8},{4,12},{8,0},{12,4},{1,9},{5,13},{9,1},{13,5},{2,10},{6,14},... | collective-permute-start | bytes 98312 | tf_op jit(solution)/shard_map/ppermute | solution.py:22
  20.3 3.3 %collective-permute-start.5 = (f32[32,256]{1,0:T(8,128)S(1)}, f32[32,256]{1,0:T(8,128)S(1)}, u32[]{:S(2)}, u32[]{:S(2)}) collective-permute-start(f32[32,256]{1,0:T(8,128)S(1)} %shard_map.122.refs_0_), channel_id=1, source_target_pairs={{0,12},{4,8},{8,4},{12,0},{1,13},{5,9},{9,5},{13,1},{2,14},{6,10},... | collective-permute-start | bytes 98312 | tf_op jit(solution)/shard_map/ppermute | solution.py:22
  23.6 0.8 %copy-start.6 = (f32[25,256]{1,0:T(8,128)S(1)}, f32[25,256]{1,0:T(8,128)}, u32[]{:S(2)}) copy-start(f32[25,256]{1,0:T(8,128)} %target.3) | copy-start | bytes 76804
  24.4 0.7 %copy-start.12 = (f32[256]{0:T(256)S(1)}, f32[256]{0:T(256)}, u32[]{:S(2)}) copy-start(f32[256]{0:T(256)} %param.13) | copy-start | bytes 3076
  25.1 0.7 %copy-start.13 = (f32[25]{0:T(128)S(1)}, f32[25]{0:T(128)}, u32[]{:S(2)}) copy-start(f32[25]{0:T(128)} %param.14) | copy-start | bytes 304
  26.0 7.2 %collective-permute-start.6 = (f32[32,256]{1,0:T(8,128)S(1)}, f32[32,256]{1,0:T(8,128)S(1)}, u32[]{:S(2)}, u32[]{:S(2)}) collective-permute-start(f32[32,256]{1,0:T(8,128)S(1)} %shard_map.123.refs_0_), channel_id=1, source_target_pairs={{0,1},{1,0},{2,3},{3,2},{4,5},{5,4},{6,7},{7,6},{8,9},{9,8},{10,11... | collective-permute-start | bytes 98312 | tf_op jit(solution)/shard_map/ppermute | solution.py:22
  26.1 7.2 %collective-permute-start.7 = (f32[32,256]{1,0:T(8,128)S(1)}, f32[32,256]{1,0:T(8,128)S(1)}, u32[]{:S(2)}, u32[]{:S(2)}) collective-permute-start(f32[32,256]{1,0:T(8,128)S(1)} %shard_map.123.refs_0_), channel_id=1, source_target_pairs={{0,2},{1,3},{2,0},{3,1},{4,6},{5,7},{6,4},{7,5},{8,10},{9,11},{10,... | collective-permute-start | bytes 98312 | tf_op jit(solution)/shard_map/ppermute | solution.py:22
  27.4 5.9 %collective-permute-start.8 = (f32[32,256]{1,0:T(8,128)S(1)}, f32[32,256]{1,0:T(8,128)S(1)}, u32[]{:S(2)}, u32[]{:S(2)}) collective-permute-start(f32[32,256]{1,0:T(8,128)S(1)} %shard_map.123.refs_0_), channel_id=1, source_target_pairs={{0,3},{1,2},{2,1},{3,0},{4,7},{5,6},{6,5},{7,4},{8,11},{9,10},{10,... | collective-permute-start | bytes 98312 | tf_op jit(solution)/shard_map/ppermute | solution.py:22
  30.5 0.7 %copy-start.8 = (s32[4,4,384]{2,1,0:T(4,128)S(1)}, s32[4,4,384]{2,1,0:T(4,128)}, u32[]{:S(2)}) copy-start(s32[4,4,384]{2,1,0:T(4,128)} %source.3) | copy-start | bytes 73732
  31.2 0.7 %copy-start.10 = (s32[4,4,384]{2,1,0:T(4,128)S(1)}, s32[4,4,384]{2,1,0:T(4,128)}, u32[]{:S(2)}) copy-start(s32[4,4,384]{2,1,0:T(4,128)} %weight.3) | copy-start | bytes 73732
  38.1 1.3 %collective-permute-start.9 = (f32[48,512]{1,0:T(8,128)S(1)}, f32[48,512]{1,0:T(8,128)S(1)}, u32[]{:S(2)}, u32[]{:S(2)}) collective-permute-start(f32[48,512]{1,0:T(8,128)S(1)} %get-tuple-element.20), channel_id=1, source_target_pairs={{0,4},{4,0},{8,12},{12,8},{1,5},{5,1},{9,13},{13,9},{2,6},{6,2},{1... | collective-permute-start | bytes 294920 | tf_op jit(solution)/shard_map/ppermute | solution.py:22
  39.4 4.9 %collective-permute-start.10 = (f32[48,512]{1,0:T(8,128)S(1)}, f32[48,512]{1,0:T(8,128)S(1)}, u32[]{:S(2)}, u32[]{:S(2)}) collective-permute-start(f32[48,512]{1,0:T(8,128)S(1)} %add.12), channel_id=1, source_target_pairs={{0,8},{4,12},{8,0},{12,4},{1,9},{5,13},{9,1},{13,5},{2,10},{6,14},... | collective-permute-start | bytes 294920 | tf_op jit(solution)/shard_map/ppermute | solution.py:22
  44.3 4.7 %collective-permute-start.11 = (f32[48,512]{1,0:T(8,128)S(1)}, f32[48,512]{1,0:T(8,128)S(1)}, u32[]{:S(2)}, u32[]{:S(2)}) collective-permute-start(f32[48,512]{1,0:T(8,128)S(1)} %add.13), channel_id=1, source_target_pairs={{0,1},{1,0},{2,3},{3,2},{4,5},{5,4},{6,7},{7,6},{8,9},{9,8},{10,11... | collective-permute-start | bytes 294920 | tf_op jit(solution)/shard_map/ppermute | solution.py:22
  49.0 6.6 %collective-permute-start.12 = (f32[48,512]{1,0:T(8,128)S(1)}, f32[48,512]{1,0:T(8,128)S(1)}, u32[]{:S(2)}, u32[]{:S(2)}) collective-permute-start(f32[48,512]{1,0:T(8,128)S(1)} %add.14), channel_id=1, source_target_pairs={{0,2},{1,3},{2,0},{3,1},{4,6},{5,7},{6,4},{7,5},{8,10},{9,11},{10,... | collective-permute-start | bytes 294920 | tf_op jit(solution)/shard_map/ppermute | solution.py:22
  55.6 1.4 %collective-permute-start.13 = (f32[48,512]{1,0:T(8,128)S(1)}, f32[48,512]{1,0:T(8,128)S(1)}, u32[]{:S(2)}, u32[]{:S(2)}) collective-permute-start(f32[48,512]{1,0:T(8,128)S(1)} %add.15), channel_id=1, source_target_pairs={{0,4},{4,0},{8,12},{12,8},{1,5},{5,1},{9,13},{13,9},{2,6},{6,2},{1... | collective-permute-start | bytes 294920 | tf_op jit(solution)/shard_map/ppermute | solution.py:22

commit v2 on v1

--- a/solution.py
+++ b/solution.py
@@ -14,6 +14,7 @@
 F32 = jnp.float32
 BF16 = jnp.bfloat16
 VMEM = pl.BlockSpec(memory_space=pltpu.VMEM)
+HBM = pl.BlockSpec(memory_space=pltpu.HBM)
 PARAMS = pltpu.CompilerParams(vmem_limit_bytes=48 * 1024 * 1024)
 
 
@@ -58,14 +59,36 @@
     return jnp.where(rows == ids, 1.0, 0.0).astype(BF16)
 
 
-def project_kernel(latent, coef, proj, source, weight, target, *out):
-    *payloads, products, proj_pad = out
+def project_kernel(*refs):
+    (latent_in, coef_in, proj_in, source_in, weight_in, target_in, wanted_in, area_in, factor_in, *rest) = refs
+    *payloads, products, pair_ids, target, wanted, area, factor = rest[:-7]
+    latent, coef, proj, source, weight, proj_pad, arrivals = rest[-7:]
+    moves = [
+        pltpu.make_async_copy(there, here, arrivals.at[n])
+        for n, (there, here) in enumerate(
+            [
+                (latent_in, latent),
+                (coef_in, coef),
+                (proj_in, proj),
+                (source_in, source),
+                (weight_in, weight),
+                (target_in, target),
+                (wanted_in, wanted),
+                (area_in, area),
+                (factor_in, factor),
+            ]
+        )
+    ]
+    for move in moves:
+        move.start()
     bands = len(payloads)
     here = lax.axis_index("band")
     rows, hidden = latent.shape
     table = coef.shape[0]
     variables = proj.shape[0]
     proj_pad[...] = jnp.zeros_like(proj_pad)
+    for move in moves:
+        move.wait()
     proj_pad[0:variables, :] = proj[...]
     wide = latent[...].astype(F32)
     scale = coef[...].astype(F32)
@@ -76,6 +99,7 @@
     for i in range(bands):
         there = lax.bitwise_xor(here, i)
         ids = weight[here, pl.ds(there, 1), :] * rows + source[here, pl.ds(there, 1), :]
+        pair_ids[i] = ids
         at_slots = whole(dot(split, hot(ids, table * rows), 1, 0))
         cells = target[there, :, :].astype(F32)
         row = lax.broadcasted_iota(jnp.int32, at_slots.shape, 0)
@@ -96,18 +120,15 @@
     predicted[...] = whole(total)
 
 
-def count_kernel(variables, cells_dev, rows, table, source, weight, *refs):
+def count_kernel(variables, cells_dev, pair_ids, *refs):
     *payloads, counts = refs
-    here = lax.axis_index("band")
     for i, payload in enumerate(payloads):
-        there = lax.bitwise_xor(here, i)
-        ids = weight[here, pl.ds(there, 1), :] * rows + source[here, pl.ds(there, 1), :]
         cells = payload[variables : variables + 1, :].astype(jnp.int32)
-        block = dot(hot(ids, table * rows), hot(cells, cells_dev), 1, 1)
+        block = dot(hot(pair_ids[i], counts.shape[0]), hot(cells, cells_dev), 1, 1)
         counts[:, i * cells_dev : (i + 1) * cells_dev] = block.astype(BF16)
 
 
-def grade_kernel(pair_coef, target, area, var_weight, *refs):
+def grade_kernel(pair_coef, target, area, var_weight, counts, *refs):
     *predicted, grad = refs
     members = len(predicted)
     here = lax.axis_index("member")
@@ -188,12 +209,43 @@
     send[...] = jnp.where(side == 0, right, left)
 
 
-def call(kernel, outs, operands, scratch=(), flops=0):
+def write_kernel(scaled, other, latent_grad, mean_loss, *refs):
+    latent_out, proj_out, coef_out, loss_out, proj, coef, leaves = refs
+    early = [
+        pltpu.make_async_copy(latent_grad, latent_out, leaves.at[0]),
+        pltpu.make_async_copy(mean_loss, loss_out, leaves.at[1]),
+    ]
+    for move in early:
+        move.start()
+    side = lax.bitwise_and(lax.axis_index("member"), 1)
+    half = scaled.shape[1]
+    variables, table = proj.shape[0], coef.shape[0]
+    first = scaled.shape[0] - table
+    here, there = scaled[...], other[...]
+    left = jnp.where(side == 0, here, there)
+    right = jnp.where(side == 0, there, here)
+    proj[:, 0:half] = left[0:variables]
+    proj[:, half : 2 * half] = right[0:variables]
+    coef[:, 0:half] = left[first:]
+    coef[:, half : 2 * half] = right[first:]
+    late = [
+        pltpu.make_async_copy(proj, proj_out, leaves.at[2]),
+        pltpu.make_async_copy(coef, coef_out, leaves.at[3]),
+    ]
+    for move in late:
+        move.start()
+    for move in early + late:
+        move.wait()
+
+
+def call(kernel, outs, operands, scratch=(), flops=0, source=VMEM, sink=VMEM):
+    if source is HBM:
+        operands = [pltpu.with_memory_space_constraint(x, pltpu.HBM) for x in operands]
     return pl.pallas_call(
         kernel,
         out_shape=outs,
-        in_specs=[VMEM] * len(operands),
-        out_specs=[VMEM] * len(outs),
+        in_specs=[source] * len(operands),
+        out_specs=[sink] * len(outs),
         scratch_shapes=list(scratch),
         compiler_params=PARAMS,
         cost_estimate=pl.CostEstimate(flops=flops, bytes_accessed=1 << 20, transcendentals=0),
@@ -227,29 +279,58 @@
     padded = up(variables + 1, 16)
     pair_coef = FAIR_ALPHA / (members - 1) + (1.0 - FAIR_ALPHA) / members
 
-    *payloads, products = call(
+    *payloads, products, pair_ids, cell_ids, wanted, area, factor = call(
         project_kernel,
-        [shape(padded, slots)] * bands + [shape(pairs, hidden, dtype=BF16)],
-        (latent_rows, coef_table, out_proj, edge_source, edge_weight, edge_target),
-        [pltpu.VMEM((padded, hidden), BF16)],
+        [shape(padded, slots)] * bands
+        + [
+            shape(pairs, hidden, dtype=BF16),
+            shape(bands, 1, slots, dtype=jnp.int32),
+            shape(bands, 1, slots, dtype=jnp.int32),
+            shape(variables, cells_dev),
+            shape(1, cells_dev),
+            shape(1, variables),
+        ],
+        (
+            latent_rows,
+            coef_table,
+            out_proj,
+            edge_source,
+            edge_weight,
+            edge_target,
+            target,
+            cell_area.reshape(1, -1),
+            var_weight.reshape(1, -1),
+        ),
+        [
+            pltpu.VMEM((rows, hidden), BF16),
+            pltpu.VMEM((table, hidden), BF16),
+            pltpu.VMEM((variables, hidden), BF16),
+            pltpu.VMEM(edge_source.shape, jnp.int32),
+            pltpu.VMEM(edge_weight.shape, jnp.int32),
+            pltpu.VMEM((padded, hidden), BF16),
+            pltpu.SemaphoreType.DMA((9,)),
+        ],
+        source=HBM,
     )
     arrived = [payloads[0]] + [swap(payloads[i], "band", i) for i in range(1, bands)]
     (predicted,) = call(
         functools.partial(predict_kernel, variables),
         [shape(padded, cells_dev)],
-        (*arrived, edge_target),
+        (*arrived, cell_ids),
     )
     (counts,) = call(
-        functools.partial(count_kernel, variables, cells_dev, rows, table),
+        functools.partial(count_kernel, variables, cells_dev),
         [shape(pairs, cells_all, dtype=BF16)],
-        (edge_source, edge_weight, *arrived),
+        (pair_ids, *arrived),
         flops=2 * pairs * slots * cells_all,
     )
-    others = [predicted] + [swap(predicted, "member", i) for i in range(1, members)]
+    members_here = [predicted]
+    for i in range(1, members):
+        members_here.append(swap(members_here[i ^ 1], "member", 1) if i & 1 else swap(predicted, "member", i))
     (grad,) = call(
         functools.partial(grade_kernel, pair_coef),
         [shape(padded, cells_dev)],
-        (target, cell_area.reshape(1, -1), var_weight.reshape(1, -1), *others),
+        (wanted, area, factor, counts, *members_here),
     )
     grads = [grad] + [swap(grad, "band", i) for i in range(1, bands)]
     latent_grad, keep, send, mean_loss = call(
@@ -282,16 +363,23 @@
         total = total + swap(total, "band", step)
         step *= 2
     other = swap(total, "member", 1)
-    side = lax.bitwise_and(lax.axis_index("member"), 1)
-    left = jnp.where(side == 0, total, other)
-    right = jnp.where(side == 0, other, total)
-    full = jnp.concatenate([left, right], axis=1)
-    return (
-        latent_grad[None],
-        full[:variables],
-        full[padded : padded + table],
-        mean_loss.reshape(1),
-    )
+    latent_out, proj_grad, coef_grad, loss_out = call(
+        write_kernel,
+        [
+            shape(rows, hidden, dtype=BF16),
+            shape(variables, hidden),
+            shape(table, hidden),
+            shape(1, 1),
+        ],
+        (total, other, latent_grad, mean_loss),
+        [
+            pltpu.VMEM((variables, hidden), F32),
+            pltpu.VMEM((table, hidden), F32),
+            pltpu.SemaphoreType.DMA((4,)),
+        ],
+        sink=HBM,
+    )
+    return (latent_out[None], proj_grad, coef_grad, loss_out.reshape(1))
 
 
 def solution(mesh):

time: 59 us -> 51.5 us (0.87)
  local copies, waits for them, and re-layouts: 8.23 us -> 0.01 us
  Pallas kernels: 8.1 us -> 10.5 us
  starting transfers between devices: 14.6 us -> 16 us
  other arithmetic: 1.38 us -> 0.06 us
  waiting for transfers between devices: 25.2 us -> 24.1 us
    unnamed x28 -> x6, local copies, waits for them, and re-layouts: 8.23 us -> 0.01 us
    pallas_call x5 -> x6, Pallas kernels: 8.1 us -> 10.5 us  [call(): pl.pallas_call(kernel, out_shape=outs, in_specs=[source] * len(operands),...]
    ppermute x14, starting transfers between devices: 14.6 us -> 16 us  [swap(): return lax.ppermute(shard, axis, [(i, i ^ mask) for i in range(peers)])]
    concatenate x2 -> x0, other arithmetic: 1.3 us -> none  [local(): full = jnp.concatenate([left, right], axis=1)]
    ppermute x14, waiting for transfers between devices: 25.2 us -> 24.1 us  [swap(): return lax.ppermute(shard, axis, [(i, i ^ mask) for i in range(peers)])]
  transfers between devices with their start and end apart: 14 -> 14, of which waited for: 9 -> 10; matrix products, arithmetic and copies ran while one was open for 0% -> 0% of each run, Pallas kernels for 2% -> 3%
where the time goes in v2:
time: 51.5 us; the launch traced here: 51.4 us
  waiting for transfers between devices  24.1 us (47%)
  starting transfers between devices  16 us (31%)
  Pallas kernels  10.5 us (20%)
  between operations  0.72 us (1%)
    ppermute x14, waiting for transfers between devices, swap(): return lax.ppermute(shard, axis, [(i, i ^ mask) for i in range(peers)])  24.1 us
    ppermute x14, starting transfers between devices, swap(): return lax.ppermute(shard, axis, [(i, i ^ mask) for i in range(peers)])  16 us
    pallas_call x6, Pallas kernels, call(): pl.pallas_call(kernel, out_shape=outs, in_specs=[source] * len(operands),...  10.5 us
  transfers between devices with their start and end apart: 14, of which 10 were waited for; matrix products, arithmetic and copies ran while one was open for 0% of the time, Pallas kernels for 3%

profile of v2, /device:TPU:0, one launch (start us, length us, event | category | flops | bytes accessed | tf_op | source)
XLA Modules:
  0.0 51.4 jit_solution(13281902393514866413)
XLA Ops:
  0.6 2.4 %shard_map.120 = (f32[32,384]{1,0:T(8,128)S(1)}, f32[32,384]{1,0:T(8,128)S(1)}, f32[32,384]{1,0:T(8,128)S(1)}, f32[32,384]{1,0:T(8,128)S(1)}, bf16[1024,1024]{1,...) custom-call(bf16[64,1024]{1,0:T(8,128)(2,1)} %bitcast.5, ...), custom_call_target="tpu_custom_call" | custom-call | bytes 1048576 | tf_op jit(solution)/shard_map/pallas_call | solution.py:244
  3.1 3.1 %collective-permute-start = (f32[32,384]{1,0:T(8,128)S(1)}, f32[32,384]{1,0:T(8,128)S(1)}, u32[]{:S(2)}, u32[]{:S(2)}) collective-permute-start(f32[32,384]{1,0:T(8,128)S(1)} %get-tuple-element.24), channel_id=1, source_target_pairs={{0,1},{1,0},{2,3},{3,2},{4,5},{5,4},{6,7},{7,6},{8,9},{9,8},{10,11... | collective-permute-start | bytes 147464 | tf_op jit(solution)/shard_map/ppermute | solution.py:23
  6.2 2.6 %collective-permute-start.1 = (f32[32,384]{1,0:T(8,128)S(1)}, f32[32,384]{1,0:T(8,128)S(1)}, u32[]{:S(2)}, u32[]{:S(2)}) collective-permute-start(f32[32,384]{1,0:T(8,128)S(1)} %get-tuple-element.25), channel_id=1, source_target_pairs={{0,2},{1,3},{2,0},{3,1},{4,6},{5,7},{6,4},{7,5},{8,10},{9,11},{10,... | collective-permute-start | bytes 147464 | tf_op jit(solution)/shard_map/ppermute | solution.py:23
  8.8 0.0 collective-permute-start.2
  8.8 0.0 collective-permute-done.refs_1_
  8.8 3.3 %collective-permute-done.1.refs_2_ = f32[32,384]{1,0:T(8,128)S(1)} collective-permute-done((f32[32,384]{1,0:T(8,128)S(1)}, f32[32,384]{1,0:T(8,128)S(1)}, u32[]{:S(2)}, u32[]{:S(2)}) %collective-permute-start.1) | collective-permute-done | bytes 49184 | tf_op jit(solution)/shard_map/ppermute | solution.py:23
  12.1 2.6 %collective-permute-done.2.refs_3_ = f32[32,384]{1,0:T(8,128)S(1)} collective-permute-done((f32[32,384]{1,0:T(8,128)S(1)}, f32[32,384]{1,0:T(8,128)S(1)}, u32[]{:S(2)}, u32[]{:S(2)}) %collective-permute-start.2) | collective-permute-done | bytes 49184 | tf_op jit(solution)/shard_map/ppermute | solution.py:23
  14.6 0.4 shard_map.122.refs_0_
  15.0 1.6 %collective-permute-start.4 = (f32[32,256]{1,0:T(8,128)S(1)}, f32[32,256]{1,0:T(8,128)S(1)}, u32[]{:S(2)}, u32[]{:S(2)}) collective-permute-start(f32[32,256]{1,0:T(8,128)S(1)} %shard_map.122.refs_0_), channel_id=1, source_target_pairs={{0,8},{4,12},{8,0},{12,4},{1,9},{5,13},{9,1},{13,5},{2,10},{6,14},... | collective-permute-start | bytes 98312 | tf_op jit(solution)/shard_map/ppermute | solution.py:23
  16.6 0.0 collective-permute-start.3
  16.6 2.4 %collective-permute-done.4.refs_2_ = f32[32,256]{1,0:T(8,128)S(1)} collective-permute-done((f32[32,256]{1,0:T(8,128)S(1)}, f32[32,256]{1,0:T(8,128)S(1)}, u32[]{:S(2)}, u32[]{:S(2)}) %collective-permute-start.4) | collective-permute-done | bytes 32800 | tf_op jit(solution)/shard_map/ppermute | solution.py:23
  19.0 0.0 collective-permute-start.5
  19.0 0.0 copy-start
  19.0 0.0 copy-start.1
  19.0 0.0 copy-start.2
  19.0 1.3 %shard_map.121.counts = bf16[1024,1024]{1,0:T(8,128)(2,1)S(1)} custom-call(s32[4,1,384]{2,1,0:T(1,128)S(1)} %get-tuple-element.22.pair_ids, f32[32,384]{1,0:T(8,128)S(1)} %get-tuple-element.23.refs_0_, f32[32,384]{1,0:T(8,128)S(1)} %collective-permute-done.refs_1_, f32[32,384]{1,0:T(8,128)S(1)} %collective-permute-done.1.refs_2_, ...), custom_call_target="tpu_custom_call" | custom-call | flops 805306368 | bytes 1048576 | tf_op jit(solution)/shard_map/pallas_call | solution.py:244
  20.3 0.0 collective-permute-done.3.refs_1_
  20.3 0.0 collective-permute-done.5.refs_3_
  20.3 0.3 shard_map.123.refs_0_
  20.6 0.8 %collective-permute-start.8 = (f32[32,256]{1,0:T(8,128)S(1)}, f32[32,256]{1,0:T(8,128)S(1)}, u32[]{:S(2)}, u32[]{:S(2)}) collective-permute-start(f32[32,256]{1,0:T(8,128)S(1)} %shard_map.123.refs_0_), channel_id=1, source_target_pairs={{0,3},{1,2},{2,1},{3,0},{4,7},{5,6},{6,5},{7,4},{8,11},{9,10},{10,... | collective-permute-start | bytes 98312 | tf_op jit(solution)/shard_map/ppermute | solution.py:23
  21.4 0.0 collective-permute-start.7
  21.4 3.7 %collective-permute-start.6 = (f32[32,256]{1,0:T(8,128)S(1)}, f32[32,256]{1,0:T(8,128)S(1)}, u32[]{:S(2)}, u32[]{:S(2)}) collective-permute-start(f32[32,256]{1,0:T(8,128)S(1)} %shard_map.123.refs_0_), channel_id=1, source_target_pairs={{0,1},{1,0},{2,3},{3,2},{4,5},{5,4},{6,7},{7,6},{8,9},{9,8},{10,11... | collective-permute-start | bytes 98312 | tf_op jit(solution)/shard_map/ppermute | solution.py:23
  25.1 1.6 %collective-permute-done.8.refs_3_ = f32[32,256]{1,0:T(8,128)S(1)} collective-permute-done((f32[32,256]{1,0:T(8,128)S(1)}, f32[32,256]{1,0:T(8,128)S(1)}, u32[]{:S(2)}, u32[]{:S(2)}) %collective-permute-start.8) | collective-permute-done | bytes 32800 | tf_op jit(solution)/shard_map/ppermute | solution.py:23
  26.7 0.6 %collective-permute-done.7.refs_2_ = f32[32,256]{1,0:T(8,128)S(1)} collective-permute-done((f32[32,256]{1,0:T(8,128)S(1)}, f32[32,256]{1,0:T(8,128)S(1)}, u32[]{:S(2)}, u32[]{:S(2)}) %collective-permute-start.7) | collective-permute-done | bytes 32800 | tf_op jit(solution)/shard_map/ppermute | solution.py:23
  27.3 0.0 collective-permute-done.6.refs_1_
  27.3 0.0 copy-done
  27.3 0.0 copy-done.1
  27.4 0.0 copy-done.2
  27.4 4.7 %shard_map.124 = (bf16[64,1024]{1,0:T(8,128)(2,1)S(1)}, f32[48,512]{1,0:T(8,128)S(1)}, f32[48,512]{1,0:T(8,128)S(1)}, f32[1,1]{1,0:T(1,128)}) custom-call(bf16[64,1024]{1,0:T(8,128)(2,1)S(1)} %bitcast.6, bf16[16,1024]{1,0:T(8,128)(2,1)S(1)} %copy-done.2, bf16[25,1024]{1,0:T(8,128)(2,1)S(1)} %copy-done.1, bf16[1024,1024]{1,0:T(8,128)(2,1)S(1)} %shard_map.121.counts, ...), custom_call_target="tpu_custom_call" | custom-call | bytes 1048576 | tf_op jit(solution)/shard_map/pallas_call | solution.py:244
  32.0 0.0 collective-permute-start.9
  32.0 1.3 %collective-permute-done.9 = f32[48,512]{1,0:T(8,128)S(1)} collective-permute-done((f32[48,512]{1,0:T(8,128)S(1)}, f32[48,512]{1,0:T(8,128)S(1)}, u32[]{:S(2)}, u32[]{:S(2)}) %collective-permute-start.9) | collective-permute-done | bytes 98336 | tf_op jit(solution)/shard_map/ppermute | solution.py:23
  33.3 1.6 %collective-permute-start.10 = (f32[48,512]{1,0:T(8,128)S(1)}, f32[48,512]{1,0:T(8,128)S(1)}, u32[]{:S(2)}, u32[]{:S(2)}) collective-permute-start(f32[48,512]{1,0:T(8,128)S(1)} %add.12), channel_id=1, source_target_pairs={{0,8},{4,12},{8,0},{12,4},{1,9},{5,13},{9,1},{13,5},{2,10},{6,14},... | collective-permute-start | bytes 294920 | tf_op jit(solution)/shard_map/ppermute | solution.py:23
  34.9 3.4 %collective-permute-done.10 = f32[48,512]{1,0:T(8,128)S(1)} collective-permute-done((f32[48,512]{1,0:T(8,128)S(1)}, f32[48,512]{1,0:T(8,128)S(1)}, u32[]{:S(2)}, u32[]{:S(2)}) %collective-permute-start.10) | collective-permute-done | bytes 98336 | tf_op jit(solution)/shard_map/ppermute | solution.py:23
  38.3 1.7 %collective-permute-start.11 = (f32[48,512]{1,0:T(8,128)S(1)}, f32[48,512]{1,0:T(8,128)S(1)}, u32[]{:S(2)}, u32[]{:S(2)}) collective-permute-start(f32[48,512]{1,0:T(8,128)S(1)} %add.13), channel_id=1, source_target_pairs={{0,1},{1,0},{2,3},{3,2},{4,5},{5,4},{6,7},{7,6},{8,9},{9,8},{10,11... | collective-permute-start | bytes 294920 | tf_op jit(solution)/shard_map/ppermute | solution.py:23
  40.0 3.0 %collective-permute-done.11 = f32[48,512]{1,0:T(8,128)S(1)} collective-permute-done((f32[48,512]{1,0:T(8,128)S(1)}, f32[48,512]{1,0:T(8,128)S(1)}, u32[]{:S(2)}, u32[]{:S(2)}) %collective-permute-start.11) | collective-permute-done | bytes 98336 | tf_op jit(solution)/shard_map/ppermute | solution.py:23
  43.0 1.0 %collective-permute-start.12 = (f32[48,512]{1,0:T(8,128)S(1)}, f32[48,512]{1,0:T(8,128)S(1)}, u32[]{:S(2)}, u32[]{:S(2)}) collective-permute-start(f32[48,512]{1,0:T(8,128)S(1)} %add.14), channel_id=1, source_target_pairs={{0,2},{1,3},{2,0},{3,1},{4,6},{5,7},{6,4},{7,5},{8,10},{9,11},{10,... | collective-permute-start | bytes 294920 | tf_op jit(solution)/shard_map/ppermute | solution.py:23
  44.0 4.6 %collective-permute-done.12 = f32[48,512]{1,0:T(8,128)S(1)} collective-permute-done((f32[48,512]{1,0:T(8,128)S(1)}, f32[48,512]{1,0:T(8,128)S(1)}, u32[]{:S(2)}, u32[]{:S(2)}) %collective-permute-start.12) | collective-permute-done | bytes 98336 | tf_op jit(solution)/shard_map/ppermute | solution.py:23
  48.6 0.1 collective-permute-start.13
  48.7 1.3 %collective-permute-done.13.other = f32[48,512]{1,0:T(8,128)S(1)} collective-permute-done((f32[48,512]{1,0:T(8,128)S(1)}, f32[48,512]{1,0:T(8,128)S(1)}, u32[]{:S(2)}, u32[]{:S(2)}) %collective-permute-start.13) | collective-permute-done | bytes 98336 | tf_op jit(solution)/shard_map/ppermute | solution.py:23
  49.9 1.4 %shard_map.125 = (bf16[64,1024]{1,0:T(8,128)(2,1)}, f32[25,1024]{1,0:T(8,128)}, f32[16,1024]{1,0:T(8,128)}, f32[1,1]{1,0:T(1,128)}) custom-call(f32[48,512]{1,0:T(8,128)S(1)} %add.15.scaled, f32[48,512]{1,0:T(8,128)S(1)} %collective-permute-done.13.other, bf16[64,1024]{1,0:T(8,128)(2,1)S(1)} %get-tuple-element.34.latent_grad, f32[1,1]{1,0:T(1,128)} %get-tuple-element.35.mean_loss), custom_call_target="tpu_custom_call" | custom-call | bytes 1048576 | tf_op jit(solution)/shard_map/pallas_call | solution.py:244
  (4 shorter events, 0.1 us)
Async XLA Ops:
  3.1 5.7 %collective-permute-start = (f32[32,384]{1,0:T(8,128)S(1)}, f32[32,384]{1,0:T(8,128)S(1)}, u32[]{:S(2)}, u32[]{:S(2)}) collective-permute-start(f32[32,384]{1,0:T(8,128)S(1)} %get-tuple-element.24), channel_id=1, source_target_pairs={{0,1},{1,0},{2,3},{3,2},{4,5},{5,4},{6,7},{7,6},{8,9},{9,8},{10,11... | collective-permute-start | bytes 147464 | tf_op jit(solution)/shard_map/ppermute | solution.py:23
  6.2 5.9 %collective-permute-start.1 = (f32[32,384]{1,0:T(8,128)S(1)}, f32[32,384]{1,0:T(8,128)S(1)}, u32[]{:S(2)}, u32[]{:S(2)}) collective-permute-start(f32[32,384]{1,0:T(8,128)S(1)} %get-tuple-element.25), channel_id=1, source_target_pairs={{0,2},{1,3},{2,0},{3,1},{4,6},{5,7},{6,4},{7,5},{8,10},{9,11},{10,... | collective-permute-start | bytes 147464 | tf_op jit(solution)/shard_map/ppermute | solution.py:23
  8.8 5.9 %collective-permute-start.2 = (f32[32,384]{1,0:T(8,128)S(1)}, f32[32,384]{1,0:T(8,128)S(1)}, u32[]{:S(2)}, u32[]{:S(2)}) collective-permute-start(f32[32,384]{1,0:T(8,128)S(1)} %get-tuple-element.26), channel_id=1, source_target_pairs={{0,3},{1,2},{2,1},{3,0},{4,7},{5,6},{6,5},{7,4},{8,11},{9,10},{10,... | collective-permute-start | bytes 147464 | tf_op jit(solution)/shard_map/ppermute | solution.py:23
  15.0 4.0 %collective-permute-start.4 = (f32[32,256]{1,0:T(8,128)S(1)}, f32[32,256]{1,0:T(8,128)S(1)}, u32[]{:S(2)}, u32[]{:S(2)}) collective-permute-start(f32[32,256]{1,0:T(8,128)S(1)} %shard_map.122.refs_0_), channel_id=1, source_target_pairs={{0,8},{4,12},{8,0},{12,4},{1,9},{5,13},{9,1},{13,5},{2,10},{6,14},... | collective-permute-start | bytes 98312 | tf_op jit(solution)/shard_map/ppermute | solution.py:23
  16.6 3.7 %collective-permute-start.3 = (f32[32,256]{1,0:T(8,128)S(1)}, f32[32,256]{1,0:T(8,128)S(1)}, u32[]{:S(2)}, u32[]{:S(2)}) collective-permute-start(f32[32,256]{1,0:T(8,128)S(1)} %shard_map.122.refs_0_), channel_id=1, source_target_pairs={{0,4},{4,0},{8,12},{12,8},{1,5},{5,1},{9,13},{13,9},{2,6},{6,2},{1... | collective-permute-start | bytes 98312 | tf_op jit(solution)/shard_map/ppermute | solution.py:23
  19.0 1.3 %collective-permute-start.5 = (f32[32,256]{1,0:T(8,128)S(1)}, f32[32,256]{1,0:T(8,128)S(1)}, u32[]{:S(2)}, u32[]{:S(2)}) collective-permute-start(f32[32,256]{1,0:T(8,128)S(1)} %collective-permute-done.4.refs_2_), channel_id=1, source_target_pairs={{0,4},{4,0},{8,12},{12,8},{1,5},{5,1},{9,13},{13,9},{2,6},{6,2},{1... | collective-permute-start | bytes 98312 | tf_op jit(solution)/shard_map/ppermute | solution.py:23
  19.0 8.4 %copy-start = (bf16[1,64,1024]{2,1,0:T(8,128)(2,1)S(1)}, bf16[1,64,1024]{2,1,0:T(8,128)(2,1)}, u32[]{:S(2)}) copy-start(bf16[1,64,1024]{2,1,0:T(8,128)(2,1)} %param.9) | copy-start | bytes 393220
  19.0 8.4 %copy-start.1 = (bf16[25,1024]{1,0:T(8,128)(2,1)S(1)}, bf16[25,1024]{1,0:T(8,128)(2,1)}, u32[]{:S(2)}) copy-start(bf16[25,1024]{1,0:T(8,128)(2,1)} %proj.1) | copy-start | bytes 153604
  19.0 8.4 %copy-start.2 = (bf16[16,1024]{1,0:T(8,128)(2,1)S(1)}, bf16[16,1024]{1,0:T(8,128)(2,1)}, u32[]{:S(2)}) copy-start(bf16[16,1024]{1,0:T(8,128)(2,1)} %coef.1) | copy-start | bytes 98308
  20.6 6.1 %collective-permute-start.8 = (f32[32,256]{1,0:T(8,128)S(1)}, f32[32,256]{1,0:T(8,128)S(1)}, u32[]{:S(2)}, u32[]{:S(2)}) collective-permute-start(f32[32,256]{1,0:T(8,128)S(1)} %shard_map.123.refs_0_), channel_id=1, source_target_pairs={{0,3},{1,2},{2,1},{3,0},{4,7},{5,6},{6,5},{7,4},{8,11},{9,10},{10,... | collective-permute-start | bytes 98312 | tf_op jit(solution)/shard_map/ppermute | solution.py:23
  21.4 5.9 %collective-permute-start.7 = (f32[32,256]{1,0:T(8,128)S(1)}, f32[32,256]{1,0:T(8,128)S(1)}, u32[]{:S(2)}, u32[]{:S(2)}) collective-permute-start(f32[32,256]{1,0:T(8,128)S(1)} %shard_map.123.refs_0_), channel_id=1, source_target_pairs={{0,2},{1,3},{2,0},{3,1},{4,6},{5,7},{6,4},{7,5},{8,10},{9,11},{10,... | collective-permute-start | bytes 98312 | tf_op jit(solution)/shard_map/ppermute | solution.py:23
  21.4 5.9 %collective-permute-start.6 = (f32[32,256]{1,0:T(8,128)S(1)}, f32[32,256]{1,0:T(8,128)S(1)}, u32[]{:S(2)}, u32[]{:S(2)}) collective-permute-start(f32[32,256]{1,0:T(8,128)S(1)} %shard_map.123.refs_0_), channel_id=1, source_target_pairs={{0,1},{1,0},{2,3},{3,2},{4,5},{5,4},{6,7},{7,6},{8,9},{9,8},{10,11... | collective-permute-start | bytes 98312 | tf_op jit(solution)/shard_map/ppermute | solution.py:23
  32.0 1.3 %collective-permute-start.9 = (f32[48,512]{1,0:T(8,128)S(1)}, f32[48,512]{1,0:T(8,128)S(1)}, u32[]{:S(2)}, u32[]{:S(2)}) collective-permute-start(f32[48,512]{1,0:T(8,128)S(1)} %get-tuple-element.33), channel_id=1, source_target_pairs={{0,4},{4,0},{8,12},{12,8},{1,5},{5,1},{9,13},{13,9},{2,6},{6,2},{1... | collective-permute-start | bytes 294920 | tf_op jit(solution)/shard_map/ppermute | solution.py:23
  33.3 4.9 %collective-permute-start.10 = (f32[48,512]{1,0:T(8,128)S(1)}, f32[48,512]{1,0:T(8,128)S(1)}, u32[]{:S(2)}, u32[]{:S(2)}) collective-permute-start(f32[48,512]{1,0:T(8,128)S(1)} %add.12), channel_id=1, source_target_pairs={{0,8},{4,12},{8,0},{12,4},{1,9},{5,13},{9,1},{13,5},{2,10},{6,14},... | collective-permute-start | bytes 294920 | tf_op jit(solution)/shard_map/ppermute | solution.py:23
  38.3 4.7 %collective-permute-start.11 = (f32[48,512]{1,0:T(8,128)S(1)}, f32[48,512]{1,0:T(8,128)S(1)}, u32[]{:S(2)}, u32[]{:S(2)}) collective-permute-start(f32[48,512]{1,0:T(8,128)S(1)} %add.13), channel_id=1, source_target_pairs={{0,1},{1,0},{2,3},{3,2},{4,5},{5,4},{6,7},{7,6},{8,9},{9,8},{10,11... | collective-permute-start | bytes 294920 | tf_op jit(solution)/shard_map/ppermute | solution.py:23
  43.0 5.6 %collective-permute-start.12 = (f32[48,512]{1,0:T(8,128)S(1)}, f32[48,512]{1,0:T(8,128)S(1)}, u32[]{:S(2)}, u32[]{:S(2)}) collective-permute-start(f32[48,512]{1,0:T(8,128)S(1)} %add.14), channel_id=1, source_target_pairs={{0,2},{1,3},{2,0},{3,1},{4,6},{5,7},{6,4},{7,5},{8,10},{9,11},{10,... | collective-permute-start | bytes 294920 | tf_op jit(solution)/shard_map/ppermute | solution.py:23
  48.6 1.4 %collective-permute-start.13 = (f32[48,512]{1,0:T(8,128)S(1)}, f32[48,512]{1,0:T(8,128)S(1)}, u32[]{:S(2)}, u32[]{:S(2)}) collective-permute-start(f32[48,512]{1,0:T(8,128)S(1)} %add.15.scaled), channel_id=1, source_target_pairs={{0,4},{4,0},{8,12},{12,8},{1,5},{5,1},{9,13},{13,9},{2,6},{6,2},{1... | collective-permute-start | bytes 294920 | tf_op jit(solution)/shard_map/ppermute | solution.py:23

commit v3 on v2

--- a/solution.py
+++ b/solution.py
@@ -41,12 +41,16 @@
     )
 
 
-def parts(values):
+def pieces_of(values):
     high = values.astype(BF16)
     rest = values - high.astype(F32)
     mid = rest.astype(BF16)
     low = (rest - mid.astype(F32)).astype(BF16)
-    return jnp.concatenate([high, mid, low], axis=0)
+    return high, mid, low
+
+
+def parts(values):
+    return jnp.concatenate(pieces_of(values), axis=0)
 
 
 def whole(stacked):
@@ -128,8 +132,8 @@
         counts[:, i * cells_dev : (i + 1) * cells_dev] = block.astype(BF16)
 
 
-def grade_kernel(pair_coef, target, area, var_weight, counts, *refs):
-    *predicted, grad = refs
+def grade_kernel(pair_coef, target, area, var_weight, *refs):
+    *predicted, grad, rows = refs
     members = len(predicted)
     here = lax.axis_index("member")
     variables = target.shape[0]
@@ -160,8 +164,11 @@
         for k in range(m + 1, members):
             spread = spread + soft_abs(values[m] - values[k])
     total = jnp.sum(weights * (loss - pair_coef * spread), axis=(0, 1), keepdims=True)
-    grad[...] = jnp.broadcast_to(total, grad.shape)
-    grad[0:variables, :] = grad_pred
+    lane = lax.broadcasted_iota(jnp.int32, rows.shape, 1)
+    pieces = [piece.astype(F32) for piece in pieces_of(total)]
+    rows[...] = jnp.where(lane == 0, pieces[0], jnp.where(lane == 1, pieces[1], jnp.where(lane == 2, pieces[2], 0.0)))
+    rows[0:variables, :] = grad_pred
+    grad[...] = rows[...].astype(BF16)
 
 
 def backward_kernel(scale_proj, scale_coef, scale_loss, latent, coef, proj, counts, products, *refs):
@@ -178,18 +185,18 @@
     proj_pad[0:variables, :] = proj[...]
     lane = lax.broadcasted_iota(jnp.int32, (1, 128), 1)
     losses = jnp.zeros((1, 128), F32)
-    pair_grad = jnp.zeros((3 * padded, table * rows), F32)
+    pair_grad = jnp.zeros((padded, table * rows), F32)
     for i in range(bands):
-        arrived = grads[i][...]
+        arrived = grads[i][...].astype(F32)
         there = lax.bitwise_xor(band, i)
-        losses = losses + jnp.where(lane == there, arrived[variables : variables + 1, 0:128], 0.0)
+        loss = jnp.sum(arrived[variables : variables + 1, 0:128], axis=1, keepdims=True)
+        losses = losses + jnp.where(lane == there, loss, 0.0)
         row = lax.broadcasted_iota(jnp.int32, arrived.shape, 0)
-        split = parts(jnp.where(row < variables, arrived, 0.0))
-        pair_grad = pair_grad + dot(split, counts[:, i * cells_dev : (i + 1) * cells_dev], 1, 1)
-        three = jnp.concatenate([proj_pad[...]] * 3, axis=0)
-        cell_grad[i * cells_dev : (i + 1) * cells_dev, :] = dot(split, three, 0, 0).astype(BF16)
+        grad = jnp.where(row < variables, arrived, 0.0).astype(BF16)
+        pair_grad = pair_grad + dot(grad, counts[:, i * cells_dev : (i + 1) * cells_dev], 1, 1)
+        cell_grad[i * cells_dev : (i + 1) * cells_dev, :] = dot(grad, proj_pad[...], 0, 0).astype(BF16)
     mean_loss[...] = jnp.sum(losses, axis=1, keepdims=True) * scale_loss
-    sums[0:padded, :] = whole(dot(parts(whole(pair_grad)), products[...], 1, 0)) * scale_proj
+    sums[0:padded, :] = whole(dot(parts(pair_grad), products[...], 1, 0)) * scale_proj
     step = 256
     for h in range(0, hidden, step):
         block = dot(counts[...], cell_grad[:, h : h + step], 1, 0)
@@ -329,8 +336,9 @@
         members_here.append(swap(members_here[i ^ 1], "member", 1) if i & 1 else swap(predicted, "member", i))
     (grad,) = call(
         functools.partial(grade_kernel, pair_coef),
-        [shape(padded, cells_dev)],
-        (wanted, area, factor, counts, *members_here),
+        [shape(padded, cells_dev, dtype=BF16)],
+        (wanted, area, factor, *members_here),
+        [pltpu.VMEM((padded, cells_dev), F32)],
     )
     grads = [grad] + [swap(grad, "band", i) for i in range(1, bands)]
     latent_grad, keep, send, mean_loss = call(
@@ -354,14 +362,12 @@
         ],
     )
     total = keep + swap(send, "member", 1)
-    step = 2
-    while step < members:
-        total = total + swap(total, "member", step)
-        step *= 2
-    step = 1
-    while step < bands:
-        total = total + swap(total, "band", step)
-        step *= 2
+    for axis, first, peers in (("member", 2, members), ("band", 1, bands)):
+        step = first
+        while step < peers:
+            rounded = total.astype(BF16)
+            total = rounded.astype(F32) + swap(rounded, axis, step).astype(F32)
+            step *= 2
     other = swap(total, "member", 1)
     latent_out, proj_grad, coef_grad, loss_out = call(
         write_kernel,

time: 51.5 us -> 49.1 us (0.953)
  waiting for transfers between devices: 24.1 us -> 20.9 us
  starting transfers between devices: 16 us -> 16.8 us
    ppermute x14, waiting for transfers between devices: 24.1 us -> 20.9 us  [swap(): return lax.ppermute(shard, axis, [(i, i ^ mask) for i in range(peers)])]
    ppermute x14, starting transfers between devices: 16 us -> 16.8 us  [swap(): return lax.ppermute(shard, axis, [(i, i ^ mask) for i in range(peers)])]
where the time goes in v3:
time: 49.1 us; the launch traced here: 48.9 us
  waiting for transfers between devices  20.9 us (43%)
  starting transfers between devices  16.8 us (34%)
  Pallas kernels  10.5 us (21%)
  between operations  0.73 us (1%)
    ppermute x14, waiting for transfers between devices, swap(): return lax.ppermute(shard, axis, [(i, i ^ mask) for i in range(peers)])  20.9 us
    ppermute x14, starting transfers between devices, swap(): return lax.ppermute(shard, axis, [(i, i ^ mask) for i in range(peers)])  16.8 us
    pallas_call x6, Pallas kernels, call(): pl.pallas_call(kernel, out_shape=outs, in_specs=[source] * len(operands),...  10.5 us
  transfers between devices with their start and end apart: 14, of which 10 were waited for; matrix products, arithmetic and copies ran while one was open for 0% of the time, Pallas kernels for 3%

profile of v3, /device:TPU:0, one launch (start us, length us, event | category | flops | bytes accessed | tf_op | source)
XLA Modules:
  0.0 48.9 jit_solution(10371548406572806602)
XLA Ops:
  0.6 0.0 copy-start.1
  0.6 0.0 copy-start.2
  0.7 0.0 copy-start
  0.7 2.5 %shard_map.120 = (f32[32,384]{1,0:T(8,128)S(1)}, f32[32,384]{1,0:T(8,128)S(1)}, f32[32,384]{1,0:T(8,128)S(1)}, f32[32,384]{1,0:T(8,128)S(1)}, bf16[1024,1024]{1,...) custom-call(bf16[64,1024]{1,0:T(8,128)(2,1)} %bitcast.5, ...), custom_call_target="tpu_custom_call" | custom-call | bytes 1048576 | tf_op jit(solution)/shard_map/pallas_call | solution.py:251
  3.2 3.1 %collective-permute-start = (f32[32,384]{1,0:T(8,128)S(1)}, f32[32,384]{1,0:T(8,128)S(1)}, u32[]{:S(2)}, u32[]{:S(2)}) collective-permute-start(f32[32,384]{1,0:T(8,128)S(1)} %get-tuple-element.24), channel_id=1, source_target_pairs={{0,1},{1,0},{2,3},{3,2},{4,5},{5,4},{6,7},{7,6},{8,9},{9,8},{10,11... | collective-permute-start | bytes 147464 | tf_op jit(solution)/shard_map/ppermute | solution.py:23
  6.2 2.6 %collective-permute-start.1 = (f32[32,384]{1,0:T(8,128)S(1)}, f32[32,384]{1,0:T(8,128)S(1)}, u32[]{:S(2)}, u32[]{:S(2)}) collective-permute-start(f32[32,384]{1,0:T(8,128)S(1)} %get-tuple-element.25), channel_id=1, source_target_pairs={{0,2},{1,3},{2,0},{3,1},{4,6},{5,7},{6,4},{7,5},{8,10},{9,11},{10,... | collective-permute-start | bytes 147464 | tf_op jit(solution)/shard_map/ppermute | solution.py:23
  8.8 0.0 collective-permute-start.2
  8.8 0.0 collective-permute-done.refs_1_
  8.8 3.3 %collective-permute-done.1.refs_2_ = f32[32,384]{1,0:T(8,128)S(1)} collective-permute-done((f32[32,384]{1,0:T(8,128)S(1)}, f32[32,384]{1,0:T(8,128)S(1)}, u32[]{:S(2)}, u32[]{:S(2)}) %collective-permute-start.1) | collective-permute-done | bytes 49184 | tf_op jit(solution)/shard_map/ppermute | solution.py:23
  12.2 2.6 %collective-permute-done.2.refs_3_ = f32[32,384]{1,0:T(8,128)S(1)} collective-permute-done((f32[32,384]{1,0:T(8,128)S(1)}, f32[32,384]{1,0:T(8,128)S(1)}, u32[]{:S(2)}, u32[]{:S(2)}) %collective-permute-start.2) | collective-permute-done | bytes 49184 | tf_op jit(solution)/shard_map/ppermute | solution.py:23
  14.7 0.4 shard_map.122.refs_0_
  15.1 1.6 %collective-permute-start.4 = (f32[32,256]{1,0:T(8,128)S(1)}, f32[32,256]{1,0:T(8,128)S(1)}, u32[]{:S(2)}, u32[]{:S(2)}) collective-permute-start(f32[32,256]{1,0:T(8,128)S(1)} %shard_map.122.refs_0_), channel_id=1, source_target_pairs={{0,8},{4,12},{8,0},{12,4},{1,9},{5,13},{9,1},{13,5},{2,10},{6,14},... | collective-permute-start | bytes 98312 | tf_op jit(solution)/shard_map/ppermute | solution.py:23
  16.6 0.0 collective-permute-start.3
  16.6 2.4 %collective-permute-done.4.refs_2_ = f32[32,256]{1,0:T(8,128)S(1)} collective-permute-done((f32[32,256]{1,0:T(8,128)S(1)}, f32[32,256]{1,0:T(8,128)S(1)}, u32[]{:S(2)}, u32[]{:S(2)}) %collective-permute-start.4) | collective-permute-done | bytes 32800 | tf_op jit(solution)/shard_map/ppermute | solution.py:23
  19.1 0.0 collective-permute-start.5
  19.1 0.0 collective-permute-done.3.refs_1_
  19.1 1.2 %collective-permute-done.5.refs_3_ = f32[32,256]{1,0:T(8,128)S(1)} collective-permute-done((f32[32,256]{1,0:T(8,128)S(1)}, f32[32,256]{1,0:T(8,128)S(1)}, u32[]{:S(2)}, u32[]{:S(2)}) %collective-permute-start.5) | collective-permute-done | bytes 32800 | tf_op jit(solution)/shard_map/ppermute | solution.py:23
  20.3 0.3 shard_map.123.refs_0_
  20.6 0.8 %collective-permute-start.8 = (bf16[32,256]{1,0:T(8,128)(2,1)S(1)}, bf16[32,256]{1,0:T(8,128)(2,1)S(1)}, u32[]{:S(2)}, u32[]{:S(2)}) collective-permute-start(bf16[32,256]{1,0:T(8,128)(2,1)S(1)} %shard_map.123.refs_0_), channel_id=1, source_target_pairs={{0,3},{1,2},{2,1},{3,0},{4,7},{5,6},{6,5},{7,4},{8,11},{9,10},{10,... | collective-permute-start | bytes 49160 | tf_op jit(solution)/shard_map/ppermute | solution.py:23
  21.4 0.0 collective-permute-start.7
  21.4 3.6 %collective-permute-start.6 = (bf16[32,256]{1,0:T(8,128)(2,1)S(1)}, bf16[32,256]{1,0:T(8,128)(2,1)S(1)}, u32[]{:S(2)}, u32[]{:S(2)}) collective-permute-start(bf16[32,256]{1,0:T(8,128)(2,1)S(1)} %shard_map.123.refs_0_), channel_id=1, source_target_pairs={{0,1},{1,0},{2,3},{3,2},{4,5},{5,4},{6,7},{7,6},{8,9},{9,8},{10,11... | collective-permute-start | bytes 49160 | tf_op jit(solution)/shard_map/ppermute | solution.py:23
  25.0 1.3 %shard_map.121.counts = bf16[1024,1024]{1,0:T(8,128)(2,1)S(1)} custom-call(s32[4,1,384]{2,1,0:T(1,128)S(1)} %get-tuple-element.22.pair_ids, f32[32,384]{1,0:T(8,128)S(1)} %get-tuple-element.23.refs_0_, f32[32,384]{1,0:T(8,128)S(1)} %collective-permute-done.refs_1_, f32[32,384]{1,0:T(8,128)S(1)} %collective-permute-done.1.refs_2_, ...), custom_call_target="tpu_custom_call" | custom-call | flops 805306368 | bytes 1048576 | tf_op jit(solution)/shard_map/pallas_call | solution.py:251
  26.3 0.0 collective-permute-done.8.refs_3_
  26.3 0.0 collective-permute-done.7.refs_2_
  26.4 0.4 collective-permute-done.6.refs_1_
  26.8 0.0 copy-done.1
  26.8 0.0 copy-done.2
  26.8 0.0 copy-done
  26.8 4.6 %shard_map.124 = (bf16[64,1024]{1,0:T(8,128)(2,1)S(1)}, f32[48,512]{1,0:T(8,128)S(1)}, f32[48,512]{1,0:T(8,128)S(1)}, f32[1,1]{1,0:T(1,128)}) custom-call(bf16[64,1024]{1,0:T(8,128)(2,1)S(1)} %bitcast.6, bf16[16,1024]{1,0:T(8,128)(2,1)S(1)} %copy-done.2, bf16[25,1024]{1,0:T(8,128)(2,1)S(1)} %copy-done.1, bf16[1024,1024]{1,0:T(8,128)(2,1)S(1)} %shard_map.121.counts, ...), custom_call_target="tpu_custom_call" | custom-call | bytes 1048576 | tf_op jit(solution)/shard_map/pallas_call | solution.py:251
  31.3 0.0 collective-permute-start.9
  31.3 1.3 %collective-permute-done.9 = f32[48,512]{1,0:T(8,128)S(1)} collective-permute-done((f32[48,512]{1,0:T(8,128)S(1)}, f32[48,512]{1,0:T(8,128)S(1)}, u32[]{:S(2)}, u32[]{:S(2)}) %collective-permute-start.9) | collective-permute-done | bytes 98336 | tf_op jit(solution)/shard_map/ppermute | solution.py:23
  32.7 1.6 %collective-permute-start.10 = (bf16[48,512]{1,0:T(8,128)(2,1)S(1)}, bf16[48,512]{1,0:T(8,128)(2,1)S(1)}, u32[]{:S(2)}, u32[]{:S(2)}) collective-permute-start(bf16[48,512]{1,0:T(8,128)(2,1)S(1)} %add_convert_fusion.2), channel_id=1, source_target_pairs={{0,8},{4,12},{8,0},{12,4},{1,9},{5,13},{9,1},{13,5},{2,10},{6,14},... | collective-permute-start | bytes 147464 | tf_op jit(solution)/shard_map/ppermute | solution.py:23
  34.2 2.6 %collective-permute-done.10 = bf16[48,512]{1,0:T(8,128)(2,1)S(1)} collective-permute-done((bf16[48,512]{1,0:T(8,128)(2,1)S(1)}, bf16[48,512]{1,0:T(8,128)(2,1)S(1)}, u32[]{:S(2)}, u32[]{:S(2)}) %collective-permute-start.10) | collective-permute-done | bytes 49184 | tf_op jit(solution)/shard_map/ppermute | solution.py:23
  36.8 2.1 %collective-permute-start.11 = (bf16[48,512]{1,0:T(8,128)(2,1)S(1)}, bf16[48,512]{1,0:T(8,128)(2,1)S(1)}, u32[]{:S(2)}, u32[]{:S(2)}) collective-permute-start(bf16[48,512]{1,0:T(8,128)(2,1)S(1)} %add_convert_fusion.1), channel_id=1, source_target_pairs={{0,1},{1,0},{2,3},{3,2},{4,5},{5,4},{6,7},{7,6},{8,9},{9,8},{10,11... | collective-permute-start | bytes 147464 | tf_op jit(solution)/shard_map/ppermute | solution.py:23
  38.9 2.1 %collective-permute-done.11 = bf16[48,512]{1,0:T(8,128)(2,1)S(1)} collective-permute-done((bf16[48,512]{1,0:T(8,128)(2,1)S(1)}, bf16[48,512]{1,0:T(8,128)(2,1)S(1)}, u32[]{:S(2)}, u32[]{:S(2)}) %collective-permute-start.11) | collective-permute-done | bytes 49184 | tf_op jit(solution)/shard_map/ppermute | solution.py:23
  41.0 1.4 %collective-permute-start.12 = (bf16[48,512]{1,0:T(8,128)(2,1)S(1)}, bf16[48,512]{1,0:T(8,128)(2,1)S(1)}, u32[]{:S(2)}, u32[]{:S(2)}) collective-permute-start(bf16[48,512]{1,0:T(8,128)(2,1)S(1)} %add_convert_fusion), channel_id=1, source_target_pairs={{0,2},{1,3},{2,0},{3,1},{4,6},{5,7},{6,4},{7,5},{8,10},{9,11},{10,... | collective-permute-start | bytes 147464 | tf_op jit(solution)/shard_map/ppermute | solution.py:23
  42.4 3.7 %collective-permute-done.12 = bf16[48,512]{1,0:T(8,128)(2,1)S(1)} collective-permute-done((bf16[48,512]{1,0:T(8,128)(2,1)S(1)}, bf16[48,512]{1,0:T(8,128)(2,1)S(1)}, u32[]{:S(2)}, u32[]{:S(2)}) %collective-permute-start.12) | collective-permute-done | bytes 49184 | tf_op jit(solution)/shard_map/ppermute | solution.py:23
  46.1 0.1 collective-permute-start.13
  46.2 1.3 %collective-permute-done.13.other = f32[48,512]{1,0:T(8,128)S(1)} collective-permute-done((f32[48,512]{1,0:T(8,128)S(1)}, f32[48,512]{1,0:T(8,128)S(1)}, u32[]{:S(2)}, u32[]{:S(2)}) %collective-permute-start.13) | collective-permute-done | bytes 98336 | tf_op jit(solution)/shard_map/ppermute | solution.py:23
  47.5 1.4 %shard_map.125 = (bf16[64,1024]{1,0:T(8,128)(2,1)}, f32[25,1024]{1,0:T(8,128)}, f32[16,1024]{1,0:T(8,128)}, f32[1,1]{1,0:T(1,128)}) custom-call(f32[48,512]{1,0:T(8,128)S(1)} %convert_add_fusion.scaled, f32[48,512]{1,0:T(8,128)S(1)} %collective-permute-done.13.other, bf16[64,1024]{1,0:T(8,128)(2,1)S(1)} %get-tuple-element.34.latent_grad, ...), custom_call_target="tpu_custom_call" | custom-call | bytes 1048576 | tf_op jit(solution)/shard_map/pallas_call | solution.py:251
  (4 shorter events, 0.1 us)
Async XLA Ops:
  0.6 26.1 %copy-start.1 = (bf16[25,1024]{1,0:T(8,128)(2,1)S(1)}, bf16[25,1024]{1,0:T(8,128)(2,1)}, u32[]{:S(2)}) copy-start(bf16[25,1024]{1,0:T(8,128)(2,1)} %proj.1) | copy-start | bytes 153604
  0.6 26.1 %copy-start.2 = (bf16[16,1024]{1,0:T(8,128)(2,1)S(1)}, bf16[16,1024]{1,0:T(8,128)(2,1)}, u32[]{:S(2)}) copy-start(bf16[16,1024]{1,0:T(8,128)(2,1)} %coef.1) | copy-start | bytes 98308
  0.7 26.1 %copy-start = (bf16[1,64,1024]{2,1,0:T(8,128)(2,1)S(1)}, bf16[1,64,1024]{2,1,0:T(8,128)(2,1)}, u32[]{:S(2)}) copy-start(bf16[1,64,1024]{2,1,0:T(8,128)(2,1)} %param.9) | copy-start | bytes 393220
  3.2 5.7 %collective-permute-start = (f32[32,384]{1,0:T(8,128)S(1)}, f32[32,384]{1,0:T(8,128)S(1)}, u32[]{:S(2)}, u32[]{:S(2)}) collective-permute-start(f32[32,384]{1,0:T(8,128)S(1)} %get-tuple-element.24), channel_id=1, source_target_pairs={{0,1},{1,0},{2,3},{3,2},{4,5},{5,4},{6,7},{7,6},{8,9},{9,8},{10,11... | collective-permute-start | bytes 147464 | tf_op jit(solution)/shard_map/ppermute | solution.py:23
  6.2 5.9 %collective-permute-start.1 = (f32[32,384]{1,0:T(8,128)S(1)}, f32[32,384]{1,0:T(8,128)S(1)}, u32[]{:S(2)}, u32[]{:S(2)}) collective-permute-start(f32[32,384]{1,0:T(8,128)S(1)} %get-tuple-element.25), channel_id=1, source_target_pairs={{0,2},{1,3},{2,0},{3,1},{4,6},{5,7},{6,4},{7,5},{8,10},{9,11},{10,... | collective-permute-start | bytes 147464 | tf_op jit(solution)/shard_map/ppermute | solution.py:23
  8.8 5.9 %collective-permute-start.2 = (f32[32,384]{1,0:T(8,128)S(1)}, f32[32,384]{1,0:T(8,128)S(1)}, u32[]{:S(2)}, u32[]{:S(2)}) collective-permute-start(f32[32,384]{1,0:T(8,128)S(1)} %get-tuple-element.26), channel_id=1, source_target_pairs={{0,3},{1,2},{2,1},{3,0},{4,7},{5,6},{6,5},{7,4},{8,11},{9,10},{10,... | collective-permute-start | bytes 147464 | tf_op jit(solution)/shard_map/ppermute | solution.py:23
  15.1 4.0 %collective-permute-start.4 = (f32[32,256]{1,0:T(8,128)S(1)}, f32[32,256]{1,0:T(8,128)S(1)}, u32[]{:S(2)}, u32[]{:S(2)}) collective-permute-start(f32[32,256]{1,0:T(8,128)S(1)} %shard_map.122.refs_0_), channel_id=1, source_target_pairs={{0,8},{4,12},{8,0},{12,4},{1,9},{5,13},{9,1},{13,5},{2,10},{6,14},... | collective-permute-start | bytes 98312 | tf_op jit(solution)/shard_map/ppermute | solution.py:23
  16.6 2.4 %collective-permute-start.3 = (f32[32,256]{1,0:T(8,128)S(1)}, f32[32,256]{1,0:T(8,128)S(1)}, u32[]{:S(2)}, u32[]{:S(2)}) collective-permute-start(f32[32,256]{1,0:T(8,128)S(1)} %shard_map.122.refs_0_), channel_id=1, source_target_pairs={{0,4},{4,0},{8,12},{12,8},{1,5},{5,1},{9,13},{13,9},{2,6},{6,2},{1... | collective-permute-start | bytes 98312 | tf_op jit(solution)/shard_map/ppermute | solution.py:23
  19.1 1.2 %collective-permute-start.5 = (f32[32,256]{1,0:T(8,128)S(1)}, f32[32,256]{1,0:T(8,128)S(1)}, u32[]{:S(2)}, u32[]{:S(2)}) collective-permute-start(f32[32,256]{1,0:T(8,128)S(1)} %collective-permute-done.4.refs_2_), channel_id=1, source_target_pairs={{0,4},{4,0},{8,12},{12,8},{1,5},{5,1},{9,13},{13,9},{2,6},{6,2},{1... | collective-permute-start | bytes 98312 | tf_op jit(solution)/shard_map/ppermute | solution.py:23
  20.6 5.8 %collective-permute-start.8 = (bf16[32,256]{1,0:T(8,128)(2,1)S(1)}, bf16[32,256]{1,0:T(8,128)(2,1)S(1)}, u32[]{:S(2)}, u32[]{:S(2)}) collective-permute-start(bf16[32,256]{1,0:T(8,128)(2,1)S(1)} %shard_map.123.refs_0_), channel_id=1, source_target_pairs={{0,3},{1,2},{2,1},{3,0},{4,7},{5,6},{6,5},{7,4},{8,11},{9,10},{10,... | collective-permute-start | bytes 49160 | tf_op jit(solution)/shard_map/ppermute | solution.py:23
  21.4 5.0 %collective-permute-start.7 = (bf16[32,256]{1,0:T(8,128)(2,1)S(1)}, bf16[32,256]{1,0:T(8,128)(2,1)S(1)}, u32[]{:S(2)}, u32[]{:S(2)}) collective-permute-start(bf16[32,256]{1,0:T(8,128)(2,1)S(1)} %shard_map.123.refs_0_), channel_id=1, source_target_pairs={{0,2},{1,3},{2,0},{3,1},{4,6},{5,7},{6,4},{7,5},{8,10},{9,11},{10,... | collective-permute-start | bytes 49160 | tf_op jit(solution)/shard_map/ppermute | solution.py:23
  21.4 5.4 %collective-permute-start.6 = (bf16[32,256]{1,0:T(8,128)(2,1)S(1)}, bf16[32,256]{1,0:T(8,128)(2,1)S(1)}, u32[]{:S(2)}, u32[]{:S(2)}) collective-permute-start(bf16[32,256]{1,0:T(8,128)(2,1)S(1)} %shard_map.123.refs_0_), channel_id=1, source_target_pairs={{0,1},{1,0},{2,3},{3,2},{4,5},{5,4},{6,7},{7,6},{8,9},{9,8},{10,11... | collective-permute-start | bytes 49160 | tf_op jit(solution)/shard_map/ppermute | solution.py:23
  31.3 1.3 %collective-permute-start.9 = (f32[48,512]{1,0:T(8,128)S(1)}, f32[48,512]{1,0:T(8,128)S(1)}, u32[]{:S(2)}, u32[]{:S(2)}) collective-permute-start(f32[48,512]{1,0:T(8,128)S(1)} %get-tuple-element.33), channel_id=1, source_target_pairs={{0,4},{4,0},{8,12},{12,8},{1,5},{5,1},{9,13},{13,9},{2,6},{6,2},{1... | collective-permute-start | bytes 294920 | tf_op jit(solution)/shard_map/ppermute | solution.py:23
  32.7 4.2 %collective-permute-start.10 = (bf16[48,512]{1,0:T(8,128)(2,1)S(1)}, bf16[48,512]{1,0:T(8,128)(2,1)S(1)}, u32[]{:S(2)}, u32[]{:S(2)}) collective-permute-start(bf16[48,512]{1,0:T(8,128)(2,1)S(1)} %add_convert_fusion.2), channel_id=1, source_target_pairs={{0,8},{4,12},{8,0},{12,4},{1,9},{5,13},{9,1},{13,5},{2,10},{6,14},... | collective-permute-start | bytes 147464 | tf_op jit(solution)/shard_map/ppermute | solution.py:23
  36.8 4.2 %collective-permute-start.11 = (bf16[48,512]{1,0:T(8,128)(2,1)S(1)}, bf16[48,512]{1,0:T(8,128)(2,1)S(1)}, u32[]{:S(2)}, u32[]{:S(2)}) collective-permute-start(bf16[48,512]{1,0:T(8,128)(2,1)S(1)} %add_convert_fusion.1), channel_id=1, source_target_pairs={{0,1},{1,0},{2,3},{3,2},{4,5},{5,4},{6,7},{7,6},{8,9},{9,8},{10,11... | collective-permute-start | bytes 147464 | tf_op jit(solution)/shard_map/ppermute | solution.py:23
  41.0 5.1 %collective-permute-start.12 = (bf16[48,512]{1,0:T(8,128)(2,1)S(1)}, bf16[48,512]{1,0:T(8,128)(2,1)S(1)}, u32[]{:S(2)}, u32[]{:S(2)}) collective-permute-start(bf16[48,512]{1,0:T(8,128)(2,1)S(1)} %add_convert_fusion), channel_id=1, source_target_pairs={{0,2},{1,3},{2,0},{3,1},{4,6},{5,7},{6,4},{7,5},{8,10},{9,11},{10,... | collective-permute-start | bytes 147464 | tf_op jit(solution)/shard_map/ppermute | solution.py:23
  46.1 1.4 %collective-permute-start.13 = (f32[48,512]{1,0:T(8,128)S(1)}, f32[48,512]{1,0:T(8,128)S(1)}, u32[]{:S(2)}, u32[]{:S(2)}) collective-permute-start(f32[48,512]{1,0:T(8,128)S(1)} %convert_add_fusion.scaled), channel_id=1, source_target_pairs={{0,4},{4,0},{8,12},{12,8},{1,5},{5,1},{9,13},{13,9},{2,6},{6,2},{1... | collective-permute-start | bytes 294920 | tf_op jit(solution)/shard_map/ppermute | solution.py:23

commit v4 on v3

--- a/solution.py
+++ b/solution.py
@@ -21,6 +21,31 @@
 def swap(shard, axis, mask):
     peers = lax.axis_size(axis)
     return lax.ppermute(shard, axis, [(i, i ^ mask) for i in range(peers)])
+
+
+def cross(shard, member_mask, band_mask):
+    members, bands = lax.axis_size("member"), lax.axis_size("band")
+    pairs = [
+        (m * bands + b, (m ^ member_mask) * bands + (b ^ band_mask))
+        for m in range(members)
+        for b in range(bands)
+    ]
+    return lax.ppermute(shard, ("member", "band"), pairs)
+
+
+def odd(value):
+    return value.bit_count() & 1
+
+
+def parity(index, peers):
+    found = 0
+    for bit in range(peers.bit_length() - 1):
+        found = lax.bitwise_xor(found, lax.bitwise_and(lax.shift_right_logical(index, bit), 1))
+    return found
+
+
+def half_here(members, bands):
+    return lax.bitwise_xor(parity(lax.axis_index("member"), members), parity(lax.axis_index("band"), bands))
 
 
 def soft_abs(values):
@@ -112,6 +137,7 @@
 
 def predict_kernel(variables, *refs):
     *payloads, target, predicted = refs
+    payloads = payloads[::-1]
     bands = len(payloads)
     here = lax.axis_index("band")
     total = 0.0
@@ -126,6 +152,7 @@
 
 def count_kernel(variables, cells_dev, pair_ids, *refs):
     *payloads, counts = refs
+    payloads = payloads[::-1]
     for i, payload in enumerate(payloads):
         cells = payload[variables : variables + 1, :].astype(jnp.int32)
         block = dot(hot(pair_ids[i], counts.shape[0]), hot(cells, cells_dev), 1, 1)
@@ -135,7 +162,7 @@
 def grade_kernel(pair_coef, target, area, var_weight, *refs):
     *predicted, grad, rows = refs
     members = len(predicted)
-    here = lax.axis_index("member")
+    here = lax.bitwise_xor(lax.axis_index("member"), 1)
     variables = target.shape[0]
     wanted = target[...]
     spots = lax.broadcasted_iota(jnp.int32, (variables, variables), 0)
@@ -171,11 +198,11 @@
     grad[...] = rows[...].astype(BF16)
 
 
-def backward_kernel(scale_proj, scale_coef, scale_loss, latent, coef, proj, counts, products, *refs):
+def backward_kernel(members, scale_proj, scale_coef, scale_loss, latent, coef, proj, counts, products, *refs):
     *grads, latent_grad, keep, send, mean_loss, proj_pad, cell_grad, sums = refs
     bands = len(grads)
     band = lax.axis_index("band")
-    side = lax.bitwise_and(lax.axis_index("member"), 1)
+    side = half_here(members, bands)
     variables = proj.shape[0]
     rows, hidden = latent.shape
     table = coef.shape[0]
@@ -216,32 +243,28 @@
     send[...] = jnp.where(side == 0, right, left)
 
 
-def write_kernel(scaled, other, latent_grad, mean_loss, *refs):
-    latent_out, proj_out, coef_out, loss_out, proj, coef, leaves = refs
-    early = [
-        pltpu.make_async_copy(latent_grad, latent_out, leaves.at[0]),
-        pltpu.make_async_copy(mean_loss, loss_out, leaves.at[1]),
+def write_kernel(members, bands, variables, scaled, other, latent_grad, mean_loss, *refs):
+    latent_out, proj_out, coef_out, loss_out, proj, leaves = refs
+    side = half_here(members, bands)
+    half = scaled.shape[1]
+    first = scaled.shape[0] - coef_out.shape[0]
+    here = pl.ds(pl.multiple_of(side * half, half), half)
+    there = pl.ds(pl.multiple_of((1 - side) * half, half), half)
+    moves = [
+        (scaled.at[first:, :], coef_out.at[:, here]),
+        (other.at[first:, :], coef_out.at[:, there]),
+        (latent_grad, latent_out),
+        (mean_loss, loss_out),
+        (proj, proj_out),
     ]
-    for move in early:
+    moves = [pltpu.make_async_copy(*move, leaves.at[n]) for n, move in enumerate(moves)]
+    for move in moves[:-1]:
         move.start()
-    side = lax.bitwise_and(lax.axis_index("member"), 1)
-    half = scaled.shape[1]
-    variables, table = proj.shape[0], coef.shape[0]
-    first = scaled.shape[0] - table
-    here, there = scaled[...], other[...]
-    left = jnp.where(side == 0, here, there)
-    right = jnp.where(side == 0, there, here)
-    proj[:, 0:half] = left[0:variables]
-    proj[:, half : 2 * half] = right[0:variables]
-    coef[:, 0:half] = left[first:]
-    coef[:, half : 2 * half] = right[first:]
-    late = [
-        pltpu.make_async_copy(proj, proj_out, leaves.at[2]),
-        pltpu.make_async_copy(coef, coef_out, leaves.at[3]),
-    ]
-    for move in late:
-        move.start()
-    for move in early + late:
+    mine, theirs = scaled[0:variables, :], other[0:variables, :]
+    proj[:, 0:half] = jnp.where(side == 0, mine, theirs)
+    proj[:, half:] = jnp.where(side == 0, theirs, mine)
+    moves[-1].start()
+    for move in moves:
         move.wait()
 
 
@@ -319,7 +342,7 @@
         ],
         source=HBM,
     )
-    arrived = [payloads[0]] + [swap(payloads[i], "band", i) for i in range(1, bands)]
+    arrived = [cross(payloads[i], 1, i) for i in range(bands)][::-1]
     (predicted,) = call(
         functools.partial(predict_kernel, variables),
         [shape(padded, cells_dev)],
@@ -331,19 +354,21 @@
         (pair_ids, *arrived),
         flops=2 * pairs * slots * cells_all,
     )
-    members_here = [predicted]
-    for i in range(1, members):
-        members_here.append(swap(members_here[i ^ 1], "member", 1) if i & 1 else swap(predicted, "member", i))
+    members_here = [predicted, swap(predicted, "member", 1)]
+    for i in range(2, members, 2):
+        far = cross(predicted, i + 1, 0)
+        members_here += [swap(far, "member", 1), far]
     (grad,) = call(
         functools.partial(grade_kernel, pair_coef),
         [shape(padded, cells_dev, dtype=BF16)],
         (wanted, area, factor, *members_here),
         [pltpu.VMEM((padded, cells_dev), F32)],
     )
-    grads = [grad] + [swap(grad, "band", i) for i in range(1, bands)]
+    grads = [cross(grad, 1, i) for i in range(bands)]
     latent_grad, keep, send, mean_loss = call(
         functools.partial(
             backward_kernel,
+            members,
             1.0 / math.sqrt(members * cells_all),
             1.0 / math.sqrt(members * cells_all * K),
             1.0 / (members * variables * cells_all),
@@ -362,15 +387,22 @@
         ],
     )
     total = keep + swap(send, "member", 1)
-    for axis, first, peers in (("member", 2, members), ("band", 1, bands)):
-        step = first
-        while step < peers:
-            rounded = total.astype(BF16)
-            total = rounded.astype(F32) + swap(rounded, axis, step).astype(F32)
-            step *= 2
+    step = 2
+    while step < members:
+        rounded = total.astype(BF16)
+        total = rounded.astype(F32) + cross(rounded, step + 1, 0).astype(F32)
+        step *= 2
+    step = 1
+    while step < bands:
+        rounded = total.astype(BF16)
+        total = rounded.astype(F32) + cross(rounded, odd(step), step).astype(F32)
+        if 2 * step < bands:
+            far = [cross(rounded, odd(step * k), step * k).astype(F32) for k in (2, 3)]
+            total = total + (far[0] + far[1])
+        step *= 4
     other = swap(total, "member", 1)
     latent_out, proj_grad, coef_grad, loss_out = call(
-        write_kernel,
+        functools.partial(write_kernel, members, bands, variables),
         [
             shape(rows, hidden, dtype=BF16),
             shape(variables, hidden),
@@ -378,11 +410,7 @@
             shape(1, 1),
         ],
         (total, other, latent_grad, mean_loss),
-        [
-            pltpu.VMEM((variables, hidden), F32),
-            pltpu.VMEM((table, hidden), F32),
-            pltpu.SemaphoreType.DMA((4,)),
-        ],
+        [pltpu.VMEM((variables, hidden), F32), pltpu.SemaphoreType.DMA((5,))],
         sink=HBM,
     )
     return (latent_out[None], proj_grad, coef_grad, loss_out.reshape(1))

time: 49.1 us -> 45.4 us (0.925)
  waiting for transfers between devices: 20.9 us -> 16.5 us
  starting transfers between devices: 16.8 us -> 17.5 us
    ppermute x14 -> x4, waiting for transfers between devices: 20.9 us -> 3.15 us  [swap(): return lax.ppermute(shard, axis, [(i, i ^ mask) for i in range(peers)])]
    ppermute x0 -> x13, starting transfers between devices: none -> 16.6 us  [cross(): return lax.ppermute(shard, ('member', 'band'), pairs)]
    ppermute x14 -> x4, starting transfers between devices: 16.8 us -> 0.93 us  [swap(): return lax.ppermute(shard, axis, [(i, i ^ mask) for i in range(peers)])]
    ppermute x0 -> x13, waiting for transfers between devices: none -> 13.4 us  [cross(): return lax.ppermute(shard, ('member', 'band'), pairs)]
  transfers between devices with their start and end apart: 14 -> 17, of which waited for: 10 -> 10; matrix products, arithmetic and copies ran while one was open for 0% -> 0% of each run, Pallas kernels for 3% -> 3%
where the time goes in v4:
time: 45.4 us; the launch traced here: 45.2 us
  starting transfers between devices  17.5 us (39%)
  waiting for transfers between devices  16.5 us (36%)
  Pallas kernels  10.4 us (23%)
  between operations  0.73 us (2%)
    ppermute x13, starting transfers between devices, cross(): return lax.ppermute(shard, ('member', 'band'), pairs)  16.6 us
    ppermute x13, waiting for transfers between devices, cross(): return lax.ppermute(shard, ('member', 'band'), pairs)  13.4 us
    pallas_call x6, Pallas kernels, call(): pl.pallas_call(kernel, out_shape=outs, in_specs=[source] * len(operands),...  10.4 us
    ppermute x4, waiting for transfers between devices, swap(): return lax.ppermute(shard, axis, [(i, i ^ mask) for i in range(peers)])  3.15 us
    ppermute x4, starting transfers between devices, swap(): return lax.ppermute(shard, axis, [(i, i ^ mask) for i in range(peers)])  0.93 us
  transfers between devices with their start and end apart: 17, of which 10 were waited for; matrix products, arithmetic and copies ran while one was open for 0% of the time, Pallas kernels for 3%

profile of v4, /device:TPU:0, one launch (start us, length us, event | category | flops | bytes accessed | tf_op | source)
XLA Modules:
  0.0 45.2 jit_solution(17142499009966209441)
XLA Ops:
  0.6 0.0 copy-start.1
  0.6 0.0 copy-start.2
  0.7 0.0 copy-start
  0.7 2.5 %shard_map.120 = (f32[32,384]{1,0:T(8,128)S(1)}, f32[32,384]{1,0:T(8,128)S(1)}, f32[32,384]{1,0:T(8,128)S(1)}, f32[32,384]{1,0:T(8,128)S(1)}, bf16[1024,1024]{1,...) custom-call(bf16[64,1024]{1,0:T(8,128)(2,1)} %bitcast.5, ...), custom_call_target="tpu_custom_call" | custom-call | bytes 1048576 | tf_op jit(solution)/shard_map/pallas_call | solution.py:274
  3.2 4.6 %collective-permute-start = (f32[32,384]{1,0:T(8,128)S(1)}, f32[32,384]{1,0:T(8,128)S(1)}, u32[]{:S(2)}, u32[]{:S(2)}) collective-permute-start(f32[32,384]{1,0:T(8,128)S(1)} %get-tuple-element.23), channel_id=1, source_target_pairs={{0,7},{1,6},{2,5},{3,4},{4,3},{5,2},{6,1},{7,0},{8,15},{9,14},{10,... | collective-permute-start | bytes 147464 | tf_op jit(solution)/shard_map/ppermute | solution.py:33
  7.7 0.0 collective-permute-start.1
  7.7 0.9 %collective-permute-start.2 = (f32[32,384]{1,0:T(8,128)S(1)}, f32[32,384]{1,0:T(8,128)S(1)}, u32[]{:S(2)}, u32[]{:S(2)}) collective-permute-start(f32[32,384]{1,0:T(8,128)S(1)} %get-tuple-element.25), channel_id=1, source_target_pairs={{0,5},{1,4},{2,7},{3,6},{4,1},{5,0},{6,3},{7,2},{8,13},{9,12},{10,... | collective-permute-start | bytes 147464 | tf_op jit(solution)/shard_map/ppermute | solution.py:33
  8.6 0.0 collective-permute-start.3
  8.6 1.3 %collective-permute-done.refs_0_ = f32[32,384]{1,0:T(8,128)S(1)} collective-permute-done((f32[32,384]{1,0:T(8,128)S(1)}, f32[32,384]{1,0:T(8,128)S(1)}, u32[]{:S(2)}, u32[]{:S(2)}) %collective-permute-start) | collective-permute-done | bytes 49184 | tf_op jit(solution)/shard_map/ppermute | solution.py:33
  9.9 2.8 %collective-permute-done.1.refs_1_ = f32[32,384]{1,0:T(8,128)S(1)} collective-permute-done((f32[32,384]{1,0:T(8,128)S(1)}, f32[32,384]{1,0:T(8,128)S(1)}, u32[]{:S(2)}, u32[]{:S(2)}) %collective-permute-start.1) | collective-permute-done | bytes 49184 | tf_op jit(solution)/shard_map/ppermute | solution.py:33
  12.7 0.0 collective-permute-done.2.refs_2_
  12.7 0.0 collective-permute-done.3.refs_3_
  12.7 0.4 shard_map.122.refs_0_
  13.0 1.5 %collective-permute-start.5 = (f32[32,256]{1,0:T(8,128)S(1)}, f32[32,256]{1,0:T(8,128)S(1)}, u32[]{:S(2)}, u32[]{:S(2)}) collective-permute-start(f32[32,256]{1,0:T(8,128)S(1)} %shard_map.122.refs_0_), channel_id=1, source_target_pairs={{0,12},{1,13},{2,14},{3,15},{4,8},{5,9},{6,10},{7,11},{8,4},{9,5},... | collective-permute-start | bytes 98312 | tf_op jit(solution)/shard_map/ppermute | solution.py:33
  14.5 0.2 collective-permute-start.4
  14.7 1.7 %collective-permute-done.5.refs_3_ = f32[32,256]{1,0:T(8,128)S(1)} collective-permute-done((f32[32,256]{1,0:T(8,128)S(1)}, f32[32,256]{1,0:T(8,128)S(1)}, u32[]{:S(2)}, u32[]{:S(2)}) %collective-permute-start.5) | collective-permute-done | bytes 32800 | tf_op jit(solution)/shard_map/ppermute | solution.py:33
  16.4 0.3 collective-permute-start.6
  16.7 0.0 collective-permute-done.4.refs_1_
  16.7 0.9 %collective-permute-done.6.refs_2_ = f32[32,256]{1,0:T(8,128)S(1)} collective-permute-done((f32[32,256]{1,0:T(8,128)S(1)}, f32[32,256]{1,0:T(8,128)S(1)}, u32[]{:S(2)}, u32[]{:S(2)}) %collective-permute-start.6) | collective-permute-done | bytes 32800 | tf_op jit(solution)/shard_map/ppermute | solution.py:23
  17.6 0.3 shard_map.123
  18.0 2.6 %collective-permute-start.10 = (bf16[32,256]{1,0:T(8,128)(2,1)S(1)}, bf16[32,256]{1,0:T(8,128)(2,1)S(1)}, u32[]{:S(2)}, u32[]{:S(2)}) collective-permute-start(bf16[32,256]{1,0:T(8,128)(2,1)S(1)} %shard_map.123), channel_id=1, source_target_pairs={{0,7},{1,6},{2,5},{3,4},{4,3},{5,2},{6,1},{7,0},{8,15},{9,14},{10,... | collective-permute-start | bytes 49160 | tf_op jit(solution)/shard_map/ppermute | solution.py:33
  20.6 0.5 %collective-permute-start.9 = (bf16[32,256]{1,0:T(8,128)(2,1)S(1)}, bf16[32,256]{1,0:T(8,128)(2,1)S(1)}, u32[]{:S(2)}, u32[]{:S(2)}) collective-permute-start(bf16[32,256]{1,0:T(8,128)(2,1)S(1)} %shard_map.123), channel_id=1, source_target_pairs={{0,6},{1,7},{2,4},{3,5},{4,2},{5,3},{6,0},{7,1},{8,14},{9,15},{10,... | collective-permute-start | bytes 49160 | tf_op jit(solution)/shard_map/ppermute | solution.py:33
  21.0 1.0 %collective-permute-start.8 = (bf16[32,256]{1,0:T(8,128)(2,1)S(1)}, bf16[32,256]{1,0:T(8,128)(2,1)S(1)}, u32[]{:S(2)}, u32[]{:S(2)}) collective-permute-start(bf16[32,256]{1,0:T(8,128)(2,1)S(1)} %shard_map.123), channel_id=1, source_target_pairs={{0,5},{1,4},{2,7},{3,6},{4,1},{5,0},{6,3},{7,2},{8,13},{9,12},{10,... | collective-permute-start | bytes 49160 | tf_op jit(solution)/shard_map/ppermute | solution.py:33
  22.0 0.2 collective-permute-start.7
  22.2 1.3 %shard_map.121.counts = bf16[1024,1024]{1,0:T(8,128)(2,1)S(1)} custom-call(s32[4,1,384]{2,1,0:T(1,128)S(1)} %get-tuple-element.22.pair_ids, f32[32,384]{1,0:T(8,128)S(1)} %collective-permute-done.refs_0_, f32[32,384]{1,0:T(8,128)S(1)} %collective-permute-done.1.refs_1_, f32[32,384]{1,0:T(8,128)S(1)} %collective-permute-done.2.refs_2_, ...), custom_call_target="tpu_custom_call" | custom-call | flops 805306368 | bytes 1048576 | tf_op jit(solution)/shard_map/pallas_call | solution.py:274
  23.5 0.0 collective-permute-done.10.refs_3_
  23.6 1.2 %collective-permute-done.9.refs_2_ = bf16[32,256]{1,0:T(8,128)(2,1)S(1)} collective-permute-done((bf16[32,256]{1,0:T(8,128)(2,1)S(1)}, bf16[32,256]{1,0:T(8,128)(2,1)S(1)}, u32[]{:S(2)}, u32[]{:S(2)}) %collective-permute-start.9) | collective-permute-done | bytes 16416 | tf_op jit(solution)/shard_map/ppermute | solution.py:33
  24.7 0.0 collective-permute-done.8.refs_1_
  24.7 0.0 collective-permute-done.7.refs_0_
  24.7 0.0 copy-done.1
  24.7 0.0 copy-done.2
  24.7 0.0 copy-done
  24.7 4.5 %shard_map.124 = (bf16[64,1024]{1,0:T(8,128)(2,1)S(1)}, f32[48,512]{1,0:T(8,128)S(1)}, f32[48,512]{1,0:T(8,128)S(1)}, f32[1,1]{1,0:T(1,128)}) custom-call(bf16[64,1024]{1,0:T(8,128)(2,1)S(1)} %bitcast.6, bf16[16,1024]{1,0:T(8,128)(2,1)S(1)} %copy-done.2, bf16[25,1024]{1,0:T(8,128)(2,1)S(1)} %copy-done.1, bf16[1024,1024]{1,0:T(8,128)(2,1)S(1)} %shard_map.121.counts, ...), custom_call_target="tpu_custom_call" | custom-call | bytes 1048576 | tf_op jit(solution)/shard_map/pallas_call | solution.py:274
  29.3 0.3 collective-permute-start.11
  29.5 1.0 %collective-permute-done.11 = f32[48,512]{1,0:T(8,128)S(1)} collective-permute-done((f32[48,512]{1,0:T(8,128)S(1)}, f32[48,512]{1,0:T(8,128)S(1)}, u32[]{:S(2)}, u32[]{:S(2)}) %collective-permute-start.11) | collective-permute-done | bytes 98336 | tf_op jit(solution)/shard_map/ppermute | solution.py:23
  30.6 1.2 %collective-permute-start.12 = (bf16[48,512]{1,0:T(8,128)(2,1)S(1)}, bf16[48,512]{1,0:T(8,128)(2,1)S(1)}, u32[]{:S(2)}, u32[]{:S(2)}) collective-permute-start(bf16[48,512]{1,0:T(8,128)(2,1)S(1)} %add_convert_fusion.1), channel_id=1, source_target_pairs={{0,12},{1,13},{2,14},{3,15},{4,8},{5,9},{6,10},{7,11},{8,4},{9,5},... | collective-permute-start | bytes 147464 | tf_op jit(solution)/shard_map/ppermute | solution.py:33
  31.8 2.5 %collective-permute-done.12 = bf16[48,512]{1,0:T(8,128)(2,1)S(1)} collective-permute-done((bf16[48,512]{1,0:T(8,128)(2,1)S(1)}, bf16[48,512]{1,0:T(8,128)(2,1)S(1)}, u32[]{:S(2)}, u32[]{:S(2)}) %collective-permute-start.12) | collective-permute-done | bytes 49184 | tf_op jit(solution)/shard_map/ppermute | solution.py:33
  34.4 1.8 %collective-permute-start.15 = (bf16[48,512]{1,0:T(8,128)(2,1)S(1)}, bf16[48,512]{1,0:T(8,128)(2,1)S(1)}, u32[]{:S(2)}, u32[]{:S(2)}) collective-permute-start(bf16[48,512]{1,0:T(8,128)(2,1)S(1)} %add_convert_fusion), channel_id=1, source_target_pairs={{0,3},{1,2},{2,1},{3,0},{4,7},{5,6},{6,5},{7,4},{8,11},{9,10},{10,... | collective-permute-start | bytes 147464 | tf_op jit(solution)/shard_map/ppermute | solution.py:33
  36.2 0.0 collective-permute-start.14
  36.2 2.4 %collective-permute-start.13 = (bf16[48,512]{1,0:T(8,128)(2,1)S(1)}, bf16[48,512]{1,0:T(8,128)(2,1)S(1)}, u32[]{:S(2)}, u32[]{:S(2)}) collective-permute-start(bf16[48,512]{1,0:T(8,128)(2,1)S(1)} %add_convert_fusion), channel_id=1, source_target_pairs={{0,5},{1,4},{2,7},{3,6},{4,1},{5,0},{6,3},{7,2},{8,13},{9,12},{10,... | collective-permute-start | bytes 147464 | tf_op jit(solution)/shard_map/ppermute | solution.py:33
  38.5 2.0 %collective-permute-done.15 = bf16[48,512]{1,0:T(8,128)(2,1)S(1)} collective-permute-done((bf16[48,512]{1,0:T(8,128)(2,1)S(1)}, bf16[48,512]{1,0:T(8,128)(2,1)S(1)}, u32[]{:S(2)}, u32[]{:S(2)}) %collective-permute-start.15) | collective-permute-done | bytes 49184 | tf_op jit(solution)/shard_map/ppermute | solution.py:33
  40.6 1.9 %collective-permute-done.14 = bf16[48,512]{1,0:T(8,128)(2,1)S(1)} collective-permute-done((bf16[48,512]{1,0:T(8,128)(2,1)S(1)}, bf16[48,512]{1,0:T(8,128)(2,1)S(1)}, u32[]{:S(2)}, u32[]{:S(2)}) %collective-permute-start.14) | collective-permute-done | bytes 49184 | tf_op jit(solution)/shard_map/ppermute | solution.py:33
  42.4 0.0 collective-permute-done.13
  42.5 0.2 collective-permute-start.16
  42.6 1.2 %collective-permute-done.16.other = f32[48,512]{1,0:T(8,128)S(1)} collective-permute-done((f32[48,512]{1,0:T(8,128)S(1)}, f32[48,512]{1,0:T(8,128)S(1)}, u32[]{:S(2)}, u32[]{:S(2)}) %collective-permute-start.16) | collective-permute-done | bytes 98336 | tf_op jit(solution)/shard_map/ppermute | solution.py:23
  43.8 1.4 %shard_map.125 = (bf16[64,1024]{1,0:T(8,128)(2,1)}, f32[25,1024]{1,0:T(8,128)}, f32[16,1024]{1,0:T(8,128)}, f32[1,1]{1,0:T(1,128)}) custom-call(f32[48,512]{1,0:T(8,128)S(1)} %add_add_fusion.scaled, f32[48,512]{1,0:T(8,128)S(1)} %collective-permute-done.16.other, bf16[64,1024]{1,0:T(8,128)(2,1)S(1)} %get-tuple-element.34.latent_grad, ...), custom_call_target="tpu_custom_call" | custom-call | bytes 1048576 | tf_op jit(solution)/shard_map/pallas_call | solution.py:274
  (3 shorter events, 0.1 us)
Async XLA Ops:
  0.6 24.1 %copy-start.1 = (bf16[25,1024]{1,0:T(8,128)(2,1)S(1)}, bf16[25,1024]{1,0:T(8,128)(2,1)}, u32[]{:S(2)}) copy-start(bf16[25,1024]{1,0:T(8,128)(2,1)} %proj.1) | copy-start | bytes 153604
  0.6 24.1 %copy-start.2 = (bf16[16,1024]{1,0:T(8,128)(2,1)S(1)}, bf16[16,1024]{1,0:T(8,128)(2,1)}, u32[]{:S(2)}) copy-start(bf16[16,1024]{1,0:T(8,128)(2,1)} %coef.1) | copy-start | bytes 98308
  0.7 24.1 %copy-start = (bf16[1,64,1024]{2,1,0:T(8,128)(2,1)S(1)}, bf16[1,64,1024]{2,1,0:T(8,128)(2,1)}, u32[]{:S(2)}) copy-start(bf16[1,64,1024]{2,1,0:T(8,128)(2,1)} %param.9) | copy-start | bytes 393220
  3.2 6.7 %collective-permute-start = (f32[32,384]{1,0:T(8,128)S(1)}, f32[32,384]{1,0:T(8,128)S(1)}, u32[]{:S(2)}, u32[]{:S(2)}) collective-permute-start(f32[32,384]{1,0:T(8,128)S(1)} %get-tuple-element.23), channel_id=1, source_target_pairs={{0,7},{1,6},{2,5},{3,4},{4,3},{5,2},{6,1},{7,0},{8,15},{9,14},{10,... | collective-permute-start | bytes 147464 | tf_op jit(solution)/shard_map/ppermute | solution.py:33
  7.7 4.9 %collective-permute-start.1 = (f32[32,384]{1,0:T(8,128)S(1)}, f32[32,384]{1,0:T(8,128)S(1)}, u32[]{:S(2)}, u32[]{:S(2)}) collective-permute-start(f32[32,384]{1,0:T(8,128)S(1)} %get-tuple-element.24), channel_id=1, source_target_pairs={{0,6},{1,7},{2,4},{3,5},{4,2},{5,3},{6,0},{7,1},{8,14},{9,15},{10,... | collective-permute-start | bytes 147464 | tf_op jit(solution)/shard_map/ppermute | solution.py:33
  7.7 4.9 %collective-permute-start.2 = (f32[32,384]{1,0:T(8,128)S(1)}, f32[32,384]{1,0:T(8,128)S(1)}, u32[]{:S(2)}, u32[]{:S(2)}) collective-permute-start(f32[32,384]{1,0:T(8,128)S(1)} %get-tuple-element.25), channel_id=1, source_target_pairs={{0,5},{1,4},{2,7},{3,6},{4,1},{5,0},{6,3},{7,2},{8,13},{9,12},{10,... | collective-permute-start | bytes 147464 | tf_op jit(solution)/shard_map/ppermute | solution.py:33
  8.6 4.0 %collective-permute-start.3 = (f32[32,384]{1,0:T(8,128)S(1)}, f32[32,384]{1,0:T(8,128)S(1)}, u32[]{:S(2)}, u32[]{:S(2)}) collective-permute-start(f32[32,384]{1,0:T(8,128)S(1)} %get-tuple-element.26), channel_id=1, source_target_pairs={{0,4},{1,5},{2,6},{3,7},{4,0},{5,1},{6,2},{7,3},{8,12},{9,13},{10,... | collective-permute-start | bytes 147464 | tf_op jit(solution)/shard_map/ppermute | solution.py:33
  13.0 3.4 %collective-permute-start.5 = (f32[32,256]{1,0:T(8,128)S(1)}, f32[32,256]{1,0:T(8,128)S(1)}, u32[]{:S(2)}, u32[]{:S(2)}) collective-permute-start(f32[32,256]{1,0:T(8,128)S(1)} %shard_map.122.refs_0_), channel_id=1, source_target_pairs={{0,12},{1,13},{2,14},{3,15},{4,8},{5,9},{6,10},{7,11},{8,4},{9,5},... | collective-permute-start | bytes 98312 | tf_op jit(solution)/shard_map/ppermute | solution.py:33
  14.5 2.2 %collective-permute-start.4 = (f32[32,256]{1,0:T(8,128)S(1)}, f32[32,256]{1,0:T(8,128)S(1)}, u32[]{:S(2)}, u32[]{:S(2)}) collective-permute-start(f32[32,256]{1,0:T(8,128)S(1)} %shard_map.122.refs_0_), channel_id=1, source_target_pairs={{0,4},{4,0},{8,12},{12,8},{1,5},{5,1},{9,13},{13,9},{2,6},{6,2},{1... | collective-permute-start | bytes 98312 | tf_op jit(solution)/shard_map/ppermute | solution.py:23
  16.4 1.2 %collective-permute-start.6 = (f32[32,256]{1,0:T(8,128)S(1)}, f32[32,256]{1,0:T(8,128)S(1)}, u32[]{:S(2)}, u32[]{:S(2)}) collective-permute-start(f32[32,256]{1,0:T(8,128)S(1)} %collective-permute-done.5.refs_3_), channel_id=1, source_target_pairs={{0,4},{4,0},{8,12},{12,8},{1,5},{5,1},{9,13},{13,9},{2,6},{6,2},{1... | collective-permute-start | bytes 98312 | tf_op jit(solution)/shard_map/ppermute | solution.py:23
  18.0 5.6 %collective-permute-start.10 = (bf16[32,256]{1,0:T(8,128)(2,1)S(1)}, bf16[32,256]{1,0:T(8,128)(2,1)S(1)}, u32[]{:S(2)}, u32[]{:S(2)}) collective-permute-start(bf16[32,256]{1,0:T(8,128)(2,1)S(1)} %shard_map.123), channel_id=1, source_target_pairs={{0,7},{1,6},{2,5},{3,4},{4,3},{5,2},{6,1},{7,0},{8,15},{9,14},{10,... | collective-permute-start | bytes 49160 | tf_op jit(solution)/shard_map/ppermute | solution.py:33
  20.6 4.2 %collective-permute-start.9 = (bf16[32,256]{1,0:T(8,128)(2,1)S(1)}, bf16[32,256]{1,0:T(8,128)(2,1)S(1)}, u32[]{:S(2)}, u32[]{:S(2)}) collective-permute-start(bf16[32,256]{1,0:T(8,128)(2,1)S(1)} %shard_map.123), channel_id=1, source_target_pairs={{0,6},{1,7},{2,4},{3,5},{4,2},{5,3},{6,0},{7,1},{8,14},{9,15},{10,... | collective-permute-start | bytes 49160 | tf_op jit(solution)/shard_map/ppermute | solution.py:33
  21.0 3.7 %collective-permute-start.8 = (bf16[32,256]{1,0:T(8,128)(2,1)S(1)}, bf16[32,256]{1,0:T(8,128)(2,1)S(1)}, u32[]{:S(2)}, u32[]{:S(2)}) collective-permute-start(bf16[32,256]{1,0:T(8,128)(2,1)S(1)} %shard_map.123), channel_id=1, source_target_pairs={{0,5},{1,4},{2,7},{3,6},{4,1},{5,0},{6,3},{7,2},{8,13},{9,12},{10,... | collective-permute-start | bytes 49160 | tf_op jit(solution)/shard_map/ppermute | solution.py:33
  22.0 2.7 %collective-permute-start.7 = (bf16[32,256]{1,0:T(8,128)(2,1)S(1)}, bf16[32,256]{1,0:T(8,128)(2,1)S(1)}, u32[]{:S(2)}, u32[]{:S(2)}) collective-permute-start(bf16[32,256]{1,0:T(8,128)(2,1)S(1)} %shard_map.123), channel_id=1, source_target_pairs={{0,4},{1,5},{2,6},{3,7},{4,0},{5,1},{6,2},{7,3},{8,12},{9,13},{10,... | collective-permute-start | bytes 49160 | tf_op jit(solution)/shard_map/ppermute | solution.py:33
  29.3 1.3 %collective-permute-start.11 = (f32[48,512]{1,0:T(8,128)S(1)}, f32[48,512]{1,0:T(8,128)S(1)}, u32[]{:S(2)}, u32[]{:S(2)}) collective-permute-start(f32[48,512]{1,0:T(8,128)S(1)} %get-tuple-element.33), channel_id=1, source_target_pairs={{0,4},{4,0},{8,12},{12,8},{1,5},{5,1},{9,13},{13,9},{2,6},{6,2},{1... | collective-permute-start | bytes 294920 | tf_op jit(solution)/shard_map/ppermute | solution.py:23
  30.6 3.8 %collective-permute-start.12 = (bf16[48,512]{1,0:T(8,128)(2,1)S(1)}, bf16[48,512]{1,0:T(8,128)(2,1)S(1)}, u32[]{:S(2)}, u32[]{:S(2)}) collective-permute-start(bf16[48,512]{1,0:T(8,128)(2,1)S(1)} %add_convert_fusion.1), channel_id=1, source_target_pairs={{0,12},{1,13},{2,14},{3,15},{4,8},{5,9},{6,10},{7,11},{8,4},{9,5},... | collective-permute-start | bytes 147464 | tf_op jit(solution)/shard_map/ppermute | solution.py:33
  34.4 6.2 %collective-permute-start.15 = (bf16[48,512]{1,0:T(8,128)(2,1)S(1)}, bf16[48,512]{1,0:T(8,128)(2,1)S(1)}, u32[]{:S(2)}, u32[]{:S(2)}) collective-permute-start(bf16[48,512]{1,0:T(8,128)(2,1)S(1)} %add_convert_fusion), channel_id=1, source_target_pairs={{0,3},{1,2},{2,1},{3,0},{4,7},{5,6},{6,5},{7,4},{8,11},{9,10},{10,... | collective-permute-start | bytes 147464 | tf_op jit(solution)/shard_map/ppermute | solution.py:33
  36.2 6.3 %collective-permute-start.14 = (bf16[48,512]{1,0:T(8,128)(2,1)S(1)}, bf16[48,512]{1,0:T(8,128)(2,1)S(1)}, u32[]{:S(2)}, u32[]{:S(2)}) collective-permute-start(bf16[48,512]{1,0:T(8,128)(2,1)S(1)} %add_convert_fusion), channel_id=1, source_target_pairs={{0,6},{1,7},{2,4},{3,5},{4,2},{5,3},{6,0},{7,1},{8,14},{9,15},{10,... | collective-permute-start | bytes 147464 | tf_op jit(solution)/shard_map/ppermute | solution.py:33
  36.2 6.3 %collective-permute-start.13 = (bf16[48,512]{1,0:T(8,128)(2,1)S(1)}, bf16[48,512]{1,0:T(8,128)(2,1)S(1)}, u32[]{:S(2)}, u32[]{:S(2)}) collective-permute-start(bf16[48,512]{1,0:T(8,128)(2,1)S(1)} %add_convert_fusion), channel_id=1, source_target_pairs={{0,5},{1,4},{2,7},{3,6},{4,1},{5,0},{6,3},{7,2},{8,13},{9,12},{10,... | collective-permute-start | bytes 147464 | tf_op jit(solution)/shard_map/ppermute | solution.py:33
  42.5 1.4 %collective-permute-start.16 = (f32[48,512]{1,0:T(8,128)S(1)}, f32[48,512]{1,0:T(8,128)S(1)}, u32[]{:S(2)}, u32[]{:S(2)}) collective-permute-start(f32[48,512]{1,0:T(8,128)S(1)} %add_add_fusion.scaled), channel_id=1, source_target_pairs={{0,4},{4,0},{8,12},{12,8},{1,5},{5,1},{9,13},{13,9},{2,6},{6,2},{1... | collective-permute-start | bytes 294920 | tf_op jit(solution)/shard_map/ppermute | solution.py:23

commit v5 on v4

--- a/solution.py
+++ b/solution.py
@@ -9,13 +9,14 @@
 from jax.sharding import PartitionSpec as P
 
 K = 4
+LANES = 128
 FAIR_ALPHA = 0.95
 SOFTNESS = 0.1
 F32 = jnp.float32
 BF16 = jnp.bfloat16
 VMEM = pl.BlockSpec(memory_space=pltpu.VMEM)
 HBM = pl.BlockSpec(memory_space=pltpu.HBM)
-PARAMS = pltpu.CompilerParams(vmem_limit_bytes=48 * 1024 * 1024)
+PARAMS = pltpu.CompilerParams(vmem_limit_bytes=24 * 1024 * 1024)
 
 
 def swap(shard, axis, mask):
@@ -88,10 +89,64 @@
     return jnp.where(rows == ids, 1.0, 0.0).astype(BF16)
 
 
+def pick(table, ids):
+    rows, size = table.shape
+    slots = ids.shape[1]
+    if slots % LANES or size % LANES:
+        return [whole(dot(parts(table), hot(ids, size), 1, 0))]
+    pieces = []
+    for first in range(0, slots, LANES):
+        chosen = jnp.broadcast_to(ids[:, first : first + LANES], (rows, LANES))
+        lane = lax.rem(chosen, LANES)
+        block = lax.div(chosen, LANES)
+        found = jnp.zeros((rows, LANES), F32)
+        for start in range(0, size, LANES):
+            there = jnp.take_along_axis(table[:, start : start + LANES], lane, axis=1, mode="promise_in_bounds")
+            found = jnp.where(block == start // LANES, there, found)
+        pieces.append(found)
+    return pieces
+
+
+def packed_shape(variables, slots):
+    pieces = slots // LANES if slots % LANES == 0 else 1
+    return up(pieces * (variables + 1), 8), slots // pieces
+
+
+def pack(payload, pieces, cells, variables):
+    lanes = payload.shape[1]
+    full = variables // 8 * 8
+    base = len(pieces) * full
+    payload[base:, :] = jnp.zeros((payload.shape[0] - base, lanes), F32)
+    for n, piece in enumerate(pieces):
+        payload[n * full : (n + 1) * full, :] = piece[0:full]
+        row = base + n * (variables + 1 - full)
+        payload[row : row + variables - full, :] = piece[full:variables]
+        payload[row + variables - full : row + variables - full + 1, :] = cells[:, n * lanes : (n + 1) * lanes]
+
+
+def unpack(payload, variables, slots):
+    lanes = payload.shape[1]
+    full = variables // 8 * 8
+    base = slots // lanes * full
+    values, cells = [], []
+    for n in range(slots // lanes):
+        row = base + n * (variables + 1 - full)
+        piece = payload[n * full : (n + 1) * full, :]
+        for extra in range(variables - full):
+            here = lax.broadcasted_iota(jnp.int32, (8, lanes), 0) == extra
+            one = jnp.where(here, payload[row + extra : row + extra + 1, :], 0.0)
+            tail = one if extra == 0 else tail + one
+        values.append(jnp.concatenate([piece, tail], axis=0) if variables > full else piece)
+        cells.append(payload[row + variables - full : row + variables - full + 1, :])
+    if len(values) == 1:
+        return values[0], cells[0]
+    return jnp.concatenate(values, axis=1), jnp.concatenate(cells, axis=1)
+
+
 def project_kernel(*refs):
     (latent_in, coef_in, proj_in, source_in, weight_in, target_in, wanted_in, area_in, factor_in, *rest) = refs
-    *payloads, products, pair_ids, target, wanted, area, factor = rest[:-7]
-    latent, coef, proj, source, weight, proj_pad, arrivals = rest[-7:]
+    *payloads, proj_pad, products, pair_ids, target, wanted, area, factor = rest[:-6]
+    latent, coef, proj, source, weight, arrivals = rest[-6:]
     moves = [
         pltpu.make_async_copy(there, here, arrivals.at[n])
         for n, (there, here) in enumerate(
@@ -116,7 +171,7 @@
     table = coef.shape[0]
     variables = proj.shape[0]
     proj_pad[...] = jnp.zeros_like(proj_pad)
-    for move in moves:
+    for move in moves[:3]:
         move.wait()
     proj_pad[0:variables, :] = proj[...]
     wide = latent[...].astype(F32)
@@ -124,15 +179,13 @@
     for q in range(table):
         products[q * rows : (q + 1) * rows, :] = (wide * scale[q : q + 1, :]).astype(BF16)
     projected = dot(proj_pad[...], products[...], 1, 1)
-    split = parts(projected)
+    for move in moves[3:]:
+        move.wait()
     for i in range(bands):
         there = lax.bitwise_xor(here, i)
         ids = weight[here, pl.ds(there, 1), :] * rows + source[here, pl.ds(there, 1), :]
         pair_ids[i] = ids
-        at_slots = whole(dot(split, hot(ids, table * rows), 1, 0))
-        cells = target[there, :, :].astype(F32)
-        row = lax.broadcasted_iota(jnp.int32, at_slots.shape, 0)
-        payloads[i][...] = jnp.where(row == variables, cells, at_slots)
+        pack(payloads[i], pick(projected, ids), target[there, :, :].astype(F32), variables)
 
 
 def predict_kernel(variables, *refs):
@@ -143,10 +196,8 @@
     total = 0.0
     for i in range(bands):
         there = lax.bitwise_xor(here, i)
-        arrived = payloads[i][...]
-        row = lax.broadcasted_iota(jnp.int32, arrived.shape, 0)
-        split = parts(jnp.where(row < variables, arrived, 0.0))
-        total = total + dot(split, hot(target[there, :, :], predicted.shape[1]), 1, 1)
+        arrived, _ = unpack(payloads[i], variables, target.shape[2])
+        total = total + dot(parts(arrived), hot(target[there, :, :], predicted.shape[1]), 1, 1)
     predicted[...] = whole(total)
 
 
@@ -154,7 +205,7 @@
     *payloads, counts = refs
     payloads = payloads[::-1]
     for i, payload in enumerate(payloads):
-        cells = payload[variables : variables + 1, :].astype(jnp.int32)
+        cells = unpack(payload, variables, pair_ids.shape[2])[1].astype(jnp.int32)
         block = dot(hot(pair_ids[i], counts.shape[0]), hot(cells, cells_dev), 1, 1)
         counts[:, i * cells_dev : (i + 1) * cells_dev] = block.astype(BF16)
 
@@ -198,35 +249,57 @@
     grad[...] = rows[...].astype(BF16)
 
 
-def backward_kernel(members, scale_proj, scale_coef, scale_loss, latent, coef, proj, counts, products, *refs):
-    *grads, latent_grad, keep, send, mean_loss, proj_pad, cell_grad, sums = refs
+def back_to_pairs(grad, proj, counts):
+    return dot(grad, proj, 0, 0).astype(BF16), dot(grad, counts, 1, 1)
+
+
+def only_grads(arrived, variables):
+    row = lax.broadcasted_iota(jnp.int32, arrived.shape, 0)
+    return jnp.where(row < variables, arrived.astype(F32), 0.0).astype(BF16)
+
+
+def early_kernel(index, variables, proj, counts, grad, *refs):
+    *before, pair_grad, block, cell_grad = refs
+    cells_dev = grad.shape[1]
+    own = counts[:, index * cells_dev : (index + 1) * cells_dev]
+    cell_grad[...], pairs_here = back_to_pairs(only_grads(grad[...], variables), proj[...], own)
+    pair_grad[...] = before[0][...] + pairs_here if before else pairs_here
+    step = 256
+    for h in range(0, block.shape[1], step):
+        here = dot(own, cell_grad[:, h : h + step], 1, 0)
+        block[:, h : h + step] = before[1][:, h : h + step] + here if before else here
+
+
+def backward_kernel(members, variables, early, scale_proj, scale_coef, scale_loss, latent, coef, proj, counts, products, *refs):
+    near_pair_grad, near_block, *grads = refs[:-6]
+    latent_grad, keep, send, mean_loss, cell_grad, sums = refs[-6:]
     bands = len(grads)
     band = lax.axis_index("band")
     side = half_here(members, bands)
-    variables = proj.shape[0]
     rows, hidden = latent.shape
     table = coef.shape[0]
     cells_dev = grads[0].shape[1]
     padded = grads[0].shape[0]
-    proj_pad[...] = jnp.zeros_like(proj_pad)
-    proj_pad[0:variables, :] = proj[...]
     lane = lax.broadcasted_iota(jnp.int32, (1, 128), 1)
     losses = jnp.zeros((1, 128), F32)
-    pair_grad = jnp.zeros((padded, table * rows), F32)
+    pair_grad = near_pair_grad[...]
     for i in range(bands):
-        arrived = grads[i][...].astype(F32)
         there = lax.bitwise_xor(band, i)
-        loss = jnp.sum(arrived[variables : variables + 1, 0:128], axis=1, keepdims=True)
+        loss = jnp.sum(grads[i][variables : variables + 1, 0:128].astype(F32), axis=1, keepdims=True)
         losses = losses + jnp.where(lane == there, loss, 0.0)
-        row = lax.broadcasted_iota(jnp.int32, arrived.shape, 0)
-        grad = jnp.where(row < variables, arrived, 0.0).astype(BF16)
-        pair_grad = pair_grad + dot(grad, counts[:, i * cells_dev : (i + 1) * cells_dev], 1, 1)
-        cell_grad[i * cells_dev : (i + 1) * cells_dev, :] = dot(grad, proj_pad[...], 0, 0).astype(BF16)
+        if i not in early:
+            spot = slice((i - 1) * cells_dev, i * cells_dev)
+            cell_grad[spot, :], here = back_to_pairs(
+                only_grads(grads[i][...], variables),
+                proj[...],
+                counts[:, i * cells_dev : (i + 1) * cells_dev],
+            )
+            pair_grad = pair_grad + here
     mean_loss[...] = jnp.sum(losses, axis=1, keepdims=True) * scale_loss
     sums[0:padded, :] = whole(dot(parts(pair_grad), products[...], 1, 0)) * scale_proj
     step = 256
     for h in range(0, hidden, step):
-        block = dot(counts[...], cell_grad[:, h : h + step], 1, 0)
+        block = near_block[:, h : h + step] + dot(counts[:, cells_dev : cells_dev + cell_grad.shape[0]], cell_grad[:, h : h + step], 1, 0)
         wide = latent[:, h : h + step].astype(F32)
         scale = coef[:, h : h + step].astype(F32)
         into_latent = 0.0
@@ -309,10 +382,11 @@
     padded = up(variables + 1, 16)
     pair_coef = FAIR_ALPHA / (members - 1) + (1.0 - FAIR_ALPHA) / members
 
-    *payloads, products, pair_ids, cell_ids, wanted, area, factor = call(
+    *payloads, proj_pad, products, pair_ids, cell_ids, wanted, area, factor = call(
         project_kernel,
-        [shape(padded, slots)] * bands
+        [shape(*packed_shape(variables, slots))] * bands
         + [
+            shape(padded, hidden, dtype=BF16),
             shape(pairs, hidden, dtype=BF16),
             shape(bands, 1, slots, dtype=jnp.int32),
             shape(bands, 1, slots, dtype=jnp.int32),
@@ -337,7 +411,6 @@
             pltpu.VMEM((variables, hidden), BF16),
             pltpu.VMEM(edge_source.shape, jnp.int32),
             pltpu.VMEM(edge_weight.shape, jnp.int32),
-            pltpu.VMEM((padded, hidden), BF16),
             pltpu.SemaphoreType.DMA((9,)),
         ],
         source=HBM,
@@ -345,7 +418,7 @@
     arrived = [cross(payloads[i], 1, i) for i in range(bands)][::-1]
     (predicted,) = call(
         functools.partial(predict_kernel, variables),
-        [shape(padded, cells_dev)],
+        [shape(up(variables, 8), cells_dev)],
         (*arrived, cell_ids),
     )
     (counts,) = call(
@@ -357,6 +430,8 @@
     members_here = [predicted, swap(predicted, "member", 1)]
     for i in range(2, members, 2):
         far = cross(predicted, i + 1, 0)
+        if i == 2:
+            far, counts = lax.optimization_barrier((far, counts))
         members_here += [swap(far, "member", 1), far]
     (grad,) = call(
         functools.partial(grade_kernel, pair_coef),
@@ -365,10 +440,22 @@
         [pltpu.VMEM((padded, cells_dev), F32)],
     )
     grads = [cross(grad, 1, i) for i in range(bands)]
+    early = sorted({0, bands - 1})
+    sums = ()
+    for index in early:
+        sums = call(
+            functools.partial(early_kernel, index, variables),
+            [shape(padded, pairs), shape(pairs, hidden)],
+            (proj_pad, counts, grads[index], *sums),
+            [pltpu.VMEM((cells_dev, hidden), BF16)],
+            flops=2 * pairs * cells_dev * hidden,
+        )
     latent_grad, keep, send, mean_loss = call(
         functools.partial(
             backward_kernel,
             members,
+            variables,
+            early,
             1.0 / math.sqrt(members * cells_all),
             1.0 / math.sqrt(members * cells_all * K),
             1.0 / (members * variables * cells_all),
@@ -379,10 +466,9 @@
             shape(padded + table, hidden // 2),
             shape(1, 1),
         ],
-        (latent_rows, coef_table, out_proj, counts, products, *grads),
+        (latent_rows, coef_table, proj_pad, counts, products, *sums, *grads),
         [
-            pltpu.VMEM((padded, hidden), BF16),
-            pltpu.VMEM((cells_all, hidden), BF16),
+            pltpu.VMEM((cells_all - len(early) * cells_dev, hidden), BF16),
             pltpu.VMEM((padded + table, hidden), F32),
         ],
     )

time: 45.4 us -> 43.6 us (0.960)
  waiting for transfers between devices: 16.5 us -> 14 us
    ppermute x13, waiting for transfers between devices: 13.4 us -> 10.9 us  [cross(): return lax.ppermute(shard, ('member', 'band'), pairs)]
    pallas_call x6 -> x8, Pallas kernels: 10.4 us -> 10.8 us  [call(): pl.pallas_call(kernel, out_shape=outs, in_specs=[source] * len(operands),...]
  transfers between devices with their start and end apart: 17 -> 17, of which waited for: 10 -> 10; matrix products, arithmetic and copies ran while one was open for 0% -> 0% of each run, Pallas kernels for 3% -> 8%
where the time goes in v5:
time: 43.6 us; the launch traced here: 43.5 us
  starting transfers between devices  17.9 us (41%)
  waiting for transfers between devices  14 us (32%)
  Pallas kernels  10.8 us (25%)
  between operations  0.7 us (2%)
    ppermute x13, starting transfers between devices, cross(): return lax.ppermute(shard, ('member', 'band'), pairs)  16.9 us
    ppermute x13, waiting for transfers between devices, cross(): return lax.ppermute(shard, ('member', 'band'), pairs)  10.9 us
    pallas_call x8, Pallas kernels, call(): pl.pallas_call(kernel, out_shape=outs, in_specs=[source] * len(operands),...  10.8 us
    ppermute x4, waiting for transfers between devices, swap(): return lax.ppermute(shard, axis, [(i, i ^ mask) for i in range(peers)])  3.05 us
    ppermute x4, starting transfers between devices, swap(): return lax.ppermute(shard, axis, [(i, i ^ mask) for i in range(peers)])  1.04 us
  transfers between devices with their start and end apart: 17, of which 10 were waited for; matrix products, arithmetic and copies ran while one was open for 0% of the time, Pallas kernels for 8%

profile of v5, /device:TPU:0, one launch (start us, length us, event | category | flops | bytes accessed | tf_op | source)
XLA Modules:
  0.0 43.5 jit_solution(10442206207035750463)
XLA Ops:
  0.6 2.3 %shard_map.120 = (f32[80,128]{1,0:T(8,128)S(1)}, f32[80,128]{1,0:T(8,128)S(1)}, f32[80,128]{1,0:T(8,128)S(1)}, f32[80,128]{1,0:T(8,128)S(1)}, bf16[32,1024]{1,0:...) custom-call(bf16[64,1024]{1,0:T(8,128)(2,1)} %bitcast.5, ...), custom_call_target="tpu_custom_call" | custom-call | bytes 1048576 | tf_op jit(solution)/shard_map/pallas_call | solution.py:347
  3.0 4.6 %collective-permute-start = (f32[80,128]{1,0:T(8,128)S(1)}, f32[80,128]{1,0:T(8,128)S(1)}, u32[]{:S(2)}, u32[]{:S(2)}) collective-permute-start(f32[80,128]{1,0:T(8,128)S(1)} %get-tuple-element.30), channel_id=1, source_target_pairs={{0,7},{1,6},{2,5},{3,4},{4,3},{5,2},{6,1},{7,0},{8,15},{9,14},{10,... | collective-permute-start | bytes 122888 | tf_op jit(solution)/shard_map/ppermute | solution.py:34
  7.5 0.0 collective-permute-start.1
  7.5 0.9 %collective-permute-start.2 = (f32[80,128]{1,0:T(8,128)S(1)}, f32[80,128]{1,0:T(8,128)S(1)}, u32[]{:S(2)}, u32[]{:S(2)}) collective-permute-start(f32[80,128]{1,0:T(8,128)S(1)} %get-tuple-element.32), channel_id=1, source_target_pairs={{0,5},{1,4},{2,7},{3,6},{4,1},{5,0},{6,3},{7,2},{8,13},{9,12},{10,... | collective-permute-start | bytes 122888 | tf_op jit(solution)/shard_map/ppermute | solution.py:34
  8.5 0.0 collective-permute-start.3
  8.5 1.0 %collective-permute-done.refs_0_ = f32[80,128]{1,0:T(8,128)S(1)} collective-permute-done((f32[80,128]{1,0:T(8,128)S(1)}, f32[80,128]{1,0:T(8,128)S(1)}, u32[]{:S(2)}, u32[]{:S(2)}) %collective-permute-start) | collective-permute-done | bytes 40992 | tf_op jit(solution)/shard_map/ppermute | solution.py:34
  9.5 2.8 %collective-permute-done.1.refs_1_ = f32[80,128]{1,0:T(8,128)S(1)} collective-permute-done((f32[80,128]{1,0:T(8,128)S(1)}, f32[80,128]{1,0:T(8,128)S(1)}, u32[]{:S(2)}, u32[]{:S(2)}) %collective-permute-start.1) | collective-permute-done | bytes 40992 | tf_op jit(solution)/shard_map/ppermute | solution.py:34
  12.2 0.0 collective-permute-done.2.refs_2_
  12.2 0.0 collective-permute-done.3.refs_3_
  12.2 0.4 shard_map.121.refs_0_
  12.6 1.4 %collective-permute-start.4 = (f32[32,256]{1,0:T(8,128)S(1)}, f32[32,256]{1,0:T(8,128)S(1)}, u32[]{:S(2)}, u32[]{:S(2)}) collective-permute-start(f32[32,256]{1,0:T(8,128)S(1)} %shard_map.121.refs_0_), channel_id=1, source_target_pairs={{0,12},{1,13},{2,14},{3,15},{4,8},{5,9},{6,10},{7,11},{8,4},{9,5},... | collective-permute-start | bytes 98312 | tf_op jit(solution)/shard_map/ppermute | solution.py:34
  14.0 0.2 collective-permute-start.5
  14.3 1.3 %shard_map.122.counts = bf16[1024,1024]{1,0:T(8,128)(2,1)S(1)} custom-call(s32[4,1,384]{2,1,0:T(1,128)S(1)} %get-tuple-element.35.pair_ids, f32[80,128]{1,0:T(8,128)S(1)} %collective-permute-done.refs_0_, f32[80,128]{1,0:T(8,128)S(1)} %collective-permute-done.1.refs_1_, f32[80,128]{1,0:T(8,128)S(1)} %collective-permute-done.2.refs_2_, ...), custom_call_target="tpu_custom_call" | custom-call | flops 805306368 | bytes 1048576 | tf_op jit(solution)/shard_map/pallas_call | solution.py:347
  15.6 0.4 collective-permute-done.4.refs_3_
  16.0 0.3 collective-permute-start.6
  16.3 0.0 collective-permute-done.5.refs_1_
  16.3 0.9 %collective-permute-done.6.refs_2_ = f32[32,256]{1,0:T(8,128)S(1)} collective-permute-done((f32[32,256]{1,0:T(8,128)S(1)}, f32[32,256]{1,0:T(8,128)S(1)}, u32[]{:S(2)}, u32[]{:S(2)}) %collective-permute-start.6) | collective-permute-done | bytes 32800 | tf_op jit(solution)/shard_map/ppermute | solution.py:24
  17.2 0.3 shard_map.123
  17.5 0.4 collective-permute-start.8
  17.9 2.2 %collective-permute-start.7 = (bf16[32,256]{1,0:T(8,128)(2,1)S(1)}, bf16[32,256]{1,0:T(8,128)(2,1)S(1)}, u32[]{:S(2)}, u32[]{:S(2)}) collective-permute-start(bf16[32,256]{1,0:T(8,128)(2,1)S(1)} %shard_map.123), channel_id=1, source_target_pairs={{0,7},{1,6},{2,5},{3,4},{4,3},{5,2},{6,1},{7,0},{8,15},{9,14},{10,... | collective-permute-start | bytes 49160 | tf_op jit(solution)/shard_map/ppermute | solution.py:34
  20.1 0.3 collective-permute-start.9
  20.4 1.4 %collective-permute-start.10 = (bf16[32,256]{1,0:T(8,128)(2,1)S(1)}, bf16[32,256]{1,0:T(8,128)(2,1)S(1)}, u32[]{:S(2)}, u32[]{:S(2)}) collective-permute-start(bf16[32,256]{1,0:T(8,128)(2,1)S(1)} %shard_map.123), channel_id=1, source_target_pairs={{0,6},{1,7},{2,4},{3,5},{4,2},{5,3},{6,0},{7,1},{8,14},{9,15},{10,... | collective-permute-start | bytes 49160 | tf_op jit(solution)/shard_map/ppermute | solution.py:34
  21.8 0.0 collective-permute-done.8.grad.refs_2_
  21.8 0.0 copy-start
  21.8 0.0 copy-start.1
  21.8 1.0 %shard_map.124 = (f32[32,1024]{1,0:T(8,128)S(1)}, f32[1024,1024]{1,0:T(8,128)S(1)}) custom-call(bf16[32,1024]{1,0:T(8,128)(2,1)S(1)} %get-tuple-element.29.proj, bf16[1024,1024]{1,0:T(8,128)(2,1)S(1)} %shard_map.122.counts, bf16[32,256]{1,0:T(8,128)(2,1)S(1)} %collective-permute-done.8.grad.refs_2_), custom_call_target="tpu_custom_call" | custom-call | flops 536870912 | bytes 1048576 | tf_op jit(solution)/shard_map/pallas_call | solution.py:347
  22.8 0.0 collective-permute-done.7.grad.refs_5_
  22.9 1.0 %shard_map.125 = (f32[32,1024]{1,0:T(8,128)S(1)}, f32[1024,1024]{1,0:T(8,128)S(1)}) custom-call(bf16[32,1024]{1,0:T(8,128)(2,1)S(1)} %get-tuple-element.29.proj, bf16[1024,1024]{1,0:T(8,128)(2,1)S(1)} %shard_map.122.counts, bf16[32,256]{1,0:T(8,128)(2,1)S(1)} %collective-permute-done.7.grad.refs_5_, f32[32,1024]{1,0:T(8,128)S(1)} %get-tuple-element.42.refs_0_, ...), custom_call_target="tpu_custom_call" | custom-call | flops 536870912 | bytes 1048576 | tf_op jit(solution)/shard_map/pallas_call | solution.py:347
  23.9 0.0 collective-permute-done.9.refs_3_
  23.9 0.6 %collective-permute-done.10.refs_4_ = bf16[32,256]{1,0:T(8,128)(2,1)S(1)} collective-permute-done((bf16[32,256]{1,0:T(8,128)(2,1)S(1)}, bf16[32,256]{1,0:T(8,128)(2,1)S(1)}, u32[]{:S(2)}, u32[]{:S(2)}) %collective-permute-start.10) | collective-permute-done | bytes 16416 | tf_op jit(solution)/shard_map/ppermute | solution.py:34
  24.5 0.0 copy-done
  24.5 0.0 copy-done.1
  24.5 3.1 %shard_map.126 = (bf16[64,1024]{1,0:T(8,128)(2,1)S(1)}, f32[48,512]{1,0:T(8,128)S(1)}, f32[48,512]{1,0:T(8,128)S(1)}, f32[1,1]{1,0:T(1,128)}) custom-call(bf16[64,1024]{1,0:T(8,128)(2,1)S(1)} %bitcast.6, bf16[16,1024]{1,0:T(8,128)(2,1)S(1)} %copy-done.1, bf16[32,1024]{1,0:T(8,128)(2,1)S(1)} %get-tuple-element.29.proj, ...), custom_call_target="tpu_custom_call" | custom-call | bytes 1048576 | tf_op jit(solution)/shard_map/pallas_call | solution.py:347
  27.6 0.3 collective-permute-start.11
  28.0 1.0 %collective-permute-done.11 = f32[48,512]{1,0:T(8,128)S(1)} collective-permute-done((f32[48,512]{1,0:T(8,128)S(1)}, f32[48,512]{1,0:T(8,128)S(1)}, u32[]{:S(2)}, u32[]{:S(2)}) %collective-permute-start.11) | collective-permute-done | bytes 98336 | tf_op jit(solution)/shard_map/ppermute | solution.py:24
  28.9 1.5 %collective-permute-start.12 = (bf16[48,512]{1,0:T(8,128)(2,1)S(1)}, bf16[48,512]{1,0:T(8,128)(2,1)S(1)}, u32[]{:S(2)}, u32[]{:S(2)}) collective-permute-start(bf16[48,512]{1,0:T(8,128)(2,1)S(1)} %add_convert_fusion.1), channel_id=1, source_target_pairs={{0,12},{1,13},{2,14},{3,15},{4,8},{5,9},{6,10},{7,11},{8,4},{9,5},... | collective-permute-start | bytes 147464 | tf_op jit(solution)/shard_map/ppermute | solution.py:34
  30.4 2.1 %collective-permute-done.12 = bf16[48,512]{1,0:T(8,128)(2,1)S(1)} collective-permute-done((bf16[48,512]{1,0:T(8,128)(2,1)S(1)}, bf16[48,512]{1,0:T(8,128)(2,1)S(1)}, u32[]{:S(2)}, u32[]{:S(2)}) %collective-permute-start.12) | collective-permute-done | bytes 49184 | tf_op jit(solution)/shard_map/ppermute | solution.py:34
  32.5 1.9 %collective-permute-start.15 = (bf16[48,512]{1,0:T(8,128)(2,1)S(1)}, bf16[48,512]{1,0:T(8,128)(2,1)S(1)}, u32[]{:S(2)}, u32[]{:S(2)}) collective-permute-start(bf16[48,512]{1,0:T(8,128)(2,1)S(1)} %add_convert_fusion), channel_id=1, source_target_pairs={{0,3},{1,2},{2,1},{3,0},{4,7},{5,6},{6,5},{7,4},{8,11},{9,10},{10,... | collective-permute-start | bytes 147464 | tf_op jit(solution)/shard_map/ppermute | solution.py:34
  34.4 0.8 %collective-permute-start.14 = (bf16[48,512]{1,0:T(8,128)(2,1)S(1)}, bf16[48,512]{1,0:T(8,128)(2,1)S(1)}, u32[]{:S(2)}, u32[]{:S(2)}) collective-permute-start(bf16[48,512]{1,0:T(8,128)(2,1)S(1)} %add_convert_fusion), channel_id=1, source_target_pairs={{0,6},{1,7},{2,4},{3,5},{4,2},{5,3},{6,0},{7,1},{8,14},{9,15},{10,... | collective-permute-start | bytes 147464 | tf_op jit(solution)/shard_map/ppermute | solution.py:34
  35.2 1.5 %collective-permute-start.13 = (bf16[48,512]{1,0:T(8,128)(2,1)S(1)}, bf16[48,512]{1,0:T(8,128)(2,1)S(1)}, u32[]{:S(2)}, u32[]{:S(2)}) collective-permute-start(bf16[48,512]{1,0:T(8,128)(2,1)S(1)} %add_convert_fusion), channel_id=1, source_target_pairs={{0,5},{1,4},{2,7},{3,6},{4,1},{5,0},{6,3},{7,2},{8,13},{9,12},{10,... | collective-permute-start | bytes 147464 | tf_op jit(solution)/shard_map/ppermute | solution.py:34
  36.7 2.0 %collective-permute-done.15 = bf16[48,512]{1,0:T(8,128)(2,1)S(1)} collective-permute-done((bf16[48,512]{1,0:T(8,128)(2,1)S(1)}, bf16[48,512]{1,0:T(8,128)(2,1)S(1)}, u32[]{:S(2)}, u32[]{:S(2)}) %collective-permute-start.15) | collective-permute-done | bytes 49184 | tf_op jit(solution)/shard_map/ppermute | solution.py:34
  38.8 1.9 %collective-permute-done.14 = bf16[48,512]{1,0:T(8,128)(2,1)S(1)} collective-permute-done((bf16[48,512]{1,0:T(8,128)(2,1)S(1)}, bf16[48,512]{1,0:T(8,128)(2,1)S(1)}, u32[]{:S(2)}, u32[]{:S(2)}) %collective-permute-start.14) | collective-permute-done | bytes 49184 | tf_op jit(solution)/shard_map/ppermute | solution.py:34
  40.7 0.0 collective-permute-done.13
  40.7 0.2 collective-permute-start.16
  40.9 1.2 %collective-permute-done.16.other = f32[48,512]{1,0:T(8,128)S(1)} collective-permute-done((f32[48,512]{1,0:T(8,128)S(1)}, f32[48,512]{1,0:T(8,128)S(1)}, u32[]{:S(2)}, u32[]{:S(2)}) %collective-permute-start.16) | collective-permute-done | bytes 98336 | tf_op jit(solution)/shard_map/ppermute | solution.py:24
  42.1 1.4 %shard_map.127 = (bf16[64,1024]{1,0:T(8,128)(2,1)}, f32[25,1024]{1,0:T(8,128)}, f32[16,1024]{1,0:T(8,128)}, f32[1,1]{1,0:T(1,128)}) custom-call(f32[48,512]{1,0:T(8,128)S(1)} %add_add_fusion.scaled, f32[48,512]{1,0:T(8,128)S(1)} %collective-permute-done.16.other, bf16[64,1024]{1,0:T(8,128)(2,1)S(1)} %get-tuple-element.48.latent_grad, ...), custom_call_target="tpu_custom_call" | custom-call | bytes 1048576 | tf_op jit(solution)/shard_map/pallas_call | solution.py:347
  (3 shorter events, 0.1 us)
Async XLA Ops:
  3.0 6.5 %collective-permute-start = (f32[80,128]{1,0:T(8,128)S(1)}, f32[80,128]{1,0:T(8,128)S(1)}, u32[]{:S(2)}, u32[]{:S(2)}) collective-permute-start(f32[80,128]{1,0:T(8,128)S(1)} %get-tuple-element.30), channel_id=1, source_target_pairs={{0,7},{1,6},{2,5},{3,4},{4,3},{5,2},{6,1},{7,0},{8,15},{9,14},{10,... | collective-permute-start | bytes 122888 | tf_op jit(solution)/shard_map/ppermute | solution.py:34
  7.5 4.7 %collective-permute-start.1 = (f32[80,128]{1,0:T(8,128)S(1)}, f32[80,128]{1,0:T(8,128)S(1)}, u32[]{:S(2)}, u32[]{:S(2)}) collective-permute-start(f32[80,128]{1,0:T(8,128)S(1)} %get-tuple-element.31), channel_id=1, source_target_pairs={{0,6},{1,7},{2,4},{3,5},{4,2},{5,3},{6,0},{7,1},{8,14},{9,15},{10,... | collective-permute-start | bytes 122888 | tf_op jit(solution)/shard_map/ppermute | solution.py:34
  7.5 4.7 %collective-permute-start.2 = (f32[80,128]{1,0:T(8,128)S(1)}, f32[80,128]{1,0:T(8,128)S(1)}, u32[]{:S(2)}, u32[]{:S(2)}) collective-permute-start(f32[80,128]{1,0:T(8,128)S(1)} %get-tuple-element.32), channel_id=1, source_target_pairs={{0,5},{1,4},{2,7},{3,6},{4,1},{5,0},{6,3},{7,2},{8,13},{9,12},{10,... | collective-permute-start | bytes 122888 | tf_op jit(solution)/shard_map/ppermute | solution.py:34
  8.5 3.8 %collective-permute-start.3 = (f32[80,128]{1,0:T(8,128)S(1)}, f32[80,128]{1,0:T(8,128)S(1)}, u32[]{:S(2)}, u32[]{:S(2)}) collective-permute-start(f32[80,128]{1,0:T(8,128)S(1)} %get-tuple-element.33), channel_id=1, source_target_pairs={{0,4},{1,5},{2,6},{3,7},{4,0},{5,1},{6,2},{7,3},{8,12},{9,13},{10,... | collective-permute-start | bytes 122888 | tf_op jit(solution)/shard_map/ppermute | solution.py:34
  12.6 3.4 %collective-permute-start.4 = (f32[32,256]{1,0:T(8,128)S(1)}, f32[32,256]{1,0:T(8,128)S(1)}, u32[]{:S(2)}, u32[]{:S(2)}) collective-permute-start(f32[32,256]{1,0:T(8,128)S(1)} %shard_map.121.refs_0_), channel_id=1, source_target_pairs={{0,12},{1,13},{2,14},{3,15},{4,8},{5,9},{6,10},{7,11},{8,4},{9,5},... | collective-permute-start | bytes 98312 | tf_op jit(solution)/shard_map/ppermute | solution.py:34
  14.0 2.2 %collective-permute-start.5 = (f32[32,256]{1,0:T(8,128)S(1)}, f32[32,256]{1,0:T(8,128)S(1)}, u32[]{:S(2)}, u32[]{:S(2)}) collective-permute-start(f32[32,256]{1,0:T(8,128)S(1)} %shard_map.121.refs_0_), channel_id=1, source_target_pairs={{0,4},{4,0},{8,12},{12,8},{1,5},{5,1},{9,13},{13,9},{2,6},{6,2},{1... | collective-permute-start | bytes 98312 | tf_op jit(solution)/shard_map/ppermute | solution.py:24
  16.0 1.2 %collective-permute-start.6 = (f32[32,256]{1,0:T(8,128)S(1)}, f32[32,256]{1,0:T(8,128)S(1)}, u32[]{:S(2)}, u32[]{:S(2)}) collective-permute-start(f32[32,256]{1,0:T(8,128)S(1)} %collective-permute-done.4.refs_3_), channel_id=1, source_target_pairs={{0,4},{4,0},{8,12},{12,8},{1,5},{5,1},{9,13},{13,9},{2,6},{6,2},{1... | collective-permute-start | bytes 98312 | tf_op jit(solution)/shard_map/ppermute | solution.py:24
  17.5 4.3 %collective-permute-start.8 = (bf16[32,256]{1,0:T(8,128)(2,1)S(1)}, bf16[32,256]{1,0:T(8,128)(2,1)S(1)}, u32[]{:S(2)}, u32[]{:S(2)}) collective-permute-start(bf16[32,256]{1,0:T(8,128)(2,1)S(1)} %shard_map.123), channel_id=1, source_target_pairs={{0,4},{1,5},{2,6},{3,7},{4,0},{5,1},{6,2},{7,3},{8,12},{9,13},{10,... | collective-permute-start | bytes 49160 | tf_op jit(solution)/shard_map/ppermute | solution.py:34
  17.9 5.0 %collective-permute-start.7 = (bf16[32,256]{1,0:T(8,128)(2,1)S(1)}, bf16[32,256]{1,0:T(8,128)(2,1)S(1)}, u32[]{:S(2)}, u32[]{:S(2)}) collective-permute-start(bf16[32,256]{1,0:T(8,128)(2,1)S(1)} %shard_map.123), channel_id=1, source_target_pairs={{0,7},{1,6},{2,5},{3,4},{4,3},{5,2},{6,1},{7,0},{8,15},{9,14},{10,... | collective-permute-start | bytes 49160 | tf_op jit(solution)/shard_map/ppermute | solution.py:34
  20.1 3.7 %collective-permute-start.9 = (bf16[32,256]{1,0:T(8,128)(2,1)S(1)}, bf16[32,256]{1,0:T(8,128)(2,1)S(1)}, u32[]{:S(2)}, u32[]{:S(2)}) collective-permute-start(bf16[32,256]{1,0:T(8,128)(2,1)S(1)} %shard_map.123), channel_id=1, source_target_pairs={{0,5},{1,4},{2,7},{3,6},{4,1},{5,0},{6,3},{7,2},{8,13},{9,12},{10,... | collective-permute-start | bytes 49160 | tf_op jit(solution)/shard_map/ppermute | solution.py:34
  20.4 4.1 %collective-permute-start.10 = (bf16[32,256]{1,0:T(8,128)(2,1)S(1)}, bf16[32,256]{1,0:T(8,128)(2,1)S(1)}, u32[]{:S(2)}, u32[]{:S(2)}) collective-permute-start(bf16[32,256]{1,0:T(8,128)(2,1)S(1)} %shard_map.123), channel_id=1, source_target_pairs={{0,6},{1,7},{2,4},{3,5},{4,2},{5,3},{6,0},{7,1},{8,14},{9,15},{10,... | collective-permute-start | bytes 49160 | tf_op jit(solution)/shard_map/ppermute | solution.py:34
  21.8 2.7 %copy-start = (bf16[1,64,1024]{2,1,0:T(8,128)(2,1)S(1)}, bf16[1,64,1024]{2,1,0:T(8,128)(2,1)}, u32[]{:S(2)}) copy-start(bf16[1,64,1024]{2,1,0:T(8,128)(2,1)} %param.9) | copy-start | bytes 393220
  21.8 2.7 %copy-start.1 = (bf16[16,1024]{1,0:T(8,128)(2,1)S(1)}, bf16[16,1024]{1,0:T(8,128)(2,1)}, u32[]{:S(2)}) copy-start(bf16[16,1024]{1,0:T(8,128)(2,1)} %coef.1) | copy-start | bytes 98308
  27.6 1.3 %collective-permute-start.11 = (f32[48,512]{1,0:T(8,128)S(1)}, f32[48,512]{1,0:T(8,128)S(1)}, u32[]{:S(2)}, u32[]{:S(2)}) collective-permute-start(f32[48,512]{1,0:T(8,128)S(1)} %get-tuple-element.47), channel_id=1, source_target_pairs={{0,4},{4,0},{8,12},{12,8},{1,5},{5,1},{9,13},{13,9},{2,6},{6,2},{1... | collective-permute-start | bytes 294920 | tf_op jit(solution)/shard_map/ppermute | solution.py:24
  28.9 3.6 %collective-permute-start.12 = (bf16[48,512]{1,0:T(8,128)(2,1)S(1)}, bf16[48,512]{1,0:T(8,128)(2,1)S(1)}, u32[]{:S(2)}, u32[]{:S(2)}) collective-permute-start(bf16[48,512]{1,0:T(8,128)(2,1)S(1)} %add_convert_fusion.1), channel_id=1, source_target_pairs={{0,12},{1,13},{2,14},{3,15},{4,8},{5,9},{6,10},{7,11},{8,4},{9,5},... | collective-permute-start | bytes 147464 | tf_op jit(solution)/shard_map/ppermute | solution.py:34
  32.5 6.2 %collective-permute-start.15 = (bf16[48,512]{1,0:T(8,128)(2,1)S(1)}, bf16[48,512]{1,0:T(8,128)(2,1)S(1)}, u32[]{:S(2)}, u32[]{:S(2)}) collective-permute-start(bf16[48,512]{1,0:T(8,128)(2,1)S(1)} %add_convert_fusion), channel_id=1, source_target_pairs={{0,3},{1,2},{2,1},{3,0},{4,7},{5,6},{6,5},{7,4},{8,11},{9,10},{10,... | collective-permute-start | bytes 147464 | tf_op jit(solution)/shard_map/ppermute | solution.py:34
  34.4 6.2 %collective-permute-start.14 = (bf16[48,512]{1,0:T(8,128)(2,1)S(1)}, bf16[48,512]{1,0:T(8,128)(2,1)S(1)}, u32[]{:S(2)}, u32[]{:S(2)}) collective-permute-start(bf16[48,512]{1,0:T(8,128)(2,1)S(1)} %add_convert_fusion), channel_id=1, source_target_pairs={{0,6},{1,7},{2,4},{3,5},{4,2},{5,3},{6,0},{7,1},{8,14},{9,15},{10,... | collective-permute-start | bytes 147464 | tf_op jit(solution)/shard_map/ppermute | solution.py:34
  35.2 5.4 %collective-permute-start.13 = (bf16[48,512]{1,0:T(8,128)(2,1)S(1)}, bf16[48,512]{1,0:T(8,128)(2,1)S(1)}, u32[]{:S(2)}, u32[]{:S(2)}) collective-permute-start(bf16[48,512]{1,0:T(8,128)(2,1)S(1)} %add_convert_fusion), channel_id=1, source_target_pairs={{0,5},{1,4},{2,7},{3,6},{4,1},{5,0},{6,3},{7,2},{8,13},{9,12},{10,... | collective-permute-start | bytes 147464 | tf_op jit(solution)/shard_map/ppermute | solution.py:34
  40.7 1.4 %collective-permute-start.16 = (f32[48,512]{1,0:T(8,128)S(1)}, f32[48,512]{1,0:T(8,128)S(1)}, u32[]{:S(2)}, u32[]{:S(2)}) collective-permute-start(f32[48,512]{1,0:T(8,128)S(1)} %add_add_fusion.scaled), channel_id=1, source_target_pairs={{0,4},{4,0},{8,12},{12,8},{1,5},{5,1},{9,13},{13,9},{2,6},{6,2},{1... | collective-permute-start | bytes 294920 | tf_op jit(solution)/shard_map/ppermute | solution.py:24

commit v6 on v5

--- a/solution.py
+++ b/solution.py
@@ -145,8 +145,8 @@
 
 def project_kernel(*refs):
     (latent_in, coef_in, proj_in, source_in, weight_in, target_in, wanted_in, area_in, factor_in, *rest) = refs
-    *payloads, proj_pad, products, pair_ids, target, wanted, area, factor = rest[:-6]
-    latent, coef, proj, source, weight, arrivals = rest[-6:]
+    *payloads, proj, proj_pad, products, pair_ids, target, wanted, area, factor = rest[:-5]
+    latent, coef, source, weight, arrivals = rest[-5:]
     moves = [
         pltpu.make_async_copy(there, here, arrivals.at[n])
         for n, (there, here) in enumerate(
@@ -285,7 +285,8 @@
     pair_grad = near_pair_grad[...]
     for i in range(bands):
         there = lax.bitwise_xor(band, i)
-        loss = jnp.sum(grads[i][variables : variables + 1, 0:128].astype(F32), axis=1, keepdims=True)
+        arrived = grads[i][...].astype(F32)
+        loss = jnp.sum(arrived[variables : variables + 1, 0:128], axis=1, keepdims=True)
         losses = losses + jnp.where(lane == there, loss, 0.0)
         if i not in early:
             spot = slice((i - 1) * cells_dev, i * cells_dev)
@@ -382,10 +383,11 @@
     padded = up(variables + 1, 16)
     pair_coef = FAIR_ALPHA / (members - 1) + (1.0 - FAIR_ALPHA) / members
 
-    *payloads, proj_pad, products, pair_ids, cell_ids, wanted, area, factor = call(
+    *payloads, _, proj_pad, products, pair_ids, cell_ids, wanted, area, factor = call(
         project_kernel,
         [shape(*packed_shape(variables, slots))] * bands
         + [
+            shape(variables, hidden, dtype=BF16),
             shape(padded, hidden, dtype=BF16),
             shape(pairs, hidden, dtype=BF16),
             shape(bands, 1, slots, dtype=jnp.int32),
@@ -408,7 +410,6 @@
         [
             pltpu.VMEM((rows, hidden), BF16),
             pltpu.VMEM((table, hidden), BF16),
-            pltpu.VMEM((variables, hidden), BF16),
             pltpu.VMEM(edge_source.shape, jnp.int32),
             pltpu.VMEM(edge_weight.shape, jnp.int32),
             pltpu.SemaphoreType.DMA((9,)),

time: 43.6 us -> 43.9 us (level)
  transfers between devices with their start and end apart: 17 -> 17, of which waited for: 10 -> 10; matrix products, arithmetic and copies ran while one was open for 0% -> 0% of each run, Pallas kernels for 8% -> 7%
where the time goes in v6:
time: 43.9 us; the launch traced here: 43.8 us
  starting transfers between devices  17.9 us (41%)
  waiting for transfers between devices  14 us (32%)
  Pallas kernels  11.1 us (25%)
  between operations  0.7 us (2%)
    ppermute x13, starting transfers between devices, cross(): return lax.ppermute(shard, ('member', 'band'), pairs)  16.9 us
    pallas_call x8, Pallas kernels, call(): pl.pallas_call(kernel, out_shape=outs, in_specs=[source] * len(operands),...  11.1 us
    ppermute x13, waiting for transfers between devices, cross(): return lax.ppermute(shard, ('member', 'band'), pairs)  10.9 us
    ppermute x4, waiting for transfers between devices, swap(): return lax.ppermute(shard, axis, [(i, i ^ mask) for i in range(peers)])  3.05 us
    ppermute x4, starting transfers between devices, swap(): return lax.ppermute(shard, axis, [(i, i ^ mask) for i in range(peers)])  1.05 us
  transfers between devices with their start and end apart: 17, of which 10 were waited for; matrix products, arithmetic and copies ran while one was open for 0% of the time, Pallas kernels for 7%

profile of v6, /device:TPU:0, one launch (start us, length us, event | category | flops | bytes accessed | tf_op | source)
XLA Modules:
  0.0 43.8 jit_solution(14621929899857945283)
XLA Ops:
  0.6 2.6 %shard_map.120 = (f32[80,128]{1,0:T(8,128)S(1)}, f32[80,128]{1,0:T(8,128)S(1)}, f32[80,128]{1,0:T(8,128)S(1)}, f32[80,128]{1,0:T(8,128)S(1)}, bf16[25,1024]{1,0:...) custom-call(bf16[64,1024]{1,0:T(8,128)(2,1)} %bitcast.5, ...), custom_call_target="tpu_custom_call" | custom-call | bytes 1048576 | tf_op jit(solution)/shard_map/pallas_call | solution.py:348
  3.3 4.6 %collective-permute-start = (f32[80,128]{1,0:T(8,128)S(1)}, f32[80,128]{1,0:T(8,128)S(1)}, u32[]{:S(2)}, u32[]{:S(2)}) collective-permute-start(f32[80,128]{1,0:T(8,128)S(1)} %get-tuple-element.30), channel_id=1, source_target_pairs={{0,7},{1,6},{2,5},{3,4},{4,3},{5,2},{6,1},{7,0},{8,15},{9,14},{10,... | collective-permute-start | bytes 122888 | tf_op jit(solution)/shard_map/ppermute | solution.py:34
  7.8 0.0 collective-permute-start.1
  7.8 0.9 %collective-permute-start.2 = (f32[80,128]{1,0:T(8,128)S(1)}, f32[80,128]{1,0:T(8,128)S(1)}, u32[]{:S(2)}, u32[]{:S(2)}) collective-permute-start(f32[80,128]{1,0:T(8,128)S(1)} %get-tuple-element.32), channel_id=1, source_target_pairs={{0,5},{1,4},{2,7},{3,6},{4,1},{5,0},{6,3},{7,2},{8,13},{9,12},{10,... | collective-permute-start | bytes 122888 | tf_op jit(solution)/shard_map/ppermute | solution.py:34
  8.8 0.0 collective-permute-start.3
  8.8 1.0 %collective-permute-done.refs_0_ = f32[80,128]{1,0:T(8,128)S(1)} collective-permute-done((f32[80,128]{1,0:T(8,128)S(1)}, f32[80,128]{1,0:T(8,128)S(1)}, u32[]{:S(2)}, u32[]{:S(2)}) %collective-permute-start) | collective-permute-done | bytes 40992 | tf_op jit(solution)/shard_map/ppermute | solution.py:34
  9.8 2.8 %collective-permute-done.1.refs_1_ = f32[80,128]{1,0:T(8,128)S(1)} collective-permute-done((f32[80,128]{1,0:T(8,128)S(1)}, f32[80,128]{1,0:T(8,128)S(1)}, u32[]{:S(2)}, u32[]{:S(2)}) %collective-permute-start.1) | collective-permute-done | bytes 40992 | tf_op jit(solution)/shard_map/ppermute | solution.py:34
  12.5 0.0 collective-permute-done.2.refs_2_
  12.5 0.0 collective-permute-done.3.refs_3_
  12.6 0.4 shard_map.121.refs_0_
  12.9 1.4 %collective-permute-start.4 = (f32[32,256]{1,0:T(8,128)S(1)}, f32[32,256]{1,0:T(8,128)S(1)}, u32[]{:S(2)}, u32[]{:S(2)}) collective-permute-start(f32[32,256]{1,0:T(8,128)S(1)} %shard_map.121.refs_0_), channel_id=1, source_target_pairs={{0,12},{1,13},{2,14},{3,15},{4,8},{5,9},{6,10},{7,11},{8,4},{9,5},... | collective-permute-start | bytes 98312 | tf_op jit(solution)/shard_map/ppermute | solution.py:34
  14.4 0.2 collective-permute-start.5
  14.6 1.3 %shard_map.122.counts = bf16[1024,1024]{1,0:T(8,128)(2,1)S(1)} custom-call(s32[4,1,384]{2,1,0:T(1,128)S(1)} %get-tuple-element.35.pair_ids, f32[80,128]{1,0:T(8,128)S(1)} %collective-permute-done.refs_0_, f32[80,128]{1,0:T(8,128)S(1)} %collective-permute-done.1.refs_1_, f32[80,128]{1,0:T(8,128)S(1)} %collective-permute-done.2.refs_2_, ...), custom_call_target="tpu_custom_call" | custom-call | flops 805306368 | bytes 1048576 | tf_op jit(solution)/shard_map/pallas_call | solution.py:348
  15.9 0.4 collective-permute-done.4.refs_3_
  16.3 0.3 collective-permute-start.6
  16.6 0.0 collective-permute-done.5.refs_1_
  16.6 0.9 %collective-permute-done.6.refs_2_ = f32[32,256]{1,0:T(8,128)S(1)} collective-permute-done((f32[32,256]{1,0:T(8,128)S(1)}, f32[32,256]{1,0:T(8,128)S(1)}, u32[]{:S(2)}, u32[]{:S(2)}) %collective-permute-start.6) | collective-permute-done | bytes 32800 | tf_op jit(solution)/shard_map/ppermute | solution.py:24
  17.5 0.3 shard_map.123
  17.8 0.4 collective-permute-start.8
  18.2 2.2 %collective-permute-start.7 = (bf16[32,256]{1,0:T(8,128)(2,1)S(1)}, bf16[32,256]{1,0:T(8,128)(2,1)S(1)}, u32[]{:S(2)}, u32[]{:S(2)}) collective-permute-start(bf16[32,256]{1,0:T(8,128)(2,1)S(1)} %shard_map.123), channel_id=1, source_target_pairs={{0,7},{1,6},{2,5},{3,4},{4,3},{5,2},{6,1},{7,0},{8,15},{9,14},{10,... | collective-permute-start | bytes 49160 | tf_op jit(solution)/shard_map/ppermute | solution.py:34
  20.4 0.3 collective-permute-start.9
  20.7 1.4 %collective-permute-start.10 = (bf16[32,256]{1,0:T(8,128)(2,1)S(1)}, bf16[32,256]{1,0:T(8,128)(2,1)S(1)}, u32[]{:S(2)}, u32[]{:S(2)}) collective-permute-start(bf16[32,256]{1,0:T(8,128)(2,1)S(1)} %shard_map.123), channel_id=1, source_target_pairs={{0,6},{1,7},{2,4},{3,5},{4,2},{5,3},{6,0},{7,1},{8,14},{9,15},{10,... | collective-permute-start | bytes 49160 | tf_op jit(solution)/shard_map/ppermute | solution.py:34
  22.1 0.0 collective-permute-done.8.grad.refs_2_
  22.1 0.0 copy-start
  22.1 0.0 copy-start.1
  22.1 1.0 %shard_map.124 = (f32[32,1024]{1,0:T(8,128)S(1)}, f32[1024,1024]{1,0:T(8,128)S(1)}) custom-call(bf16[32,1024]{1,0:T(8,128)(2,1)S(1)} %get-tuple-element.29.proj, bf16[1024,1024]{1,0:T(8,128)(2,1)S(1)} %shard_map.122.counts, bf16[32,256]{1,0:T(8,128)(2,1)S(1)} %collective-permute-done.8.grad.refs_2_), custom_call_target="tpu_custom_call" | custom-call | flops 536870912 | bytes 1048576 | tf_op jit(solution)/shard_map/pallas_call | solution.py:348
  23.1 0.0 collective-permute-done.7.grad.refs_5_
  23.2 1.0 %shard_map.125 = (f32[32,1024]{1,0:T(8,128)S(1)}, f32[1024,1024]{1,0:T(8,128)S(1)}) custom-call(bf16[32,1024]{1,0:T(8,128)(2,1)S(1)} %get-tuple-element.29.proj, bf16[1024,1024]{1,0:T(8,128)(2,1)S(1)} %shard_map.122.counts, bf16[32,256]{1,0:T(8,128)(2,1)S(1)} %collective-permute-done.7.grad.refs_5_, f32[32,1024]{1,0:T(8,128)S(1)} %get-tuple-element.42.refs_0_, ...), custom_call_target="tpu_custom_call" | custom-call | flops 536870912 | bytes 1048576 | tf_op jit(solution)/shard_map/pallas_call | solution.py:348
  24.2 0.0 collective-permute-done.9.refs_3_
  24.2 0.6 %collective-permute-done.10.refs_4_ = bf16[32,256]{1,0:T(8,128)(2,1)S(1)} collective-permute-done((bf16[32,256]{1,0:T(8,128)(2,1)S(1)}, bf16[32,256]{1,0:T(8,128)(2,1)S(1)}, u32[]{:S(2)}, u32[]{:S(2)}) %collective-permute-start.10) | collective-permute-done | bytes 16416 | tf_op jit(solution)/shard_map/ppermute | solution.py:34
  24.8 0.0 copy-done
  24.8 0.0 copy-done.1
  24.8 3.1 %shard_map.126 = (bf16[64,1024]{1,0:T(8,128)(2,1)S(1)}, f32[48,512]{1,0:T(8,128)S(1)}, f32[48,512]{1,0:T(8,128)S(1)}, f32[1,1]{1,0:T(1,128)}) custom-call(bf16[64,1024]{1,0:T(8,128)(2,1)S(1)} %bitcast.6, bf16[16,1024]{1,0:T(8,128)(2,1)S(1)} %copy-done.1, bf16[32,1024]{1,0:T(8,128)(2,1)S(1)} %get-tuple-element.29.proj, ...), custom_call_target="tpu_custom_call" | custom-call | bytes 1048576 | tf_op jit(solution)/shard_map/pallas_call | solution.py:348
  27.9 0.3 collective-permute-start.11
  28.3 1.0 %collective-permute-done.11 = f32[48,512]{1,0:T(8,128)S(1)} collective-permute-done((f32[48,512]{1,0:T(8,128)S(1)}, f32[48,512]{1,0:T(8,128)S(1)}, u32[]{:S(2)}, u32[]{:S(2)}) %collective-permute-start.11) | collective-permute-done | bytes 98336 | tf_op jit(solution)/shard_map/ppermute | solution.py:24
  29.2 1.5 %collective-permute-start.12 = (bf16[48,512]{1,0:T(8,128)(2,1)S(1)}, bf16[48,512]{1,0:T(8,128)(2,1)S(1)}, u32[]{:S(2)}, u32[]{:S(2)}) collective-permute-start(bf16[48,512]{1,0:T(8,128)(2,1)S(1)} %add_convert_fusion.1), channel_id=1, source_target_pairs={{0,12},{1,13},{2,14},{3,15},{4,8},{5,9},{6,10},{7,11},{8,4},{9,5},... | collective-permute-start | bytes 147464 | tf_op jit(solution)/shard_map/ppermute | solution.py:34
  30.8 2.1 %collective-permute-done.12 = bf16[48,512]{1,0:T(8,128)(2,1)S(1)} collective-permute-done((bf16[48,512]{1,0:T(8,128)(2,1)S(1)}, bf16[48,512]{1,0:T(8,128)(2,1)S(1)}, u32[]{:S(2)}, u32[]{:S(2)}) %collective-permute-start.12) | collective-permute-done | bytes 49184 | tf_op jit(solution)/shard_map/ppermute | solution.py:34
  32.8 1.9 %collective-permute-start.15 = (bf16[48,512]{1,0:T(8,128)(2,1)S(1)}, bf16[48,512]{1,0:T(8,128)(2,1)S(1)}, u32[]{:S(2)}, u32[]{:S(2)}) collective-permute-start(bf16[48,512]{1,0:T(8,128)(2,1)S(1)} %add_convert_fusion), channel_id=1, source_target_pairs={{0,3},{1,2},{2,1},{3,0},{4,7},{5,6},{6,5},{7,4},{8,11},{9,10},{10,... | collective-permute-start | bytes 147464 | tf_op jit(solution)/shard_map/ppermute | solution.py:34
  34.7 0.8 %collective-permute-start.14 = (bf16[48,512]{1,0:T(8,128)(2,1)S(1)}, bf16[48,512]{1,0:T(8,128)(2,1)S(1)}, u32[]{:S(2)}, u32[]{:S(2)}) collective-permute-start(bf16[48,512]{1,0:T(8,128)(2,1)S(1)} %add_convert_fusion), channel_id=1, source_target_pairs={{0,6},{1,7},{2,4},{3,5},{4,2},{5,3},{6,0},{7,1},{8,14},{9,15},{10,... | collective-permute-start | bytes 147464 | tf_op jit(solution)/shard_map/ppermute | solution.py:34
  35.5 1.5 %collective-permute-start.13 = (bf16[48,512]{1,0:T(8,128)(2,1)S(1)}, bf16[48,512]{1,0:T(8,128)(2,1)S(1)}, u32[]{:S(2)}, u32[]{:S(2)}) collective-permute-start(bf16[48,512]{1,0:T(8,128)(2,1)S(1)} %add_convert_fusion), channel_id=1, source_target_pairs={{0,5},{1,4},{2,7},{3,6},{4,1},{5,0},{6,3},{7,2},{8,13},{9,12},{10,... | collective-permute-start | bytes 147464 | tf_op jit(solution)/shard_map/ppermute | solution.py:34
  37.0 2.0 %collective-permute-done.15 = bf16[48,512]{1,0:T(8,128)(2,1)S(1)} collective-permute-done((bf16[48,512]{1,0:T(8,128)(2,1)S(1)}, bf16[48,512]{1,0:T(8,128)(2,1)S(1)}, u32[]{:S(2)}, u32[]{:S(2)}) %collective-permute-start.15) | collective-permute-done | bytes 49184 | tf_op jit(solution)/shard_map/ppermute | solution.py:34
  39.1 1.9 %collective-permute-done.14 = bf16[48,512]{1,0:T(8,128)(2,1)S(1)} collective-permute-done((bf16[48,512]{1,0:T(8,128)(2,1)S(1)}, bf16[48,512]{1,0:T(8,128)(2,1)S(1)}, u32[]{:S(2)}, u32[]{:S(2)}) %collective-permute-start.14) | collective-permute-done | bytes 49184 | tf_op jit(solution)/shard_map/ppermute | solution.py:34
  41.0 0.0 collective-permute-done.13
  41.0 0.2 collective-permute-start.16
  41.2 1.2 %collective-permute-done.16.other = f32[48,512]{1,0:T(8,128)S(1)} collective-permute-done((f32[48,512]{1,0:T(8,128)S(1)}, f32[48,512]{1,0:T(8,128)S(1)}, u32[]{:S(2)}, u32[]{:S(2)}) %collective-permute-start.16) | collective-permute-done | bytes 98336 | tf_op jit(solution)/shard_map/ppermute | solution.py:24
  42.4 1.4 %shard_map.127 = (bf16[64,1024]{1,0:T(8,128)(2,1)}, f32[25,1024]{1,0:T(8,128)}, f32[16,1024]{1,0:T(8,128)}, f32[1,1]{1,0:T(1,128)}) custom-call(f32[48,512]{1,0:T(8,128)S(1)} %add_add_fusion.scaled, f32[48,512]{1,0:T(8,128)S(1)} %collective-permute-done.16.other, bf16[64,1024]{1,0:T(8,128)(2,1)S(1)} %get-tuple-element.48.latent_grad, ...), custom_call_target="tpu_custom_call" | custom-call | bytes 1048576 | tf_op jit(solution)/shard_map/pallas_call | solution.py:348
  (3 shorter events, 0.1 us)
Async XLA Ops:
  3.3 6.5 %collective-permute-start = (f32[80,128]{1,0:T(8,128)S(1)}, f32[80,128]{1,0:T(8,128)S(1)}, u32[]{:S(2)}, u32[]{:S(2)}) collective-permute-start(f32[80,128]{1,0:T(8,128)S(1)} %get-tuple-element.30), channel_id=1, source_target_pairs={{0,7},{1,6},{2,5},{3,4},{4,3},{5,2},{6,1},{7,0},{8,15},{9,14},{10,... | collective-permute-start | bytes 122888 | tf_op jit(solution)/shard_map/ppermute | solution.py:34
  7.8 4.7 %collective-permute-start.1 = (f32[80,128]{1,0:T(8,128)S(1)}, f32[80,128]{1,0:T(8,128)S(1)}, u32[]{:S(2)}, u32[]{:S(2)}) collective-permute-start(f32[80,128]{1,0:T(8,128)S(1)} %get-tuple-element.31), channel_id=1, source_target_pairs={{0,6},{1,7},{2,4},{3,5},{4,2},{5,3},{6,0},{7,1},{8,14},{9,15},{10,... | collective-permute-start | bytes 122888 | tf_op jit(solution)/shard_map/ppermute | solution.py:34
  7.8 4.7 %collective-permute-start.2 = (f32[80,128]{1,0:T(8,128)S(1)}, f32[80,128]{1,0:T(8,128)S(1)}, u32[]{:S(2)}, u32[]{:S(2)}) collective-permute-start(f32[80,128]{1,0:T(8,128)S(1)} %get-tuple-element.32), channel_id=1, source_target_pairs={{0,5},{1,4},{2,7},{3,6},{4,1},{5,0},{6,3},{7,2},{8,13},{9,12},{10,... | collective-permute-start | bytes 122888 | tf_op jit(solution)/shard_map/ppermute | solution.py:34
  8.8 3.8 %collective-permute-start.3 = (f32[80,128]{1,0:T(8,128)S(1)}, f32[80,128]{1,0:T(8,128)S(1)}, u32[]{:S(2)}, u32[]{:S(2)}) collective-permute-start(f32[80,128]{1,0:T(8,128)S(1)} %get-tuple-element.33), channel_id=1, source_target_pairs={{0,4},{1,5},{2,6},{3,7},{4,0},{5,1},{6,2},{7,3},{8,12},{9,13},{10,... | collective-permute-start | bytes 122888 | tf_op jit(solution)/shard_map/ppermute | solution.py:34
  12.9 3.4 %collective-permute-start.4 = (f32[32,256]{1,0:T(8,128)S(1)}, f32[32,256]{1,0:T(8,128)S(1)}, u32[]{:S(2)}, u32[]{:S(2)}) collective-permute-start(f32[32,256]{1,0:T(8,128)S(1)} %shard_map.121.refs_0_), channel_id=1, source_target_pairs={{0,12},{1,13},{2,14},{3,15},{4,8},{5,9},{6,10},{7,11},{8,4},{9,5},... | collective-permute-start | bytes 98312 | tf_op jit(solution)/shard_map/ppermute | solution.py:34
  14.4 2.2 %collective-permute-start.5 = (f32[32,256]{1,0:T(8,128)S(1)}, f32[32,256]{1,0:T(8,128)S(1)}, u32[]{:S(2)}, u32[]{:S(2)}) collective-permute-start(f32[32,256]{1,0:T(8,128)S(1)} %shard_map.121.refs_0_), channel_id=1, source_target_pairs={{0,4},{4,0},{8,12},{12,8},{1,5},{5,1},{9,13},{13,9},{2,6},{6,2},{1... | collective-permute-start | bytes 98312 | tf_op jit(solution)/shard_map/ppermute | solution.py:24
  16.3 1.2 %collective-permute-start.6 = (f32[32,256]{1,0:T(8,128)S(1)}, f32[32,256]{1,0:T(8,128)S(1)}, u32[]{:S(2)}, u32[]{:S(2)}) collective-permute-start(f32[32,256]{1,0:T(8,128)S(1)} %collective-permute-done.4.refs_3_), channel_id=1, source_target_pairs={{0,4},{4,0},{8,12},{12,8},{1,5},{5,1},{9,13},{13,9},{2,6},{6,2},{1... | collective-permute-start | bytes 98312 | tf_op jit(solution)/shard_map/ppermute | solution.py:24
  17.8 4.3 %collective-permute-start.8 = (bf16[32,256]{1,0:T(8,128)(2,1)S(1)}, bf16[32,256]{1,0:T(8,128)(2,1)S(1)}, u32[]{:S(2)}, u32[]{:S(2)}) collective-permute-start(bf16[32,256]{1,0:T(8,128)(2,1)S(1)} %shard_map.123), channel_id=1, source_target_pairs={{0,4},{1,5},{2,6},{3,7},{4,0},{5,1},{6,2},{7,3},{8,12},{9,13},{10,... | collective-permute-start | bytes 49160 | tf_op jit(solution)/shard_map/ppermute | solution.py:34
  18.2 5.0 %collective-permute-start.7 = (bf16[32,256]{1,0:T(8,128)(2,1)S(1)}, bf16[32,256]{1,0:T(8,128)(2,1)S(1)}, u32[]{:S(2)}, u32[]{:S(2)}) collective-permute-start(bf16[32,256]{1,0:T(8,128)(2,1)S(1)} %shard_map.123), channel_id=1, source_target_pairs={{0,7},{1,6},{2,5},{3,4},{4,3},{5,2},{6,1},{7,0},{8,15},{9,14},{10,... | collective-permute-start | bytes 49160 | tf_op jit(solution)/shard_map/ppermute | solution.py:34
  20.4 3.7 %collective-permute-start.9 = (bf16[32,256]{1,0:T(8,128)(2,1)S(1)}, bf16[32,256]{1,0:T(8,128)(2,1)S(1)}, u32[]{:S(2)}, u32[]{:S(2)}) collective-permute-start(bf16[32,256]{1,0:T(8,128)(2,1)S(1)} %shard_map.123), channel_id=1, source_target_pairs={{0,5},{1,4},{2,7},{3,6},{4,1},{5,0},{6,3},{7,2},{8,13},{9,12},{10,... | collective-permute-start | bytes 49160 | tf_op jit(solution)/shard_map/ppermute | solution.py:34
  20.7 4.1 %collective-permute-start.10 = (bf16[32,256]{1,0:T(8,128)(2,1)S(1)}, bf16[32,256]{1,0:T(8,128)(2,1)S(1)}, u32[]{:S(2)}, u32[]{:S(2)}) collective-permute-start(bf16[32,256]{1,0:T(8,128)(2,1)S(1)} %shard_map.123), channel_id=1, source_target_pairs={{0,6},{1,7},{2,4},{3,5},{4,2},{5,3},{6,0},{7,1},{8,14},{9,15},{10,... | collective-permute-start | bytes 49160 | tf_op jit(solution)/shard_map/ppermute | solution.py:34
  22.1 2.7 %copy-start = (bf16[1,64,1024]{2,1,0:T(8,128)(2,1)S(1)}, bf16[1,64,1024]{2,1,0:T(8,128)(2,1)}, u32[]{:S(2)}) copy-start(bf16[1,64,1024]{2,1,0:T(8,128)(2,1)} %param.9) | copy-start | bytes 393220
  22.1 2.7 %copy-start.1 = (bf16[16,1024]{1,0:T(8,128)(2,1)S(1)}, bf16[16,1024]{1,0:T(8,128)(2,1)}, u32[]{:S(2)}) copy-start(bf16[16,1024]{1,0:T(8,128)(2,1)} %coef.1) | copy-start | bytes 98308
  27.9 1.3 %collective-permute-start.11 = (f32[48,512]{1,0:T(8,128)S(1)}, f32[48,512]{1,0:T(8,128)S(1)}, u32[]{:S(2)}, u32[]{:S(2)}) collective-permute-start(f32[48,512]{1,0:T(8,128)S(1)} %get-tuple-element.47), channel_id=1, source_target_pairs={{0,4},{4,0},{8,12},{12,8},{1,5},{5,1},{9,13},{13,9},{2,6},{6,2},{1... | collective-permute-start | bytes 294920 | tf_op jit(solution)/shard_map/ppermute | solution.py:24
  29.2 3.6 %collective-permute-start.12 = (bf16[48,512]{1,0:T(8,128)(2,1)S(1)}, bf16[48,512]{1,0:T(8,128)(2,1)S(1)}, u32[]{:S(2)}, u32[]{:S(2)}) collective-permute-start(bf16[48,512]{1,0:T(8,128)(2,1)S(1)} %add_convert_fusion.1), channel_id=1, source_target_pairs={{0,12},{1,13},{2,14},{3,15},{4,8},{5,9},{6,10},{7,11},{8,4},{9,5},... | collective-permute-start | bytes 147464 | tf_op jit(solution)/shard_map/ppermute | solution.py:34
  32.8 6.2 %collective-permute-start.15 = (bf16[48,512]{1,0:T(8,128)(2,1)S(1)}, bf16[48,512]{1,0:T(8,128)(2,1)S(1)}, u32[]{:S(2)}, u32[]{:S(2)}) collective-permute-start(bf16[48,512]{1,0:T(8,128)(2,1)S(1)} %add_convert_fusion), channel_id=1, source_target_pairs={{0,3},{1,2},{2,1},{3,0},{4,7},{5,6},{6,5},{7,4},{8,11},{9,10},{10,... | collective-permute-start | bytes 147464 | tf_op jit(solution)/shard_map/ppermute | solution.py:34
  34.7 6.2 %collective-permute-start.14 = (bf16[48,512]{1,0:T(8,128)(2,1)S(1)}, bf16[48,512]{1,0:T(8,128)(2,1)S(1)}, u32[]{:S(2)}, u32[]{:S(2)}) collective-permute-start(bf16[48,512]{1,0:T(8,128)(2,1)S(1)} %add_convert_fusion), channel_id=1, source_target_pairs={{0,6},{1,7},{2,4},{3,5},{4,2},{5,3},{6,0},{7,1},{8,14},{9,15},{10,... | collective-permute-start | bytes 147464 | tf_op jit(solution)/shard_map/ppermute | solution.py:34
  35.5 5.5 %collective-permute-start.13 = (bf16[48,512]{1,0:T(8,128)(2,1)S(1)}, bf16[48,512]{1,0:T(8,128)(2,1)S(1)}, u32[]{:S(2)}, u32[]{:S(2)}) collective-permute-start(bf16[48,512]{1,0:T(8,128)(2,1)S(1)} %add_convert_fusion), channel_id=1, source_target_pairs={{0,5},{1,4},{2,7},{3,6},{4,1},{5,0},{6,3},{7,2},{8,13},{9,12},{10,... | collective-permute-start | bytes 147464 | tf_op jit(solution)/shard_map/ppermute | solution.py:34
  41.0 1.4 %collective-permute-start.16 = (f32[48,512]{1,0:T(8,128)S(1)}, f32[48,512]{1,0:T(8,128)S(1)}, u32[]{:S(2)}, u32[]{:S(2)}) collective-permute-start(f32[48,512]{1,0:T(8,128)S(1)} %add_add_fusion.scaled), channel_id=1, source_target_pairs={{0,4},{4,0},{8,12},{12,8},{1,5},{5,1},{9,13},{13,9},{2,6},{6,2},{1... | collective-permute-start | bytes 294920 | tf_op jit(solution)/shard_map/ppermute | solution.py:24

commit v7 on v6

--- a/solution.py
+++ b/solution.py
@@ -270,39 +270,38 @@
         block[:, h : h + step] = before[1][:, h : h + step] + here if before else here
 
 
-def backward_kernel(members, variables, early, scale_proj, scale_coef, scale_loss, latent, coef, proj, counts, products, *refs):
-    near_pair_grad, near_block, *grads = refs[:-6]
-    latent_grad, keep, send, mean_loss, cell_grad, sums = refs[-6:]
-    bands = len(grads)
-    band = lax.axis_index("band")
+def backward_kernel(members, variables, early, sent, scales, latent, coef, proj, counts, products, *refs):
+    near_pair_grad, near_block, *rest = refs
+    bands = lax.axis_size("band")
+    grads, rest = rest[:bands], rest[bands:]
+    latent_grad, sums, *all_pairs, cell_grad, wide_pairs = rest
+    scale_proj, scale_coef = scales
     side = half_here(members, bands)
-    rows, hidden = latent.shape
+    rows, half = latent_grad.shape
     table = coef.shape[0]
     cells_dev = grads[0].shape[1]
     padded = grads[0].shape[0]
-    lane = lax.broadcasted_iota(jnp.int32, (1, 128), 1)
-    losses = jnp.zeros((1, 128), F32)
-    pair_grad = near_pair_grad[...]
+    base = (1 - side if sent else side) * half
+    here = pl.ds(pl.multiple_of(base, half), half)
+    wide_pairs[...] = near_pair_grad[...]
     for i in range(bands):
-        there = lax.bitwise_xor(band, i)
-        arrived = grads[i][...].astype(F32)
-        loss = jnp.sum(arrived[variables : variables + 1, 0:128], axis=1, keepdims=True)
-        losses = losses + jnp.where(lane == there, loss, 0.0)
         if i not in early:
+            grad = only_grads(grads[i][...], variables)
             spot = slice((i - 1) * cells_dev, i * cells_dev)
-            cell_grad[spot, :], here = back_to_pairs(
-                only_grads(grads[i][...], variables),
-                proj[...],
-                counts[:, i * cells_dev : (i + 1) * cells_dev],
-            )
-            pair_grad = pair_grad + here
-    mean_loss[...] = jnp.sum(losses, axis=1, keepdims=True) * scale_loss
-    sums[0:padded, :] = whole(dot(parts(pair_grad), products[...], 1, 0)) * scale_proj
+            cell_grad[spot, :] = dot(grad, proj[:, here], 0, 0).astype(BF16)
+            if sent:
+                wide_pairs[...] += dot(grad, counts[:, i * cells_dev : (i + 1) * cells_dev], 1, 1)
+    if sent:
+        all_pairs[0][...] = wide_pairs[...]
+    sums[0:padded, :] = whole(dot(parts(wide_pairs[...]), products[:, here], 1, 0)) * scale_proj
     step = 256
-    for h in range(0, hidden, step):
-        block = near_block[:, h : h + step] + dot(counts[:, cells_dev : cells_dev + cell_grad.shape[0]], cell_grad[:, h : h + step], 1, 0)
-        wide = latent[:, h : h + step].astype(F32)
-        scale = coef[:, h : h + step].astype(F32)
+    for h in range(0, half, step):
+        spot = pl.ds(pl.multiple_of(base + h, step), step)
+        block = near_block[:, spot] + dot(
+            counts[:, cells_dev : cells_dev + cell_grad.shape[0]], cell_grad[:, h : h + step], 1, 0
+        )
+        wide = latent[:, spot].astype(F32)
+        scale = coef[:, spot].astype(F32)
         into_latent = 0.0
         for q in range(table):
             piece = block[q * rows : (q + 1) * rows, :]
@@ -311,13 +310,21 @@
                 jnp.sum(piece * wide, axis=0, keepdims=True) * scale_coef
             )
         latent_grad[:, h : h + step] = into_latent.astype(BF16)
-    half = hidden // 2
-    left, right = sums[:, 0:half], sums[:, half:hidden]
-    keep[...] = jnp.where(side == 0, left, right)
-    send[...] = jnp.where(side == 0, right, left)
-
-
-def write_kernel(members, bands, variables, scaled, other, latent_grad, mean_loss, *refs):
+
+
+def loss_kernel(variables, scale, *refs):
+    *grads, mean_loss = refs
+    band = lax.axis_index("band")
+    lane = lax.broadcasted_iota(jnp.int32, (1, 128), 1)
+    losses = jnp.zeros((1, 128), F32)
+    for i, grad in enumerate(grads):
+        arrived = grad[...].astype(F32)
+        loss = jnp.sum(arrived[variables : variables + 1, 0:128], axis=1, keepdims=True)
+        losses = losses + jnp.where(lane == lax.bitwise_xor(band, i), loss, 0.0)
+    mean_loss[...] = jnp.sum(losses, axis=1, keepdims=True) * scale
+
+
+def write_kernel(members, bands, variables, scaled, other, latent_here, latent_there, mean_loss, *refs):
     latent_out, proj_out, coef_out, loss_out, proj, leaves = refs
     side = half_here(members, bands)
     half = scaled.shape[1]
@@ -327,7 +334,8 @@
     moves = [
         (scaled.at[first:, :], coef_out.at[:, here]),
         (other.at[first:, :], coef_out.at[:, there]),
-        (latent_grad, latent_out),
+        (latent_here, latent_out.at[:, here]),
+        (latent_there, latent_out.at[:, there]),
         (mean_loss, loss_out),
         (proj, proj_out),
     ]
@@ -451,33 +459,40 @@
             [pltpu.VMEM((cells_dev, hidden), BF16)],
             flops=2 * pairs * cells_dev * hidden,
         )
-    latent_grad, keep, send, mean_loss = call(
-        functools.partial(
-            backward_kernel,
-            members,
-            variables,
-            early,
-            1.0 / math.sqrt(members * cells_all),
-            1.0 / math.sqrt(members * cells_all * K),
-            1.0 / (members * variables * cells_all),
-        ),
-        [
-            shape(rows, hidden, dtype=BF16),
-            shape(padded + table, hidden // 2),
-            shape(padded + table, hidden // 2),
-            shape(1, 1),
-        ],
-        (latent_rows, coef_table, proj_pad, counts, products, *sums, *grads),
-        [
-            pltpu.VMEM((cells_all - len(early) * cells_dev, hidden), BF16),
-            pltpu.VMEM((padded + table, hidden), F32),
-        ],
+    half = hidden // 2
+    scales = (
+        1.0 / math.sqrt(members * cells_all),
+        1.0 / math.sqrt(members * cells_all * K),
+    )
+    pair_grad, block = sums
+
+    def half_back(sent, pair_grad):
+        return call(
+            functools.partial(backward_kernel, members, variables, early, sent, scales),
+            [shape(rows, half, dtype=BF16), shape(padded + table, half)] + [shape(padded, pairs)] * sent,
+            (latent_rows, coef_table, proj_pad, counts, products, pair_grad, block, *grads),
+            [
+                pltpu.VMEM((cells_all - len(early) * cells_dev, half), BF16),
+                pltpu.VMEM((padded, pairs), F32),
+            ],
+            flops=2 * pairs * cells_all * half,
+        )
+
+    latent_there, send, pair_grad = half_back(True, pair_grad)
+    latent_here, keep = half_back(False, pair_grad)
+    (mean_loss,) = call(
+        functools.partial(loss_kernel, variables, 1.0 / (members * variables * cells_all)),
+        [shape(1, 1)],
+        grads,
     )
     total = keep + swap(send, "member", 1)
     step = 2
     while step < members:
         rounded = total.astype(BF16)
-        total = rounded.astype(F32) + cross(rounded, step + 1, 0).astype(F32)
+        far = cross(rounded, step + 1, 0)
+        if step == 2:
+            far, mean_loss = lax.optimization_barrier((far, mean_loss))
+        total = rounded.astype(F32) + far.astype(F32)
         step *= 2
     step = 1
     while step < bands:
@@ -496,8 +511,8 @@
             shape(table, hidden),
             shape(1, 1),
         ],
-        (total, other, latent_grad, mean_loss),
-        [pltpu.VMEM((variables, hidden), F32), pltpu.SemaphoreType.DMA((5,))],
+        (total, other, latent_here, latent_there, mean_loss),
+        [pltpu.VMEM((variables, hidden), F32), pltpu.SemaphoreType.DMA((6,))],
         sink=HBM,
     )
     return (latent_out[None], proj_grad, coef_grad, loss_out.reshape(1))

time: 43.9 us -> 42.8 us (0.975)
  waiting for transfers between devices: 14 us -> 12.6 us
    ppermute x4, waiting for transfers between devices: 3.05 us -> 2.11 us  [swap(): return lax.ppermute(shard, axis, [(i, i ^ mask) for i in range(peers)])]
    pallas_call x8 -> x10, Pallas kernels: 11.1 us -> 11.5 us  [call(): pl.pallas_call(kernel, out_shape=outs, in_specs=[source] * len(operands),...]
  transfers between devices with their start and end apart: 17 -> 17, of which waited for: 10 -> 9; matrix products, arithmetic and copies ran while one was open for 0% -> 0% of each run, Pallas kernels for 7% -> 12%
where the time goes in v7:
time: 42.8 us; the launch traced here: 42.7 us
  starting transfers between devices  17.8 us (42%)
  waiting for transfers between devices  12.6 us (29%)
  Pallas kernels  11.5 us (27%)
  between operations  0.73 us (2%)
    ppermute x13, starting transfers between devices, cross(): return lax.ppermute(shard, ('member', 'band'), pairs)  16.7 us
    pallas_call x10, Pallas kernels, call(): pl.pallas_call(kernel, out_shape=outs, in_specs=[source] * len(operands),...  11.5 us
    ppermute x13, waiting for transfers between devices, cross(): return lax.ppermute(shard, ('member', 'band'), pairs)  10.5 us
    ppermute x4, waiting for transfers between devices, swap(): return lax.ppermute(shard, axis, [(i, i ^ mask) for i in range(peers)])  2.11 us
    ppermute x4, starting transfers between devices, swap(): return lax.ppermute(shard, axis, [(i, i ^ mask) for i in range(peers)])  1.11 us
  transfers between devices with their start and end apart: 17, of which 9 were waited for; matrix products, arithmetic and copies ran while one was open for 0% of the time, Pallas kernels for 12%

profile of v7, /device:TPU:0, one launch (start us, length us, event | category | flops | bytes accessed | tf_op | source)
XLA Modules:
  0.0 42.7 jit_solution(11475278318836129759)
XLA Ops:
  0.6 2.6 %shard_map.120 = (f32[80,128]{1,0:T(8,128)S(1)}, f32[80,128]{1,0:T(8,128)S(1)}, f32[80,128]{1,0:T(8,128)S(1)}, f32[80,128]{1,0:T(8,128)S(1)}, bf16[25,1024]{1,0:...) custom-call(bf16[64,1024]{1,0:T(8,128)(2,1)} %bitcast.5, ...), custom_call_target="tpu_custom_call" | custom-call | bytes 1048576 | tf_op jit(solution)/shard_map/pallas_call | solution.py:356
  3.3 4.6 %collective-permute-start = (f32[80,128]{1,0:T(8,128)S(1)}, f32[80,128]{1,0:T(8,128)S(1)}, u32[]{:S(2)}, u32[]{:S(2)}) collective-permute-start(f32[80,128]{1,0:T(8,128)S(1)} %get-tuple-element.33), channel_id=1, source_target_pairs={{0,7},{1,6},{2,5},{3,4},{4,3},{5,2},{6,1},{7,0},{8,15},{9,14},{10,... | collective-permute-start | bytes 122888 | tf_op jit(solution)/shard_map/ppermute | solution.py:34
  7.8 0.0 collective-permute-start.1
  7.8 0.9 %collective-permute-start.2 = (f32[80,128]{1,0:T(8,128)S(1)}, f32[80,128]{1,0:T(8,128)S(1)}, u32[]{:S(2)}, u32[]{:S(2)}) collective-permute-start(f32[80,128]{1,0:T(8,128)S(1)} %get-tuple-element.35), channel_id=1, source_target_pairs={{0,5},{1,4},{2,7},{3,6},{4,1},{5,0},{6,3},{7,2},{8,13},{9,12},{10,... | collective-permute-start | bytes 122888 | tf_op jit(solution)/shard_map/ppermute | solution.py:34
  8.8 0.0 collective-permute-start.3
  8.8 1.0 %collective-permute-done.refs_0_ = f32[80,128]{1,0:T(8,128)S(1)} collective-permute-done((f32[80,128]{1,0:T(8,128)S(1)}, f32[80,128]{1,0:T(8,128)S(1)}, u32[]{:S(2)}, u32[]{:S(2)}) %collective-permute-start) | collective-permute-done | bytes 40992 | tf_op jit(solution)/shard_map/ppermute | solution.py:34
  9.8 2.8 %collective-permute-done.1.refs_1_ = f32[80,128]{1,0:T(8,128)S(1)} collective-permute-done((f32[80,128]{1,0:T(8,128)S(1)}, f32[80,128]{1,0:T(8,128)S(1)}, u32[]{:S(2)}, u32[]{:S(2)}) %collective-permute-start.1) | collective-permute-done | bytes 40992 | tf_op jit(solution)/shard_map/ppermute | solution.py:34
  12.5 0.0 collective-permute-done.2.refs_2_
  12.5 0.0 collective-permute-done.3.refs_3_
  12.6 0.4 shard_map.121.refs_0_
  12.9 1.4 %collective-permute-start.4 = (f32[32,256]{1,0:T(8,128)S(1)}, f32[32,256]{1,0:T(8,128)S(1)}, u32[]{:S(2)}, u32[]{:S(2)}) collective-permute-start(f32[32,256]{1,0:T(8,128)S(1)} %shard_map.121.refs_0_), channel_id=1, source_target_pairs={{0,12},{1,13},{2,14},{3,15},{4,8},{5,9},{6,10},{7,11},{8,4},{9,5},... | collective-permute-start | bytes 98312 | tf_op jit(solution)/shard_map/ppermute | solution.py:34
  14.4 0.2 collective-permute-start.5
  14.6 1.3 %shard_map.122.counts = bf16[1024,1024]{1,0:T(8,128)(2,1)S(1)} custom-call(s32[4,1,384]{2,1,0:T(1,128)S(1)} %get-tuple-element.38.pair_ids, f32[80,128]{1,0:T(8,128)S(1)} %collective-permute-done.refs_0_, f32[80,128]{1,0:T(8,128)S(1)} %collective-permute-done.1.refs_1_, f32[80,128]{1,0:T(8,128)S(1)} %collective-permute-done.2.refs_2_, ...), custom_call_target="tpu_custom_call" | custom-call | flops 805306368 | bytes 1048576 | tf_op jit(solution)/shard_map/pallas_call | solution.py:356
  15.9 0.4 %collective-permute-done.4.refs_3_ = f32[32,256]{1,0:T(8,128)S(1)} collective-permute-done((f32[32,256]{1,0:T(8,128)S(1)}, f32[32,256]{1,0:T(8,128)S(1)}, u32[]{:S(2)}, u32[]{:S(2)}) %collective-permute-start.4) | collective-permute-done | bytes 32800 | tf_op jit(solution)/shard_map/ppermute | solution.py:34
  16.3 0.3 collective-permute-start.6
  16.6 0.0 collective-permute-done.5.refs_1_
  16.6 0.9 %collective-permute-done.6.refs_2_ = f32[32,256]{1,0:T(8,128)S(1)} collective-permute-done((f32[32,256]{1,0:T(8,128)S(1)}, f32[32,256]{1,0:T(8,128)S(1)}, u32[]{:S(2)}, u32[]{:S(2)}) %collective-permute-start.6) | collective-permute-done | bytes 32800 | tf_op jit(solution)/shard_map/ppermute | solution.py:24
  17.5 0.3 shard_map.123
  17.8 0.4 collective-permute-start.8
  18.2 2.2 %collective-permute-start.7 = (bf16[32,256]{1,0:T(8,128)(2,1)S(1)}, bf16[32,256]{1,0:T(8,128)(2,1)S(1)}, u32[]{:S(2)}, u32[]{:S(2)}) collective-permute-start(bf16[32,256]{1,0:T(8,128)(2,1)S(1)} %shard_map.123), channel_id=1, source_target_pairs={{0,7},{1,6},{2,5},{3,4},{4,3},{5,2},{6,1},{7,0},{8,15},{9,14},{10,... | collective-permute-start | bytes 49160 | tf_op jit(solution)/shard_map/ppermute | solution.py:34
  20.4 0.3 collective-permute-start.9
  20.7 1.4 %collective-permute-start.10 = (bf16[32,256]{1,0:T(8,128)(2,1)S(1)}, bf16[32,256]{1,0:T(8,128)(2,1)S(1)}, u32[]{:S(2)}, u32[]{:S(2)}) collective-permute-start(bf16[32,256]{1,0:T(8,128)(2,1)S(1)} %shard_map.123), channel_id=1, source_target_pairs={{0,6},{1,7},{2,4},{3,5},{4,2},{5,3},{6,0},{7,1},{8,14},{9,15},{10,... | collective-permute-start | bytes 49160 | tf_op jit(solution)/shard_map/ppermute | solution.py:34
  22.1 0.0 collective-permute-done.8.grad.refs_2_.refs_0_
  22.1 0.0 copy-start
  22.1 0.0 copy-start.1
  22.1 1.0 %shard_map.124 = (f32[32,1024]{1,0:T(8,128)S(1)}, f32[1024,1024]{1,0:T(8,128)S(1)}) custom-call(bf16[32,1024]{1,0:T(8,128)(2,1)S(1)} %get-tuple-element.32.proj, bf16[1024,1024]{1,0:T(8,128)(2,1)S(1)} %shard_map.122.counts, bf16[32,256]{1,0:T(8,128)(2,1)S(1)} %collective-permute-done.8.grad.refs_2_.refs_0_), custom_call_target="tpu_custom_call" | custom-call | flops 536870912 | bytes 1048576 | tf_op jit(solution)/shard_map/pallas_call | solution.py:356
  23.1 0.0 collective-permute-done.7.grad.refs_5_.refs_3_
  23.2 1.0 %shard_map.125 = (f32[32,1024]{1,0:T(8,128)S(1)}, f32[1024,1024]{1,0:T(8,128)S(1)}) custom-call(bf16[32,1024]{1,0:T(8,128)(2,1)S(1)} %get-tuple-element.32.proj, bf16[1024,1024]{1,0:T(8,128)(2,1)S(1)} %shard_map.122.counts, bf16[32,256]{1,0:T(8,128)(2,1)S(1)} %collective-permute-done.7.grad.refs_5_.refs_3_, f32[32,1024]{1,0:T(8,128)S(1)} %get-tuple-element.45.refs_0_, ...), custom_call_target="tpu_custom_call" | custom-call | flops 536870912 | bytes 1048576 | tf_op jit(solution)/shard_map/pallas_call | solution.py:356
  24.2 0.0 collective-permute-done.9.refs_3_.refs_1_
  24.2 0.6 %collective-permute-done.10.refs_4_.refs_2_ = bf16[32,256]{1,0:T(8,128)(2,1)S(1)} collective-permute-done((bf16[32,256]{1,0:T(8,128)(2,1)S(1)}, bf16[32,256]{1,0:T(8,128)(2,1)S(1)}, u32[]{:S(2)}, u32[]{:S(2)}) %collective-permute-start.10) | collective-permute-done | bytes 16416 | tf_op jit(solution)/shard_map/ppermute | solution.py:34
  24.8 0.0 copy-done
  24.8 0.0 copy-done.1
  24.8 1.5 %shard_map.126 = (bf16[64,512]{1,0:T(8,128)(2,1)S(1)}, f32[48,512]{1,0:T(8,128)S(1)}, f32[32,1024]{1,0:T(8,128)S(1)}) custom-call(bf16[64,1024]{1,0:T(8,128)(2,1)S(1)} %bitcast.6, bf16[16,1024]{1,0:T(8,128)(2,1)S(1)} %copy-done.1, bf16[32,1024]{1,0:T(8,128)(2,1)S(1)} %get-tuple-element.32.proj, bf16[1024,1024]{1,0:T(8,128)(2,1)S(1)} %shard_map.122.counts, ...), custom_call_target="tpu_custom_call" | custom-call | flops 1073741824 | bytes 1048576 | tf_op jit(solution)/shard_map/pallas_call | solution.py:356
  26.3 0.4 collective-permute-start.11
  26.8 1.3 %shard_map.127 = (bf16[64,512]{1,0:T(8,128)(2,1)S(1)}, f32[48,512]{1,0:T(8,128)S(1)}) custom-call(bf16[64,1024]{1,0:T(8,128)(2,1)S(1)} %bitcast.7, bf16[16,1024]{1,0:T(8,128)(2,1)S(1)} %copy-done.1, bf16[32,1024]{1,0:T(8,128)(2,1)S(1)} %get-tuple-element.32.proj, bf16[1024,1024]{1,0:T(8,128)(2,1)S(1)} %shard_map.122.counts, ...), custom_call_target="tpu_custom_call" | custom-call | flops 1073741824 | bytes 1048576 | tf_op jit(solution)/shard_map/pallas_call | solution.py:356
  28.0 0.0 collective-permute-done.11
  28.1 1.3 %collective-permute-start.12 = (bf16[48,512]{1,0:T(8,128)(2,1)S(1)}, bf16[48,512]{1,0:T(8,128)(2,1)S(1)}, u32[]{:S(2)}, u32[]{:S(2)}) collective-permute-start(bf16[48,512]{1,0:T(8,128)(2,1)S(1)} %add_convert_fusion.1), channel_id=1, source_target_pairs={{0,12},{1,13},{2,14},{3,15},{4,8},{5,9},{6,10},{7,11},{8,4},{9,5},... | collective-permute-start | bytes 147464 | tf_op jit(solution)/shard_map/ppermute | solution.py:34
  29.4 0.7 %shard_map.128.mean_loss = f32[1,1]{1,0:T(1,128)} custom-call(bf16[32,256]{1,0:T(8,128)(2,1)S(1)} %collective-permute-done.8.grad.refs_2_.refs_0_, bf16[32,256]{1,0:T(8,128)(2,1)S(1)} %collective-permute-done.9.refs_3_.refs_1_, bf16[32,256]{1,0:T(8,128)(2,1)S(1)} %collective-permute-done.10.refs_4_.refs_2_, ...), custom_call_target="tpu_custom_call" | custom-call | bytes 1048576 | tf_op jit(solution)/shard_map/pallas_call | solution.py:356
  30.1 1.8 %collective-permute-done.12 = bf16[48,512]{1,0:T(8,128)(2,1)S(1)} collective-permute-done((bf16[48,512]{1,0:T(8,128)(2,1)S(1)}, bf16[48,512]{1,0:T(8,128)(2,1)S(1)}, u32[]{:S(2)}, u32[]{:S(2)}) %collective-permute-start.12) | collective-permute-done | bytes 49184 | tf_op jit(solution)/shard_map/ppermute | solution.py:34
  31.9 1.8 %collective-permute-start.15 = (bf16[48,512]{1,0:T(8,128)(2,1)S(1)}, bf16[48,512]{1,0:T(8,128)(2,1)S(1)}, u32[]{:S(2)}, u32[]{:S(2)}) collective-permute-start(bf16[48,512]{1,0:T(8,128)(2,1)S(1)} %add_convert_fusion), channel_id=1, source_target_pairs={{0,3},{1,2},{2,1},{3,0},{4,7},{5,6},{6,5},{7,4},{8,11},{9,10},{10,... | collective-permute-start | bytes 147464 | tf_op jit(solution)/shard_map/ppermute | solution.py:34
  33.7 0.6 %collective-permute-start.14 = (bf16[48,512]{1,0:T(8,128)(2,1)S(1)}, bf16[48,512]{1,0:T(8,128)(2,1)S(1)}, u32[]{:S(2)}, u32[]{:S(2)}) collective-permute-start(bf16[48,512]{1,0:T(8,128)(2,1)S(1)} %add_convert_fusion), channel_id=1, source_target_pairs={{0,6},{1,7},{2,4},{3,5},{4,2},{5,3},{6,0},{7,1},{8,14},{9,15},{10,... | collective-permute-start | bytes 147464 | tf_op jit(solution)/shard_map/ppermute | solution.py:34
  34.3 1.8 %collective-permute-start.13 = (bf16[48,512]{1,0:T(8,128)(2,1)S(1)}, bf16[48,512]{1,0:T(8,128)(2,1)S(1)}, u32[]{:S(2)}, u32[]{:S(2)}) collective-permute-start(bf16[48,512]{1,0:T(8,128)(2,1)S(1)} %add_convert_fusion), channel_id=1, source_target_pairs={{0,5},{1,4},{2,7},{3,6},{4,1},{5,0},{6,3},{7,2},{8,13},{9,12},{10,... | collective-permute-start | bytes 147464 | tf_op jit(solution)/shard_map/ppermute | solution.py:34
  36.1 2.3 %collective-permute-done.15 = bf16[48,512]{1,0:T(8,128)(2,1)S(1)} collective-permute-done((bf16[48,512]{1,0:T(8,128)(2,1)S(1)}, bf16[48,512]{1,0:T(8,128)(2,1)S(1)}, u32[]{:S(2)}, u32[]{:S(2)}) %collective-permute-start.15) | collective-permute-done | bytes 49184 | tf_op jit(solution)/shard_map/ppermute | solution.py:34
  38.4 1.5 %collective-permute-done.14 = bf16[48,512]{1,0:T(8,128)(2,1)S(1)} collective-permute-done((bf16[48,512]{1,0:T(8,128)(2,1)S(1)}, bf16[48,512]{1,0:T(8,128)(2,1)S(1)}, u32[]{:S(2)}, u32[]{:S(2)}) %collective-permute-start.14) | collective-permute-done | bytes 49184 | tf_op jit(solution)/shard_map/ppermute | solution.py:34
  39.9 0.0 collective-permute-done.13
  39.9 0.2 collective-permute-start.16
  40.1 1.2 %collective-permute-done.16.other = f32[48,512]{1,0:T(8,128)S(1)} collective-permute-done((f32[48,512]{1,0:T(8,128)S(1)}, f32[48,512]{1,0:T(8,128)S(1)}, u32[]{:S(2)}, u32[]{:S(2)}) %collective-permute-start.16) | collective-permute-done | bytes 98336 | tf_op jit(solution)/shard_map/ppermute | solution.py:24
  41.3 1.4 %shard_map.129 = (bf16[64,1024]{1,0:T(8,128)(2,1)}, f32[25,1024]{1,0:T(8,128)}, f32[16,1024]{1,0:T(8,128)}, f32[1,1]{1,0:T(1,128)}) custom-call(f32[48,512]{1,0:T(8,128)S(1)} %add_add_fusion.scaled, f32[48,512]{1,0:T(8,128)S(1)} %collective-permute-done.16.other, bf16[64,512]{1,0:T(8,128)(2,1)S(1)} %get-tuple-element.53.latent_here, ...), custom_call_target="tpu_custom_call" | custom-call | bytes 1048576 | tf_op jit(solution)/shard_map/pallas_call | solution.py:356
  (3 shorter events, 0.1 us)
Async XLA Ops:
  3.3 6.5 %collective-permute-start = (f32[80,128]{1,0:T(8,128)S(1)}, f32[80,128]{1,0:T(8,128)S(1)}, u32[]{:S(2)}, u32[]{:S(2)}) collective-permute-start(f32[80,128]{1,0:T(8,128)S(1)} %get-tuple-element.33), channel_id=1, source_target_pairs={{0,7},{1,6},{2,5},{3,4},{4,3},{5,2},{6,1},{7,0},{8,15},{9,14},{10,... | collective-permute-start | bytes 122888 | tf_op jit(solution)/shard_map/ppermute | solution.py:34
  7.8 4.7 %collective-permute-start.1 = (f32[80,128]{1,0:T(8,128)S(1)}, f32[80,128]{1,0:T(8,128)S(1)}, u32[]{:S(2)}, u32[]{:S(2)}) collective-permute-start(f32[80,128]{1,0:T(8,128)S(1)} %get-tuple-element.34), channel_id=1, source_target_pairs={{0,6},{1,7},{2,4},{3,5},{4,2},{5,3},{6,0},{7,1},{8,14},{9,15},{10,... | collective-permute-start | bytes 122888 | tf_op jit(solution)/shard_map/ppermute | solution.py:34
  7.8 4.7 %collective-permute-start.2 = (f32[80,128]{1,0:T(8,128)S(1)}, f32[80,128]{1,0:T(8,128)S(1)}, u32[]{:S(2)}, u32[]{:S(2)}) collective-permute-start(f32[80,128]{1,0:T(8,128)S(1)} %get-tuple-element.35), channel_id=1, source_target_pairs={{0,5},{1,4},{2,7},{3,6},{4,1},{5,0},{6,3},{7,2},{8,13},{9,12},{10,... | collective-permute-start | bytes 122888 | tf_op jit(solution)/shard_map/ppermute | solution.py:34
  8.8 3.8 %collective-permute-start.3 = (f32[80,128]{1,0:T(8,128)S(1)}, f32[80,128]{1,0:T(8,128)S(1)}, u32[]{:S(2)}, u32[]{:S(2)}) collective-permute-start(f32[80,128]{1,0:T(8,128)S(1)} %get-tuple-element.36), channel_id=1, source_target_pairs={{0,4},{1,5},{2,6},{3,7},{4,0},{5,1},{6,2},{7,3},{8,12},{9,13},{10,... | collective-permute-start | bytes 122888 | tf_op jit(solution)/shard_map/ppermute | solution.py:34
  12.9 3.4 %collective-permute-start.4 = (f32[32,256]{1,0:T(8,128)S(1)}, f32[32,256]{1,0:T(8,128)S(1)}, u32[]{:S(2)}, u32[]{:S(2)}) collective-permute-start(f32[32,256]{1,0:T(8,128)S(1)} %shard_map.121.refs_0_), channel_id=1, source_target_pairs={{0,12},{1,13},{2,14},{3,15},{4,8},{5,9},{6,10},{7,11},{8,4},{9,5},... | collective-permute-start | bytes 98312 | tf_op jit(solution)/shard_map/ppermute | solution.py:34
  14.4 2.2 %collective-permute-start.5 = (f32[32,256]{1,0:T(8,128)S(1)}, f32[32,256]{1,0:T(8,128)S(1)}, u32[]{:S(2)}, u32[]{:S(2)}) collective-permute-start(f32[32,256]{1,0:T(8,128)S(1)} %shard_map.121.refs_0_), channel_id=1, source_target_pairs={{0,4},{4,0},{8,12},{12,8},{1,5},{5,1},{9,13},{13,9},{2,6},{6,2},{1... | collective-permute-start | bytes 98312 | tf_op jit(solution)/shard_map/ppermute | solution.py:24
  16.3 1.2 %collective-permute-start.6 = (f32[32,256]{1,0:T(8,128)S(1)}, f32[32,256]{1,0:T(8,128)S(1)}, u32[]{:S(2)}, u32[]{:S(2)}) collective-permute-start(f32[32,256]{1,0:T(8,128)S(1)} %collective-permute-done.4.refs_3_), channel_id=1, source_target_pairs={{0,4},{4,0},{8,12},{12,8},{1,5},{5,1},{9,13},{13,9},{2,6},{6,2},{1... | collective-permute-start | bytes 98312 | tf_op jit(solution)/shard_map/ppermute | solution.py:24
  17.8 4.3 %collective-permute-start.8 = (bf16[32,256]{1,0:T(8,128)(2,1)S(1)}, bf16[32,256]{1,0:T(8,128)(2,1)S(1)}, u32[]{:S(2)}, u32[]{:S(2)}) collective-permute-start(bf16[32,256]{1,0:T(8,128)(2,1)S(1)} %shard_map.123), channel_id=1, source_target_pairs={{0,4},{1,5},{2,6},{3,7},{4,0},{5,1},{6,2},{7,3},{8,12},{9,13},{10,... | collective-permute-start | bytes 49160 | tf_op jit(solution)/shard_map/ppermute | solution.py:34
  18.2 5.0 %collective-permute-start.7 = (bf16[32,256]{1,0:T(8,128)(2,1)S(1)}, bf16[32,256]{1,0:T(8,128)(2,1)S(1)}, u32[]{:S(2)}, u32[]{:S(2)}) collective-permute-start(bf16[32,256]{1,0:T(8,128)(2,1)S(1)} %shard_map.123), channel_id=1, source_target_pairs={{0,7},{1,6},{2,5},{3,4},{4,3},{5,2},{6,1},{7,0},{8,15},{9,14},{10,... | collective-permute-start | bytes 49160 | tf_op jit(solution)/shard_map/ppermute | solution.py:34
  20.4 3.7 %collective-permute-start.9 = (bf16[32,256]{1,0:T(8,128)(2,1)S(1)}, bf16[32,256]{1,0:T(8,128)(2,1)S(1)}, u32[]{:S(2)}, u32[]{:S(2)}) collective-permute-start(bf16[32,256]{1,0:T(8,128)(2,1)S(1)} %shard_map.123), channel_id=1, source_target_pairs={{0,5},{1,4},{2,7},{3,6},{4,1},{5,0},{6,3},{7,2},{8,13},{9,12},{10,... | collective-permute-start | bytes 49160 | tf_op jit(solution)/shard_map/ppermute | solution.py:34
  20.7 4.1 %collective-permute-start.10 = (bf16[32,256]{1,0:T(8,128)(2,1)S(1)}, bf16[32,256]{1,0:T(8,128)(2,1)S(1)}, u32[]{:S(2)}, u32[]{:S(2)}) collective-permute-start(bf16[32,256]{1,0:T(8,128)(2,1)S(1)} %shard_map.123), channel_id=1, source_target_pairs={{0,6},{1,7},{2,4},{3,5},{4,2},{5,3},{6,0},{7,1},{8,14},{9,15},{10,... | collective-permute-start | bytes 49160 | tf_op jit(solution)/shard_map/ppermute | solution.py:34
  22.1 2.7 %copy-start = (bf16[1,64,1024]{2,1,0:T(8,128)(2,1)S(1)}, bf16[1,64,1024]{2,1,0:T(8,128)(2,1)}, u32[]{:S(2)}) copy-start(bf16[1,64,1024]{2,1,0:T(8,128)(2,1)} %param.9) | copy-start | bytes 393220
  22.1 2.7 %copy-start.1 = (bf16[16,1024]{1,0:T(8,128)(2,1)S(1)}, bf16[16,1024]{1,0:T(8,128)(2,1)}, u32[]{:S(2)}) copy-start(bf16[16,1024]{1,0:T(8,128)(2,1)} %coef.3) | copy-start | bytes 98308
  26.3 1.7 %collective-permute-start.11 = (f32[48,512]{1,0:T(8,128)S(1)}, f32[48,512]{1,0:T(8,128)S(1)}, u32[]{:S(2)}, u32[]{:S(2)}) collective-permute-start(f32[48,512]{1,0:T(8,128)S(1)} %get-tuple-element.51), channel_id=1, source_target_pairs={{0,4},{4,0},{8,12},{12,8},{1,5},{5,1},{9,13},{13,9},{2,6},{6,2},{1... | collective-permute-start | bytes 294920 | tf_op jit(solution)/shard_map/ppermute | solution.py:24
  28.1 3.8 %collective-permute-start.12 = (bf16[48,512]{1,0:T(8,128)(2,1)S(1)}, bf16[48,512]{1,0:T(8,128)(2,1)S(1)}, u32[]{:S(2)}, u32[]{:S(2)}) collective-permute-start(bf16[48,512]{1,0:T(8,128)(2,1)S(1)} %add_convert_fusion.1), channel_id=1, source_target_pairs={{0,12},{1,13},{2,14},{3,15},{4,8},{5,9},{6,10},{7,11},{8,4},{9,5},... | collective-permute-start | bytes 147464 | tf_op jit(solution)/shard_map/ppermute | solution.py:34
  31.9 6.5 %collective-permute-start.15 = (bf16[48,512]{1,0:T(8,128)(2,1)S(1)}, bf16[48,512]{1,0:T(8,128)(2,1)S(1)}, u32[]{:S(2)}, u32[]{:S(2)}) collective-permute-start(bf16[48,512]{1,0:T(8,128)(2,1)S(1)} %add_convert_fusion), channel_id=1, source_target_pairs={{0,3},{1,2},{2,1},{3,0},{4,7},{5,6},{6,5},{7,4},{8,11},{9,10},{10,... | collective-permute-start | bytes 147464 | tf_op jit(solution)/shard_map/ppermute | solution.py:34
  33.7 6.1 %collective-permute-start.14 = (bf16[48,512]{1,0:T(8,128)(2,1)S(1)}, bf16[48,512]{1,0:T(8,128)(2,1)S(1)}, u32[]{:S(2)}, u32[]{:S(2)}) collective-permute-start(bf16[48,512]{1,0:T(8,128)(2,1)S(1)} %add_convert_fusion), channel_id=1, source_target_pairs={{0,6},{1,7},{2,4},{3,5},{4,2},{5,3},{6,0},{7,1},{8,14},{9,15},{10,... | collective-permute-start | bytes 147464 | tf_op jit(solution)/shard_map/ppermute | solution.py:34
  34.3 5.5 %collective-permute-start.13 = (bf16[48,512]{1,0:T(8,128)(2,1)S(1)}, bf16[48,512]{1,0:T(8,128)(2,1)S(1)}, u32[]{:S(2)}, u32[]{:S(2)}) collective-permute-start(bf16[48,512]{1,0:T(8,128)(2,1)S(1)} %add_convert_fusion), channel_id=1, source_target_pairs={{0,5},{1,4},{2,7},{3,6},{4,1},{5,0},{6,3},{7,2},{8,13},{9,12},{10,... | collective-permute-start | bytes 147464 | tf_op jit(solution)/shard_map/ppermute | solution.py:34
  39.9 1.4 %collective-permute-start.16 = (f32[48,512]{1,0:T(8,128)S(1)}, f32[48,512]{1,0:T(8,128)S(1)}, u32[]{:S(2)}, u32[]{:S(2)}) collective-permute-start(f32[48,512]{1,0:T(8,128)S(1)} %add_add_fusion.scaled), channel_id=1, source_target_pairs={{0,4},{4,0},{8,12},{12,8},{1,5},{5,1},{9,13},{13,9},{2,6},{6,2},{1... | collective-permute-start | bytes 294920 | tf_op jit(solution)/shard_map/ppermute | solution.py:24

commit v8 on v7

--- a/solution.py
+++ b/solution.py
@@ -324,29 +324,41 @@
     mean_loss[...] = jnp.sum(losses, axis=1, keepdims=True) * scale
 
 
-def write_kernel(members, bands, variables, scaled, other, latent_here, latent_there, mean_loss, *refs):
+def write_half(side, summed, proj_out, coef_out, proj, leaves):
+    half = summed.shape[1]
+    spot = pl.ds(pl.multiple_of(side * half, half), half)
+    proj[...] = summed[0 : proj.shape[0], :]
+    moves = [
+        pltpu.make_async_copy(summed.at[summed.shape[0] - coef_out.shape[0] :, :], coef_out.at[:, spot], leaves.at[0]),
+        pltpu.make_async_copy(proj, proj_out.at[:, spot], leaves.at[1]),
+    ]
+    for move in moves:
+        move.start()
+    return moves
+
+
+def write_kernel(members, bands, summed, latent_here, latent_there, mean_loss, *refs):
     latent_out, proj_out, coef_out, loss_out, proj, leaves = refs
     side = half_here(members, bands)
-    half = scaled.shape[1]
-    first = scaled.shape[0] - coef_out.shape[0]
+    moves = write_half(side, summed, proj_out, coef_out, proj, leaves)
+    half = latent_here.shape[1]
     here = pl.ds(pl.multiple_of(side * half, half), half)
     there = pl.ds(pl.multiple_of((1 - side) * half, half), half)
-    moves = [
-        (scaled.at[first:, :], coef_out.at[:, here]),
-        (other.at[first:, :], coef_out.at[:, there]),
+    more = [
         (latent_here, latent_out.at[:, here]),
         (latent_there, latent_out.at[:, there]),
         (mean_loss, loss_out),
-        (proj, proj_out),
     ]
-    moves = [pltpu.make_async_copy(*move, leaves.at[n]) for n, move in enumerate(moves)]
-    for move in moves[:-1]:
-        move.start()
-    mine, theirs = scaled[0:variables, :], other[0:variables, :]
-    proj[:, 0:half] = jnp.where(side == 0, mine, theirs)
-    proj[:, half:] = jnp.where(side == 0, theirs, mine)
-    moves[-1].start()
+    for n, move in enumerate(more):
+        moves.append(pltpu.make_async_copy(*move, leaves.at[n + 2]))
+        moves[-1].start()
     for move in moves:
+        move.wait()
+
+
+def write_rest_kernel(members, bands, proj_in, coef_in, summed, proj_out, coef_out, proj, leaves):
+    side = half_here(members, bands)
+    for move in write_half(1 - side, summed, proj_out, coef_out, proj, leaves):
         move.wait()
 
 
@@ -504,17 +516,26 @@
         step *= 4
     other = swap(total, "member", 1)
     latent_out, proj_grad, coef_grad, loss_out = call(
-        functools.partial(write_kernel, members, bands, variables),
+        functools.partial(write_kernel, members, bands),
         [
             shape(rows, hidden, dtype=BF16),
             shape(variables, hidden),
             shape(table, hidden),
             shape(1, 1),
         ],
-        (total, other, latent_here, latent_there, mean_loss),
-        [pltpu.VMEM((variables, hidden), F32), pltpu.SemaphoreType.DMA((6,))],
+        (total, latent_here, latent_there, mean_loss),
+        [pltpu.VMEM((variables, half), F32), pltpu.SemaphoreType.DMA((5,))],
         sink=HBM,
     )
+    proj_grad, coef_grad = pl.pallas_call(
+        functools.partial(write_rest_kernel, members, bands),
+        out_shape=[shape(variables, hidden), shape(table, hidden)],
+        in_specs=[HBM, HBM, VMEM],
+        out_specs=[HBM, HBM],
+        scratch_shapes=[pltpu.VMEM((variables, half), F32), pltpu.SemaphoreType.DMA((2,))],
+        input_output_aliases={0: 0, 1: 1},
+        compiler_params=PARAMS,
+    )(proj_grad, coef_grad, other)
     return (latent_out[None], proj_grad, coef_grad, loss_out.reshape(1))
 
 

time: 42.8 us -> 42.4 us (level)
  waiting for transfers between devices: 12.6 us -> 11.3 us
  Pallas kernels: 11.5 us -> 12.2 us
    ppermute x4, waiting for transfers between devices: 2.11 us -> 0.92 us  [swap(): return lax.ppermute(shard, axis, [(i, i ^ mask) for i in range(peers)])]
    pallas_call x0 -> x1, Pallas kernels: none -> 0.67 us  [local(): pl.pallas_call(functools.partial(write_rest_kernel, members, bands), out_...]
  transfers between devices with their start and end apart: 17 -> 17, of which waited for: 9 -> 8; matrix products, arithmetic and copies ran while one was open for 0% -> 0% of each run, Pallas kernels for 12% -> 16%
where the time goes in v8:
time: 42.4 us; the launch traced here: 42.2 us
  starting transfers between devices  17.8 us (42%)
  Pallas kernels  12.2 us (29%)
  waiting for transfers between devices  11.3 us (27%)
  between operations  0.74 us (2%)
    ppermute x13, starting transfers between devices, cross(): return lax.ppermute(shard, ('member', 'band'), pairs)  16.7 us
    pallas_call x10, Pallas kernels, call(): pl.pallas_call(kernel, out_shape=outs, in_specs=[source] * len(operands),...  11.6 us
    ppermute x13, waiting for transfers between devices, cross(): return lax.ppermute(shard, ('member', 'band'), pairs)  10.4 us
    ppermute x4, starting transfers between devices, swap(): return lax.ppermute(shard, axis, [(i, i ^ mask) for i in range(peers)])  1.11 us
    ppermute x4, waiting for transfers between devices, swap(): return lax.ppermute(shard, axis, [(i, i ^ mask) for i in range(peers)])  0.92 us
  transfers between devices with their start and end apart: 17, of which 8 were waited for; matrix products, arithmetic and copies ran while one was open for 0% of the time, Pallas kernels for 16%

profile of v8, /device:TPU:0, one launch (start us, length us, event | category | flops | bytes accessed | tf_op | source)
XLA Modules:
  0.0 42.2 jit_solution(2147393788940229184)
XLA Ops:
  0.6 2.6 %shard_map.120 = (f32[80,128]{1,0:T(8,128)S(1)}, f32[80,128]{1,0:T(8,128)S(1)}, f32[80,128]{1,0:T(8,128)S(1)}, f32[80,128]{1,0:T(8,128)S(1)}, bf16[25,1024]{1,0:...) custom-call(bf16[64,1024]{1,0:T(8,128)(2,1)} %bitcast.5, ...), custom_call_target="tpu_custom_call" | custom-call | bytes 1048576 | tf_op jit(solution)/shard_map/pallas_call | solution.py:368
  3.3 4.6 %collective-permute-start = (f32[80,128]{1,0:T(8,128)S(1)}, f32[80,128]{1,0:T(8,128)S(1)}, u32[]{:S(2)}, u32[]{:S(2)}) collective-permute-start(f32[80,128]{1,0:T(8,128)S(1)} %get-tuple-element.35), channel_id=1, source_target_pairs={{0,7},{1,6},{2,5},{3,4},{4,3},{5,2},{6,1},{7,0},{8,15},{9,14},{10,... | collective-permute-start | bytes 122888 | tf_op jit(solution)/shard_map/ppermute | solution.py:34
  7.8 0.0 collective-permute-start.1
  7.8 0.9 %collective-permute-start.2 = (f32[80,128]{1,0:T(8,128)S(1)}, f32[80,128]{1,0:T(8,128)S(1)}, u32[]{:S(2)}, u32[]{:S(2)}) collective-permute-start(f32[80,128]{1,0:T(8,128)S(1)} %get-tuple-element.37), channel_id=1, source_target_pairs={{0,5},{1,4},{2,7},{3,6},{4,1},{5,0},{6,3},{7,2},{8,13},{9,12},{10,... | collective-permute-start | bytes 122888 | tf_op jit(solution)/shard_map/ppermute | solution.py:34
  8.8 0.0 collective-permute-start.3
  8.8 1.0 %collective-permute-done.refs_0_ = f32[80,128]{1,0:T(8,128)S(1)} collective-permute-done((f32[80,128]{1,0:T(8,128)S(1)}, f32[80,128]{1,0:T(8,128)S(1)}, u32[]{:S(2)}, u32[]{:S(2)}) %collective-permute-start) | collective-permute-done | bytes 40992 | tf_op jit(solution)/shard_map/ppermute | solution.py:34
  9.8 2.8 %collective-permute-done.1.refs_1_ = f32[80,128]{1,0:T(8,128)S(1)} collective-permute-done((f32[80,128]{1,0:T(8,128)S(1)}, f32[80,128]{1,0:T(8,128)S(1)}, u32[]{:S(2)}, u32[]{:S(2)}) %collective-permute-start.1) | collective-permute-done | bytes 40992 | tf_op jit(solution)/shard_map/ppermute | solution.py:34
  12.5 0.0 collective-permute-done.2.refs_2_
  12.5 0.0 collective-permute-done.3.refs_3_
  12.6 0.4 shard_map.121.refs_0_
  12.9 1.4 %collective-permute-start.4 = (f32[32,256]{1,0:T(8,128)S(1)}, f32[32,256]{1,0:T(8,128)S(1)}, u32[]{:S(2)}, u32[]{:S(2)}) collective-permute-start(f32[32,256]{1,0:T(8,128)S(1)} %shard_map.121.refs_0_), channel_id=1, source_target_pairs={{0,12},{1,13},{2,14},{3,15},{4,8},{5,9},{6,10},{7,11},{8,4},{9,5},... | collective-permute-start | bytes 98312 | tf_op jit(solution)/shard_map/ppermute | solution.py:34
  14.4 0.2 collective-permute-start.5
  14.6 1.3 %shard_map.122.counts = bf16[1024,1024]{1,0:T(8,128)(2,1)S(1)} custom-call(s32[4,1,384]{2,1,0:T(1,128)S(1)} %get-tuple-element.40.pair_ids, f32[80,128]{1,0:T(8,128)S(1)} %collective-permute-done.refs_0_, f32[80,128]{1,0:T(8,128)S(1)} %collective-permute-done.1.refs_1_, f32[80,128]{1,0:T(8,128)S(1)} %collective-permute-done.2.refs_2_, ...), custom_call_target="tpu_custom_call" | custom-call | flops 805306368 | bytes 1048576 | tf_op jit(solution)/shard_map/pallas_call | solution.py:368
  15.9 0.4 %collective-permute-done.4.refs_3_ = f32[32,256]{1,0:T(8,128)S(1)} collective-permute-done((f32[32,256]{1,0:T(8,128)S(1)}, f32[32,256]{1,0:T(8,128)S(1)}, u32[]{:S(2)}, u32[]{:S(2)}) %collective-permute-start.4) | collective-permute-done | bytes 32800 | tf_op jit(solution)/shard_map/ppermute | solution.py:34
  16.3 0.3 collective-permute-start.6
  16.6 0.0 collective-permute-done.5.refs_1_
  16.6 0.9 %collective-permute-done.6.refs_2_ = f32[32,256]{1,0:T(8,128)S(1)} collective-permute-done((f32[32,256]{1,0:T(8,128)S(1)}, f32[32,256]{1,0:T(8,128)S(1)}, u32[]{:S(2)}, u32[]{:S(2)}) %collective-permute-start.6) | collective-permute-done | bytes 32800 | tf_op jit(solution)/shard_map/ppermute | solution.py:24
  17.5 0.3 shard_map.123
  17.8 0.4 collective-permute-start.8
  18.2 2.2 %collective-permute-start.7 = (bf16[32,256]{1,0:T(8,128)(2,1)S(1)}, bf16[32,256]{1,0:T(8,128)(2,1)S(1)}, u32[]{:S(2)}, u32[]{:S(2)}) collective-permute-start(bf16[32,256]{1,0:T(8,128)(2,1)S(1)} %shard_map.123), channel_id=1, source_target_pairs={{0,7},{1,6},{2,5},{3,4},{4,3},{5,2},{6,1},{7,0},{8,15},{9,14},{10,... | collective-permute-start | bytes 49160 | tf_op jit(solution)/shard_map/ppermute | solution.py:34
  20.4 0.3 collective-permute-start.9
  20.7 1.4 %collective-permute-start.10 = (bf16[32,256]{1,0:T(8,128)(2,1)S(1)}, bf16[32,256]{1,0:T(8,128)(2,1)S(1)}, u32[]{:S(2)}, u32[]{:S(2)}) collective-permute-start(bf16[32,256]{1,0:T(8,128)(2,1)S(1)} %shard_map.123), channel_id=1, source_target_pairs={{0,6},{1,7},{2,4},{3,5},{4,2},{5,3},{6,0},{7,1},{8,14},{9,15},{10,... | collective-permute-start | bytes 49160 | tf_op jit(solution)/shard_map/ppermute | solution.py:34
  22.1 0.0 collective-permute-done.8.grad.refs_2_.refs_0_
  22.1 0.0 copy-start
  22.1 0.0 copy-start.1
  22.1 1.0 %shard_map.124 = (f32[32,1024]{1,0:T(8,128)S(1)}, f32[1024,1024]{1,0:T(8,128)S(1)}) custom-call(bf16[32,1024]{1,0:T(8,128)(2,1)S(1)} %get-tuple-element.34.proj, bf16[1024,1024]{1,0:T(8,128)(2,1)S(1)} %shard_map.122.counts, bf16[32,256]{1,0:T(8,128)(2,1)S(1)} %collective-permute-done.8.grad.refs_2_.refs_0_), custom_call_target="tpu_custom_call" | custom-call | flops 536870912 | bytes 1048576 | tf_op jit(solution)/shard_map/pallas_call | solution.py:368
  23.1 0.0 collective-permute-done.7.grad.refs_5_.refs_3_
  23.2 1.0 %shard_map.125 = (f32[32,1024]{1,0:T(8,128)S(1)}, f32[1024,1024]{1,0:T(8,128)S(1)}) custom-call(bf16[32,1024]{1,0:T(8,128)(2,1)S(1)} %get-tuple-element.34.proj, bf16[1024,1024]{1,0:T(8,128)(2,1)S(1)} %shard_map.122.counts, bf16[32,256]{1,0:T(8,128)(2,1)S(1)} %collective-permute-done.7.grad.refs_5_.refs_3_, f32[32,1024]{1,0:T(8,128)S(1)} %get-tuple-element.47.refs_0_, ...), custom_call_target="tpu_custom_call" | custom-call | flops 536870912 | bytes 1048576 | tf_op jit(solution)/shard_map/pallas_call | solution.py:368
  24.2 0.0 collective-permute-done.9.refs_3_.refs_1_
  24.2 0.6 %collective-permute-done.10.refs_4_.refs_2_ = bf16[32,256]{1,0:T(8,128)(2,1)S(1)} collective-permute-done((bf16[32,256]{1,0:T(8,128)(2,1)S(1)}, bf16[32,256]{1,0:T(8,128)(2,1)S(1)}, u32[]{:S(2)}, u32[]{:S(2)}) %collective-permute-start.10) | collective-permute-done | bytes 16416 | tf_op jit(solution)/shard_map/ppermute | solution.py:34
  24.8 0.0 copy-done
  24.8 0.0 copy-done.1
  24.8 1.5 %shard_map.126 = (bf16[64,512]{1,0:T(8,128)(2,1)S(1)}, f32[48,512]{1,0:T(8,128)S(1)}, f32[32,1024]{1,0:T(8,128)S(1)}) custom-call(bf16[64,1024]{1,0:T(8,128)(2,1)S(1)} %bitcast.6, bf16[16,1024]{1,0:T(8,128)(2,1)S(1)} %copy-done.1, bf16[32,1024]{1,0:T(8,128)(2,1)S(1)} %get-tuple-element.34.proj, bf16[1024,1024]{1,0:T(8,128)(2,1)S(1)} %shard_map.122.counts, ...), custom_call_target="tpu_custom_call" | custom-call | flops 1073741824 | bytes 1048576 | tf_op jit(solution)/shard_map/pallas_call | solution.py:368
  26.3 0.4 collective-permute-start.11
  26.8 1.3 %shard_map.127 = (bf16[64,512]{1,0:T(8,128)(2,1)S(1)}, f32[48,512]{1,0:T(8,128)S(1)}) custom-call(bf16[64,1024]{1,0:T(8,128)(2,1)S(1)} %bitcast.7, bf16[16,1024]{1,0:T(8,128)(2,1)S(1)} %copy-done.1, bf16[32,1024]{1,0:T(8,128)(2,1)S(1)} %get-tuple-element.34.proj, bf16[1024,1024]{1,0:T(8,128)(2,1)S(1)} %shard_map.122.counts, ...), custom_call_target="tpu_custom_call" | custom-call | flops 1073741824 | bytes 1048576 | tf_op jit(solution)/shard_map/pallas_call | solution.py:368
  28.0 0.0 collective-permute-done.11
  28.1 1.3 %collective-permute-start.12 = (bf16[48,512]{1,0:T(8,128)(2,1)S(1)}, bf16[48,512]{1,0:T(8,128)(2,1)S(1)}, u32[]{:S(2)}, u32[]{:S(2)}) collective-permute-start(bf16[48,512]{1,0:T(8,128)(2,1)S(1)} %add_convert_fusion.1), channel_id=1, source_target_pairs={{0,12},{1,13},{2,14},{3,15},{4,8},{5,9},{6,10},{7,11},{8,4},{9,5},... | collective-permute-start | bytes 147464 | tf_op jit(solution)/shard_map/ppermute | solution.py:34
  29.4 0.8 %shard_map.128.mean_loss = f32[1,1]{1,0:T(1,128)} custom-call(bf16[32,256]{1,0:T(8,128)(2,1)S(1)} %collective-permute-done.8.grad.refs_2_.refs_0_, bf16[32,256]{1,0:T(8,128)(2,1)S(1)} %collective-permute-done.9.refs_3_.refs_1_, bf16[32,256]{1,0:T(8,128)(2,1)S(1)} %collective-permute-done.10.refs_4_.refs_2_, ...), custom_call_target="tpu_custom_call" | custom-call | bytes 1048576 | tf_op jit(solution)/shard_map/pallas_call | solution.py:368
  30.1 1.8 %collective-permute-done.12 = bf16[48,512]{1,0:T(8,128)(2,1)S(1)} collective-permute-done((bf16[48,512]{1,0:T(8,128)(2,1)S(1)}, bf16[48,512]{1,0:T(8,128)(2,1)S(1)}, u32[]{:S(2)}, u32[]{:S(2)}) %collective-permute-start.12) | collective-permute-done | bytes 49184 | tf_op jit(solution)/shard_map/ppermute | solution.py:34
  31.9 1.8 %collective-permute-start.15 = (bf16[48,512]{1,0:T(8,128)(2,1)S(1)}, bf16[48,512]{1,0:T(8,128)(2,1)S(1)}, u32[]{:S(2)}, u32[]{:S(2)}) collective-permute-start(bf16[48,512]{1,0:T(8,128)(2,1)S(1)} %add_convert_fusion), channel_id=1, source_target_pairs={{0,3},{1,2},{2,1},{3,0},{4,7},{5,6},{6,5},{7,4},{8,11},{9,10},{10,... | collective-permute-start | bytes 147464 | tf_op jit(solution)/shard_map/ppermute | solution.py:34
  33.7 0.6 %collective-permute-start.14 = (bf16[48,512]{1,0:T(8,128)(2,1)S(1)}, bf16[48,512]{1,0:T(8,128)(2,1)S(1)}, u32[]{:S(2)}, u32[]{:S(2)}) collective-permute-start(bf16[48,512]{1,0:T(8,128)(2,1)S(1)} %add_convert_fusion), channel_id=1, source_target_pairs={{0,6},{1,7},{2,4},{3,5},{4,2},{5,3},{6,0},{7,1},{8,14},{9,15},{10,... | collective-permute-start | bytes 147464 | tf_op jit(solution)/shard_map/ppermute | solution.py:34
  34.3 1.8 %collective-permute-start.13 = (bf16[48,512]{1,0:T(8,128)(2,1)S(1)}, bf16[48,512]{1,0:T(8,128)(2,1)S(1)}, u32[]{:S(2)}, u32[]{:S(2)}) collective-permute-start(bf16[48,512]{1,0:T(8,128)(2,1)S(1)} %add_convert_fusion), channel_id=1, source_target_pairs={{0,5},{1,4},{2,7},{3,6},{4,1},{5,0},{6,3},{7,2},{8,13},{9,12},{10,... | collective-permute-start | bytes 147464 | tf_op jit(solution)/shard_map/ppermute | solution.py:34
  36.1 2.3 %collective-permute-done.15 = bf16[48,512]{1,0:T(8,128)(2,1)S(1)} collective-permute-done((bf16[48,512]{1,0:T(8,128)(2,1)S(1)}, bf16[48,512]{1,0:T(8,128)(2,1)S(1)}, u32[]{:S(2)}, u32[]{:S(2)}) %collective-permute-start.15) | collective-permute-done | bytes 49184 | tf_op jit(solution)/shard_map/ppermute | solution.py:34
  38.4 1.5 %collective-permute-done.14 = bf16[48,512]{1,0:T(8,128)(2,1)S(1)} collective-permute-done((bf16[48,512]{1,0:T(8,128)(2,1)S(1)}, bf16[48,512]{1,0:T(8,128)(2,1)S(1)}, u32[]{:S(2)}, u32[]{:S(2)}) %collective-permute-start.14) | collective-permute-done | bytes 49184 | tf_op jit(solution)/shard_map/ppermute | solution.py:34
  39.9 0.0 collective-permute-done.13
  39.9 0.2 collective-permute-start.16
  40.1 1.4 %shard_map.129 = (bf16[64,1024]{1,0:T(8,128)(2,1)}, f32[25,1024]{1,0:T(8,128)}, f32[16,1024]{1,0:T(8,128)}, f32[1,1]{1,0:T(1,128)}) custom-call(f32[48,512]{1,0:T(8,128)S(1)} %add_add_fusion.summed, bf16[64,512]{1,0:T(8,128)(2,1)S(1)} %get-tuple-element.55.latent_here, bf16[64,512]{1,0:T(8,128)(2,1)S(1)} %get-tuple-element.56.latent_there, ...), custom_call_target="tpu_custom_call" | custom-call | bytes 1048576 | tf_op jit(solution)/shard_map/pallas_call | solution.py:368
  41.5 0.0 collective-permute-done.16.summed
  41.5 0.7 %shard_map.130 = (f32[25,1024]{1,0:T(8,128)}, f32[16,1024]{1,0:T(8,128)}) custom-call(f32[25,1024]{1,0:T(8,128)} %get-tuple-element.59.proj_in, f32[16,1024]{1,0:T(8,128)} %get-tuple-element.60.coef_in, f32[48,512]{1,0:T(8,128)S(1)} %collective-permute-done.16.summed), custom_call_target="tpu_custom_call", output_to_operand_aliasing={{0}: (0, {}), {1}: (1, {})} | custom-call | tf_op jit(solution)/shard_map/pallas_call | solution.py:530
  (3 shorter events, 0.1 us)
Async XLA Ops:
  3.3 6.5 %collective-permute-start = (f32[80,128]{1,0:T(8,128)S(1)}, f32[80,128]{1,0:T(8,128)S(1)}, u32[]{:S(2)}, u32[]{:S(2)}) collective-permute-start(f32[80,128]{1,0:T(8,128)S(1)} %get-tuple-element.35), channel_id=1, source_target_pairs={{0,7},{1,6},{2,5},{3,4},{4,3},{5,2},{6,1},{7,0},{8,15},{9,14},{10,... | collective-permute-start | bytes 122888 | tf_op jit(solution)/shard_map/ppermute | solution.py:34
  7.8 4.7 %collective-permute-start.1 = (f32[80,128]{1,0:T(8,128)S(1)}, f32[80,128]{1,0:T(8,128)S(1)}, u32[]{:S(2)}, u32[]{:S(2)}) collective-permute-start(f32[80,128]{1,0:T(8,128)S(1)} %get-tuple-element.36), channel_id=1, source_target_pairs={{0,6},{1,7},{2,4},{3,5},{4,2},{5,3},{6,0},{7,1},{8,14},{9,15},{10,... | collective-permute-start | bytes 122888 | tf_op jit(solution)/shard_map/ppermute | solution.py:34
  7.8 4.7 %collective-permute-start.2 = (f32[80,128]{1,0:T(8,128)S(1)}, f32[80,128]{1,0:T(8,128)S(1)}, u32[]{:S(2)}, u32[]{:S(2)}) collective-permute-start(f32[80,128]{1,0:T(8,128)S(1)} %get-tuple-element.37), channel_id=1, source_target_pairs={{0,5},{1,4},{2,7},{3,6},{4,1},{5,0},{6,3},{7,2},{8,13},{9,12},{10,... | collective-permute-start | bytes 122888 | tf_op jit(solution)/shard_map/ppermute | solution.py:34
  8.8 3.8 %collective-permute-start.3 = (f32[80,128]{1,0:T(8,128)S(1)}, f32[80,128]{1,0:T(8,128)S(1)}, u32[]{:S(2)}, u32[]{:S(2)}) collective-permute-start(f32[80,128]{1,0:T(8,128)S(1)} %get-tuple-element.38), channel_id=1, source_target_pairs={{0,4},{1,5},{2,6},{3,7},{4,0},{5,1},{6,2},{7,3},{8,12},{9,13},{10,... | collective-permute-start | bytes 122888 | tf_op jit(solution)/shard_map/ppermute | solution.py:34
  12.9 3.4 %collective-permute-start.4 = (f32[32,256]{1,0:T(8,128)S(1)}, f32[32,256]{1,0:T(8,128)S(1)}, u32[]{:S(2)}, u32[]{:S(2)}) collective-permute-start(f32[32,256]{1,0:T(8,128)S(1)} %shard_map.121.refs_0_), channel_id=1, source_target_pairs={{0,12},{1,13},{2,14},{3,15},{4,8},{5,9},{6,10},{7,11},{8,4},{9,5},... | collective-permute-start | bytes 98312 | tf_op jit(solution)/shard_map/ppermute | solution.py:34
  14.4 2.2 %collective-permute-start.5 = (f32[32,256]{1,0:T(8,128)S(1)}, f32[32,256]{1,0:T(8,128)S(1)}, u32[]{:S(2)}, u32[]{:S(2)}) collective-permute-start(f32[32,256]{1,0:T(8,128)S(1)} %shard_map.121.refs_0_), channel_id=1, source_target_pairs={{0,4},{4,0},{8,12},{12,8},{1,5},{5,1},{9,13},{13,9},{2,6},{6,2},{1... | collective-permute-start | bytes 98312 | tf_op jit(solution)/shard_map/ppermute | solution.py:24
  16.3 1.2 %collective-permute-start.6 = (f32[32,256]{1,0:T(8,128)S(1)}, f32[32,256]{1,0:T(8,128)S(1)}, u32[]{:S(2)}, u32[]{:S(2)}) collective-permute-start(f32[32,256]{1,0:T(8,128)S(1)} %collective-permute-done.4.refs_3_), channel_id=1, source_target_pairs={{0,4},{4,0},{8,12},{12,8},{1,5},{5,1},{9,13},{13,9},{2,6},{6,2},{1... | collective-permute-start | bytes 98312 | tf_op jit(solution)/shard_map/ppermute | solution.py:24
  17.8 4.3 %collective-permute-start.8 = (bf16[32,256]{1,0:T(8,128)(2,1)S(1)}, bf16[32,256]{1,0:T(8,128)(2,1)S(1)}, u32[]{:S(2)}, u32[]{:S(2)}) collective-permute-start(bf16[32,256]{1,0:T(8,128)(2,1)S(1)} %shard_map.123), channel_id=1, source_target_pairs={{0,4},{1,5},{2,6},{3,7},{4,0},{5,1},{6,2},{7,3},{8,12},{9,13},{10,... | collective-permute-start | bytes 49160 | tf_op jit(solution)/shard_map/ppermute | solution.py:34
  18.2 5.0 %collective-permute-start.7 = (bf16[32,256]{1,0:T(8,128)(2,1)S(1)}, bf16[32,256]{1,0:T(8,128)(2,1)S(1)}, u32[]{:S(2)}, u32[]{:S(2)}) collective-permute-start(bf16[32,256]{1,0:T(8,128)(2,1)S(1)} %shard_map.123), channel_id=1, source_target_pairs={{0,7},{1,6},{2,5},{3,4},{4,3},{5,2},{6,1},{7,0},{8,15},{9,14},{10,... | collective-permute-start | bytes 49160 | tf_op jit(solution)/shard_map/ppermute | solution.py:34
  20.4 3.7 %collective-permute-start.9 = (bf16[32,256]{1,0:T(8,128)(2,1)S(1)}, bf16[32,256]{1,0:T(8,128)(2,1)S(1)}, u32[]{:S(2)}, u32[]{:S(2)}) collective-permute-start(bf16[32,256]{1,0:T(8,128)(2,1)S(1)} %shard_map.123), channel_id=1, source_target_pairs={{0,5},{1,4},{2,7},{3,6},{4,1},{5,0},{6,3},{7,2},{8,13},{9,12},{10,... | collective-permute-start | bytes 49160 | tf_op jit(solution)/shard_map/ppermute | solution.py:34
  20.7 4.1 %collective-permute-start.10 = (bf16[32,256]{1,0:T(8,128)(2,1)S(1)}, bf16[32,256]{1,0:T(8,128)(2,1)S(1)}, u32[]{:S(2)}, u32[]{:S(2)}) collective-permute-start(bf16[32,256]{1,0:T(8,128)(2,1)S(1)} %shard_map.123), channel_id=1, source_target_pairs={{0,6},{1,7},{2,4},{3,5},{4,2},{5,3},{6,0},{7,1},{8,14},{9,15},{10,... | collective-permute-start | bytes 49160 | tf_op jit(solution)/shard_map/ppermute | solution.py:34
  22.1 2.7 %copy-start = (bf16[1,64,1024]{2,1,0:T(8,128)(2,1)S(1)}, bf16[1,64,1024]{2,1,0:T(8,128)(2,1)}, u32[]{:S(2)}) copy-start(bf16[1,64,1024]{2,1,0:T(8,128)(2,1)} %param.9) | copy-start | bytes 393220
  22.1 2.7 %copy-start.1 = (bf16[16,1024]{1,0:T(8,128)(2,1)S(1)}, bf16[16,1024]{1,0:T(8,128)(2,1)}, u32[]{:S(2)}) copy-start(bf16[16,1024]{1,0:T(8,128)(2,1)} %coef.3) | copy-start | bytes 98308
  26.3 1.7 %collective-permute-start.11 = (f32[48,512]{1,0:T(8,128)S(1)}, f32[48,512]{1,0:T(8,128)S(1)}, u32[]{:S(2)}, u32[]{:S(2)}) collective-permute-start(f32[48,512]{1,0:T(8,128)S(1)} %get-tuple-element.53), channel_id=1, source_target_pairs={{0,4},{4,0},{8,12},{12,8},{1,5},{5,1},{9,13},{13,9},{2,6},{6,2},{1... | collective-permute-start | bytes 294920 | tf_op jit(solution)/shard_map/ppermute | solution.py:24
  28.1 3.8 %collective-permute-start.12 = (bf16[48,512]{1,0:T(8,128)(2,1)S(1)}, bf16[48,512]{1,0:T(8,128)(2,1)S(1)}, u32[]{:S(2)}, u32[]{:S(2)}) collective-permute-start(bf16[48,512]{1,0:T(8,128)(2,1)S(1)} %add_convert_fusion.1), channel_id=1, source_target_pairs={{0,12},{1,13},{2,14},{3,15},{4,8},{5,9},{6,10},{7,11},{8,4},{9,5},... | collective-permute-start | bytes 147464 | tf_op jit(solution)/shard_map/ppermute | solution.py:34
  31.9 6.5 %collective-permute-start.15 = (bf16[48,512]{1,0:T(8,128)(2,1)S(1)}, bf16[48,512]{1,0:T(8,128)(2,1)S(1)}, u32[]{:S(2)}, u32[]{:S(2)}) collective-permute-start(bf16[48,512]{1,0:T(8,128)(2,1)S(1)} %add_convert_fusion), channel_id=1, source_target_pairs={{0,3},{1,2},{2,1},{3,0},{4,7},{5,6},{6,5},{7,4},{8,11},{9,10},{10,... | collective-permute-start | bytes 147464 | tf_op jit(solution)/shard_map/ppermute | solution.py:34
  33.7 6.1 %collective-permute-start.14 = (bf16[48,512]{1,0:T(8,128)(2,1)S(1)}, bf16[48,512]{1,0:T(8,128)(2,1)S(1)}, u32[]{:S(2)}, u32[]{:S(2)}) collective-permute-start(bf16[48,512]{1,0:T(8,128)(2,1)S(1)} %add_convert_fusion), channel_id=1, source_target_pairs={{0,6},{1,7},{2,4},{3,5},{4,2},{5,3},{6,0},{7,1},{8,14},{9,15},{10,... | collective-permute-start | bytes 147464 | tf_op jit(solution)/shard_map/ppermute | solution.py:34
  34.3 5.5 %collective-permute-start.13 = (bf16[48,512]{1,0:T(8,128)(2,1)S(1)}, bf16[48,512]{1,0:T(8,128)(2,1)S(1)}, u32[]{:S(2)}, u32[]{:S(2)}) collective-permute-start(bf16[48,512]{1,0:T(8,128)(2,1)S(1)} %add_convert_fusion), channel_id=1, source_target_pairs={{0,5},{1,4},{2,7},{3,6},{4,1},{5,0},{6,3},{7,2},{8,13},{9,12},{10,... | collective-permute-start | bytes 147464 | tf_op jit(solution)/shard_map/ppermute | solution.py:34
  39.9 1.6 %collective-permute-start.16 = (f32[48,512]{1,0:T(8,128)S(1)}, f32[48,512]{1,0:T(8,128)S(1)}, u32[]{:S(2)}, u32[]{:S(2)}) collective-permute-start(f32[48,512]{1,0:T(8,128)S(1)} %add_add_fusion.summed), channel_id=1, source_target_pairs={{0,4},{4,0},{8,12},{12,8},{1,5},{5,1},{9,13},{13,9},{2,6},{6,2},{1... | collective-permute-start | bytes 294920 | tf_op jit(solution)/shard_map/ppermute | solution.py:24

commit v9 on v8

--- a/solution.py
+++ b/solution.py
@@ -312,8 +312,18 @@
         latent_grad[:, h : h + step] = into_latent.astype(BF16)
 
 
-def loss_kernel(variables, scale, *refs):
-    *grads, mean_loss = refs
+def loss_kernel(members, variables, scale, latent_here, latent_there, *refs):
+    *grads, mean_loss, latent_out, leaves = refs
+    side = half_here(members, len(grads))
+    half = latent_here.shape[1]
+    here = pl.ds(pl.multiple_of(side * half, half), half)
+    there = pl.ds(pl.multiple_of((1 - side) * half, half), half)
+    moves = [
+        pltpu.make_async_copy(latent_here, latent_out.at[:, here], leaves.at[0]),
+        pltpu.make_async_copy(latent_there, latent_out.at[:, there], leaves.at[1]),
+    ]
+    for move in moves:
+        move.start()
     band = lax.axis_index("band")
     lane = lax.broadcasted_iota(jnp.int32, (1, 128), 1)
     losses = jnp.zeros((1, 128), F32)
@@ -322,6 +332,8 @@
         loss = jnp.sum(arrived[variables : variables + 1, 0:128], axis=1, keepdims=True)
         losses = losses + jnp.where(lane == lax.bitwise_xor(band, i), loss, 0.0)
     mean_loss[...] = jnp.sum(losses, axis=1, keepdims=True) * scale
+    for move in moves:
+        move.wait()
 
 
 def write_half(side, summed, proj_out, coef_out, proj, leaves):
@@ -337,21 +349,12 @@
     return moves
 
 
-def write_kernel(members, bands, summed, latent_here, latent_there, mean_loss, *refs):
-    latent_out, proj_out, coef_out, loss_out, proj, leaves = refs
+def write_kernel(members, bands, summed, mean_loss, *refs):
+    proj_out, coef_out, loss_out, proj, leaves = refs
     side = half_here(members, bands)
     moves = write_half(side, summed, proj_out, coef_out, proj, leaves)
-    half = latent_here.shape[1]
-    here = pl.ds(pl.multiple_of(side * half, half), half)
-    there = pl.ds(pl.multiple_of((1 - side) * half, half), half)
-    more = [
-        (latent_here, latent_out.at[:, here]),
-        (latent_there, latent_out.at[:, there]),
-        (mean_loss, loss_out),
-    ]
-    for n, move in enumerate(more):
-        moves.append(pltpu.make_async_copy(*move, leaves.at[n + 2]))
-        moves[-1].start()
+    moves.append(pltpu.make_async_copy(mean_loss, loss_out, leaves.at[2]))
+    moves[-1].start()
     for move in moves:
         move.wait()
 
@@ -492,11 +495,14 @@
 
     latent_there, send, pair_grad = half_back(True, pair_grad)
     latent_here, keep = half_back(False, pair_grad)
-    (mean_loss,) = call(
-        functools.partial(loss_kernel, variables, 1.0 / (members * variables * cells_all)),
-        [shape(1, 1)],
-        grads,
-    )
+    mean_loss, latent_out = pl.pallas_call(
+        functools.partial(loss_kernel, members, variables, 1.0 / (members * variables * cells_all)),
+        out_shape=[shape(1, 1), shape(rows, hidden, dtype=BF16)],
+        in_specs=[VMEM] * (2 + bands),
+        out_specs=[VMEM, HBM],
+        scratch_shapes=[pltpu.SemaphoreType.DMA((2,))],
+        compiler_params=PARAMS,
+    )(latent_here, latent_there, *grads)
     total = keep + swap(send, "member", 1)
     step = 2
     while step < members:
@@ -515,16 +521,15 @@
             total = total + (far[0] + far[1])
         step *= 4
     other = swap(total, "member", 1)
-    latent_out, proj_grad, coef_grad, loss_out = call(
+    proj_grad, coef_grad, loss_out = call(
         functools.partial(write_kernel, members, bands),
         [
-            shape(rows, hidden, dtype=BF16),
             shape(variables, hidden),
             shape(table, hidden),
             shape(1, 1),
         ],
-        (total, latent_here, latent_there, mean_loss),
-        [pltpu.VMEM((variables, half), F32), pltpu.SemaphoreType.DMA((5,))],
+        (total, mean_loss),
+        [pltpu.VMEM((variables, half), F32), pltpu.SemaphoreType.DMA((3,))],
         sink=HBM,
     )
     proj_grad, coef_grad = pl.pallas_call(

time: 42.4 us -> 42.2 us (level)
    pallas_call x0 -> x1, Pallas kernels: none -> 1.19 us  [local(): pl.pallas_call(functools.partial(loss_kernel, members, variables, 1.0 / (...]
    pallas_call x10 -> x9, Pallas kernels: 11.6 us -> 10.6 us  [call(): pl.pallas_call(kernel, out_shape=outs, in_specs=[source] * len(operands),...]
    ppermute x13, waiting for transfers between devices: 10.4 us -> 9.98 us  [cross(): return lax.ppermute(shard, ('member', 'band'), pairs)]
  transfers between devices with their start and end apart: 17 -> 17, of which waited for: 8 -> 8; matrix products, arithmetic and copies ran while one was open for 0% -> 0% of each run, Pallas kernels for 16% -> 17%
where the time goes in v9:
time: 42.2 us; the launch traced here: 42 us
  starting transfers between devices  17.8 us (42%)
  Pallas kernels  12.5 us (30%)
  waiting for transfers between devices  10.9 us (26%)
  between operations  0.75 us (2%)
    ppermute x13, starting transfers between devices, cross(): return lax.ppermute(shard, ('member', 'band'), pairs)  16.7 us
    pallas_call x9, Pallas kernels, call(): pl.pallas_call(kernel, out_shape=outs, in_specs=[source] * len(operands),...  10.6 us
    ppermute x13, waiting for transfers between devices, cross(): return lax.ppermute(shard, ('member', 'band'), pairs)  9.98 us
    pallas_call x1, Pallas kernels, local(): pl.pallas_call(functools.partial(loss_kernel, members, variables, 1.0 / (...  1.19 us
    ppermute x4, starting transfers between devices, swap(): return lax.ppermute(shard, axis, [(i, i ^ mask) for i in range(peers)])  1.11 us
    ppermute x4, waiting for transfers between devices, swap(): return lax.ppermute(shard, axis, [(i, i ^ mask) for i in range(peers)])  0.92 us
  transfers between devices with their start and end apart: 17, of which 8 were waited for; matrix products, arithmetic and copies ran while one was open for 0% of the time, Pallas kernels for 17%

profile of v9, /device:TPU:0, one launch (start us, length us, event | category | flops | bytes accessed | tf_op | source)
XLA Modules:
  0.0 42.0 jit_solution(18382325939447992601)
XLA Ops:
  0.6 2.6 %shard_map.120 = (f32[80,128]{1,0:T(8,128)S(1)}, f32[80,128]{1,0:T(8,128)S(1)}, f32[80,128]{1,0:T(8,128)S(1)}, f32[80,128]{1,0:T(8,128)S(1)}, bf16[25,1024]{1,0:...) custom-call(bf16[64,1024]{1,0:T(8,128)(2,1)} %bitcast.5, ...), custom_call_target="tpu_custom_call" | custom-call | bytes 1048576 | tf_op jit(solution)/shard_map/pallas_call | solution.py:371
  3.3 4.6 %collective-permute-start = (f32[80,128]{1,0:T(8,128)S(1)}, f32[80,128]{1,0:T(8,128)S(1)}, u32[]{:S(2)}, u32[]{:S(2)}) collective-permute-start(f32[80,128]{1,0:T(8,128)S(1)} %get-tuple-element.36), channel_id=1, source_target_pairs={{0,7},{1,6},{2,5},{3,4},{4,3},{5,2},{6,1},{7,0},{8,15},{9,14},{10,... | collective-permute-start | bytes 122888 | tf_op jit(solution)/shard_map/ppermute | solution.py:34
  7.8 0.0 collective-permute-start.1
  7.8 0.9 %collective-permute-start.2 = (f32[80,128]{1,0:T(8,128)S(1)}, f32[80,128]{1,0:T(8,128)S(1)}, u32[]{:S(2)}, u32[]{:S(2)}) collective-permute-start(f32[80,128]{1,0:T(8,128)S(1)} %get-tuple-element.38), channel_id=1, source_target_pairs={{0,5},{1,4},{2,7},{3,6},{4,1},{5,0},{6,3},{7,2},{8,13},{9,12},{10,... | collective-permute-start | bytes 122888 | tf_op jit(solution)/shard_map/ppermute | solution.py:34
  8.8 0.0 collective-permute-start.3
  8.8 1.0 %collective-permute-done.refs_0_ = f32[80,128]{1,0:T(8,128)S(1)} collective-permute-done((f32[80,128]{1,0:T(8,128)S(1)}, f32[80,128]{1,0:T(8,128)S(1)}, u32[]{:S(2)}, u32[]{:S(2)}) %collective-permute-start) | collective-permute-done | bytes 40992 | tf_op jit(solution)/shard_map/ppermute | solution.py:34
  9.8 2.8 %collective-permute-done.1.refs_1_ = f32[80,128]{1,0:T(8,128)S(1)} collective-permute-done((f32[80,128]{1,0:T(8,128)S(1)}, f32[80,128]{1,0:T(8,128)S(1)}, u32[]{:S(2)}, u32[]{:S(2)}) %collective-permute-start.1) | collective-permute-done | bytes 40992 | tf_op jit(solution)/shard_map/ppermute | solution.py:34
  12.5 0.0 collective-permute-done.2.refs_2_
  12.5 0.0 collective-permute-done.3.refs_3_
  12.6 0.4 shard_map.121.refs_0_
  12.9 1.4 %collective-permute-start.4 = (f32[32,256]{1,0:T(8,128)S(1)}, f32[32,256]{1,0:T(8,128)S(1)}, u32[]{:S(2)}, u32[]{:S(2)}) collective-permute-start(f32[32,256]{1,0:T(8,128)S(1)} %shard_map.121.refs_0_), channel_id=1, source_target_pairs={{0,12},{1,13},{2,14},{3,15},{4,8},{5,9},{6,10},{7,11},{8,4},{9,5},... | collective-permute-start | bytes 98312 | tf_op jit(solution)/shard_map/ppermute | solution.py:34
  14.4 0.2 collective-permute-start.5
  14.6 1.3 %shard_map.122.counts = bf16[1024,1024]{1,0:T(8,128)(2,1)S(1)} custom-call(s32[4,1,384]{2,1,0:T(1,128)S(1)} %get-tuple-element.41.pair_ids, f32[80,128]{1,0:T(8,128)S(1)} %collective-permute-done.refs_0_, f32[80,128]{1,0:T(8,128)S(1)} %collective-permute-done.1.refs_1_, f32[80,128]{1,0:T(8,128)S(1)} %collective-permute-done.2.refs_2_, ...), custom_call_target="tpu_custom_call" | custom-call | flops 805306368 | bytes 1048576 | tf_op jit(solution)/shard_map/pallas_call | solution.py:371
  15.9 0.4 %collective-permute-done.4.refs_3_ = f32[32,256]{1,0:T(8,128)S(1)} collective-permute-done((f32[32,256]{1,0:T(8,128)S(1)}, f32[32,256]{1,0:T(8,128)S(1)}, u32[]{:S(2)}, u32[]{:S(2)}) %collective-permute-start.4) | collective-permute-done | bytes 32800 | tf_op jit(solution)/shard_map/ppermute | solution.py:34
  16.3 0.3 collective-permute-start.6
  16.6 0.0 collective-permute-done.5.refs_1_
  16.6 0.9 %collective-permute-done.6.refs_2_ = f32[32,256]{1,0:T(8,128)S(1)} collective-permute-done((f32[32,256]{1,0:T(8,128)S(1)}, f32[32,256]{1,0:T(8,128)S(1)}, u32[]{:S(2)}, u32[]{:S(2)}) %collective-permute-start.6) | collective-permute-done | bytes 32800 | tf_op jit(solution)/shard_map/ppermute | solution.py:24
  17.5 0.3 shard_map.123
  17.8 0.4 collective-permute-start.8
  18.2 2.2 %collective-permute-start.7 = (bf16[32,256]{1,0:T(8,128)(2,1)S(1)}, bf16[32,256]{1,0:T(8,128)(2,1)S(1)}, u32[]{:S(2)}, u32[]{:S(2)}) collective-permute-start(bf16[32,256]{1,0:T(8,128)(2,1)S(1)} %shard_map.123), channel_id=1, source_target_pairs={{0,7},{1,6},{2,5},{3,4},{4,3},{5,2},{6,1},{7,0},{8,15},{9,14},{10,... | collective-permute-start | bytes 49160 | tf_op jit(solution)/shard_map/ppermute | solution.py:34
  20.4 0.3 collective-permute-start.9
  20.7 1.4 %collective-permute-start.10 = (bf16[32,256]{1,0:T(8,128)(2,1)S(1)}, bf16[32,256]{1,0:T(8,128)(2,1)S(1)}, u32[]{:S(2)}, u32[]{:S(2)}) collective-permute-start(bf16[32,256]{1,0:T(8,128)(2,1)S(1)} %shard_map.123), channel_id=1, source_target_pairs={{0,6},{1,7},{2,4},{3,5},{4,2},{5,3},{6,0},{7,1},{8,14},{9,15},{10,... | collective-permute-start | bytes 49160 | tf_op jit(solution)/shard_map/ppermute | solution.py:34
  22.1 0.0 collective-permute-done.8.grad.refs_2_.refs_0_
  22.1 0.0 copy-start
  22.1 0.0 copy-start.1
  22.1 1.0 %shard_map.124 = (f32[32,1024]{1,0:T(8,128)S(1)}, f32[1024,1024]{1,0:T(8,128)S(1)}) custom-call(bf16[32,1024]{1,0:T(8,128)(2,1)S(1)} %get-tuple-element.35.proj, bf16[1024,1024]{1,0:T(8,128)(2,1)S(1)} %shard_map.122.counts, bf16[32,256]{1,0:T(8,128)(2,1)S(1)} %collective-permute-done.8.grad.refs_2_.refs_0_), custom_call_target="tpu_custom_call" | custom-call | flops 536870912 | bytes 1048576 | tf_op jit(solution)/shard_map/pallas_call | solution.py:371
  23.1 0.0 collective-permute-done.7.grad.refs_5_.refs_3_
  23.2 1.0 %shard_map.125 = (f32[32,1024]{1,0:T(8,128)S(1)}, f32[1024,1024]{1,0:T(8,128)S(1)}) custom-call(bf16[32,1024]{1,0:T(8,128)(2,1)S(1)} %get-tuple-element.35.proj, bf16[1024,1024]{1,0:T(8,128)(2,1)S(1)} %shard_map.122.counts, bf16[32,256]{1,0:T(8,128)(2,1)S(1)} %collective-permute-done.7.grad.refs_5_.refs_3_, f32[32,1024]{1,0:T(8,128)S(1)} %get-tuple-element.48.refs_0_, ...), custom_call_target="tpu_custom_call" | custom-call | flops 536870912 | bytes 1048576 | tf_op jit(solution)/shard_map/pallas_call | solution.py:371
  24.2 0.0 collective-permute-done.9.refs_3_.refs_1_
  24.2 0.6 %collective-permute-done.10.refs_4_.refs_2_ = bf16[32,256]{1,0:T(8,128)(2,1)S(1)} collective-permute-done((bf16[32,256]{1,0:T(8,128)(2,1)S(1)}, bf16[32,256]{1,0:T(8,128)(2,1)S(1)}, u32[]{:S(2)}, u32[]{:S(2)}) %collective-permute-start.10) | collective-permute-done | bytes 16416 | tf_op jit(solution)/shard_map/ppermute | solution.py:34
  24.8 0.0 copy-done
  24.8 0.0 copy-done.1
  24.8 1.5 %shard_map.126 = (bf16[64,512]{1,0:T(8,128)(2,1)S(1)}, f32[48,512]{1,0:T(8,128)S(1)}, f32[32,1024]{1,0:T(8,128)S(1)}) custom-call(bf16[64,1024]{1,0:T(8,128)(2,1)S(1)} %bitcast.6, bf16[16,1024]{1,0:T(8,128)(2,1)S(1)} %copy-done.1, bf16[32,1024]{1,0:T(8,128)(2,1)S(1)} %get-tuple-element.35.proj, bf16[1024,1024]{1,0:T(8,128)(2,1)S(1)} %shard_map.122.counts, ...), custom_call_target="tpu_custom_call" | custom-call | flops 1073741824 | bytes 1048576 | tf_op jit(solution)/shard_map/pallas_call | solution.py:371
  26.3 0.4 collective-permute-start.11
  26.8 1.3 %shard_map.127 = (bf16[64,512]{1,0:T(8,128)(2,1)S(1)}, f32[48,512]{1,0:T(8,128)S(1)}) custom-call(bf16[64,1024]{1,0:T(8,128)(2,1)S(1)} %bitcast.7, bf16[16,1024]{1,0:T(8,128)(2,1)S(1)} %copy-done.1, bf16[32,1024]{1,0:T(8,128)(2,1)S(1)} %get-tuple-element.35.proj, bf16[1024,1024]{1,0:T(8,128)(2,1)S(1)} %shard_map.122.counts, ...), custom_call_target="tpu_custom_call" | custom-call | flops 1073741824 | bytes 1048576 | tf_op jit(solution)/shard_map/pallas_call | solution.py:371
  28.0 0.0 collective-permute-done.11
  28.1 1.3 %collective-permute-start.12 = (bf16[48,512]{1,0:T(8,128)(2,1)S(1)}, bf16[48,512]{1,0:T(8,128)(2,1)S(1)}, u32[]{:S(2)}, u32[]{:S(2)}) collective-permute-start(bf16[48,512]{1,0:T(8,128)(2,1)S(1)} %add_convert_fusion.1), channel_id=1, source_target_pairs={{0,12},{1,13},{2,14},{3,15},{4,8},{5,9},{6,10},{7,11},{8,4},{9,5},... | collective-permute-start | bytes 147464 | tf_op jit(solution)/shard_map/ppermute | solution.py:34
  29.4 1.2 %shard_map.128 = (f32[1,1]{1,0:T(1,128)}, bf16[64,1024]{1,0:T(8,128)(2,1)}) custom-call(bf16[64,512]{1,0:T(8,128)(2,1)S(1)} %get-tuple-element.53.latent_here, bf16[64,512]{1,0:T(8,128)(2,1)S(1)} %get-tuple-element.54.latent_there, bf16[32,256]{1,0:T(8,128)(2,1)S(1)} %collective-permute-done.8.grad.refs_2_.refs_0_, ...), custom_call_target="tpu_custom_call" | custom-call | tf_op jit(solution)/shard_map/pallas_call | solution.py:498
  30.6 1.3 %collective-permute-done.12 = bf16[48,512]{1,0:T(8,128)(2,1)S(1)} collective-permute-done((bf16[48,512]{1,0:T(8,128)(2,1)S(1)}, bf16[48,512]{1,0:T(8,128)(2,1)S(1)}, u32[]{:S(2)}, u32[]{:S(2)}) %collective-permute-start.12) | collective-permute-done | bytes 49184 | tf_op jit(solution)/shard_map/ppermute | solution.py:34
  31.9 1.8 %collective-permute-start.15 = (bf16[48,512]{1,0:T(8,128)(2,1)S(1)}, bf16[48,512]{1,0:T(8,128)(2,1)S(1)}, u32[]{:S(2)}, u32[]{:S(2)}) collective-permute-start(bf16[48,512]{1,0:T(8,128)(2,1)S(1)} %add_convert_fusion), channel_id=1, source_target_pairs={{0,3},{1,2},{2,1},{3,0},{4,7},{5,6},{6,5},{7,4},{8,11},{9,10},{10,... | collective-permute-start | bytes 147464 | tf_op jit(solution)/shard_map/ppermute | solution.py:34
  33.7 0.6 %collective-permute-start.14 = (bf16[48,512]{1,0:T(8,128)(2,1)S(1)}, bf16[48,512]{1,0:T(8,128)(2,1)S(1)}, u32[]{:S(2)}, u32[]{:S(2)}) collective-permute-start(bf16[48,512]{1,0:T(8,128)(2,1)S(1)} %add_convert_fusion), channel_id=1, source_target_pairs={{0,6},{1,7},{2,4},{3,5},{4,2},{5,3},{6,0},{7,1},{8,14},{9,15},{10,... | collective-permute-start | bytes 147464 | tf_op jit(solution)/shard_map/ppermute | solution.py:34
  34.3 1.8 %collective-permute-start.13 = (bf16[48,512]{1,0:T(8,128)(2,1)S(1)}, bf16[48,512]{1,0:T(8,128)(2,1)S(1)}, u32[]{:S(2)}, u32[]{:S(2)}) collective-permute-start(bf16[48,512]{1,0:T(8,128)(2,1)S(1)} %add_convert_fusion), channel_id=1, source_target_pairs={{0,5},{1,4},{2,7},{3,6},{4,1},{5,0},{6,3},{7,2},{8,13},{9,12},{10,... | collective-permute-start | bytes 147464 | tf_op jit(solution)/shard_map/ppermute | solution.py:34
  36.1 2.3 %collective-permute-done.15 = bf16[48,512]{1,0:T(8,128)(2,1)S(1)} collective-permute-done((bf16[48,512]{1,0:T(8,128)(2,1)S(1)}, bf16[48,512]{1,0:T(8,128)(2,1)S(1)}, u32[]{:S(2)}, u32[]{:S(2)}) %collective-permute-start.15) | collective-permute-done | bytes 49184 | tf_op jit(solution)/shard_map/ppermute | solution.py:34
  38.4 1.5 %collective-permute-done.14 = bf16[48,512]{1,0:T(8,128)(2,1)S(1)} collective-permute-done((bf16[48,512]{1,0:T(8,128)(2,1)S(1)}, bf16[48,512]{1,0:T(8,128)(2,1)S(1)}, u32[]{:S(2)}, u32[]{:S(2)}) %collective-permute-start.14) | collective-permute-done | bytes 49184 | tf_op jit(solution)/shard_map/ppermute | solution.py:34
  39.9 0.0 collective-permute-done.13
  39.9 0.2 collective-permute-start.16
  40.1 1.2 %shard_map.129 = (f32[25,1024]{1,0:T(8,128)}, f32[16,1024]{1,0:T(8,128)}, f32[1,1]{1,0:T(1,128)}) custom-call(f32[48,512]{1,0:T(8,128)S(1)} %add_add_fusion.summed, f32[1,1]{1,0:T(1,128)} %get-tuple-element.60.mean_loss), custom_call_target="tpu_custom_call" | custom-call | bytes 1048576 | tf_op jit(solution)/shard_map/pallas_call | solution.py:371
  41.3 0.0 collective-permute-done.16.summed
  41.3 0.7 %shard_map.130 = (f32[25,1024]{1,0:T(8,128)}, f32[16,1024]{1,0:T(8,128)}) custom-call(f32[25,1024]{1,0:T(8,128)} %get-tuple-element.61.proj_in, f32[16,1024]{1,0:T(8,128)} %get-tuple-element.62.coef_in, f32[48,512]{1,0:T(8,128)S(1)} %collective-permute-done.16.summed), custom_call_target="tpu_custom_call", output_to_operand_aliasing={{0}: (0, {}), {1}: (1, {})} | custom-call | tf_op jit(solution)/shard_map/pallas_call | solution.py:535
  (3 shorter events, 0.1 us)
Async XLA Ops:
  3.3 6.5 %collective-permute-start = (f32[80,128]{1,0:T(8,128)S(1)}, f32[80,128]{1,0:T(8,128)S(1)}, u32[]{:S(2)}, u32[]{:S(2)}) collective-permute-start(f32[80,128]{1,0:T(8,128)S(1)} %get-tuple-element.36), channel_id=1, source_target_pairs={{0,7},{1,6},{2,5},{3,4},{4,3},{5,2},{6,1},{7,0},{8,15},{9,14},{10,... | collective-permute-start | bytes 122888 | tf_op jit(solution)/shard_map/ppermute | solution.py:34
  7.8 4.7 %collective-permute-start.1 = (f32[80,128]{1,0:T(8,128)S(1)}, f32[80,128]{1,0:T(8,128)S(1)}, u32[]{:S(2)}, u32[]{:S(2)}) collective-permute-start(f32[80,128]{1,0:T(8,128)S(1)} %get-tuple-element.37), channel_id=1, source_target_pairs={{0,6},{1,7},{2,4},{3,5},{4,2},{5,3},{6,0},{7,1},{8,14},{9,15},{10,... | collective-permute-start | bytes 122888 | tf_op jit(solution)/shard_map/ppermute | solution.py:34
  7.8 4.7 %collective-permute-start.2 = (f32[80,128]{1,0:T(8,128)S(1)}, f32[80,128]{1,0:T(8,128)S(1)}, u32[]{:S(2)}, u32[]{:S(2)}) collective-permute-start(f32[80,128]{1,0:T(8,128)S(1)} %get-tuple-element.38), channel_id=1, source_target_pairs={{0,5},{1,4},{2,7},{3,6},{4,1},{5,0},{6,3},{7,2},{8,13},{9,12},{10,... | collective-permute-start | bytes 122888 | tf_op jit(solution)/shard_map/ppermute | solution.py:34
  8.8 3.8 %collective-permute-start.3 = (f32[80,128]{1,0:T(8,128)S(1)}, f32[80,128]{1,0:T(8,128)S(1)}, u32[]{:S(2)}, u32[]{:S(2)}) collective-permute-start(f32[80,128]{1,0:T(8,128)S(1)} %get-tuple-element.39), channel_id=1, source_target_pairs={{0,4},{1,5},{2,6},{3,7},{4,0},{5,1},{6,2},{7,3},{8,12},{9,13},{10,... | collective-permute-start | bytes 122888 | tf_op jit(solution)/shard_map/ppermute | solution.py:34
  12.9 3.4 %collective-permute-start.4 = (f32[32,256]{1,0:T(8,128)S(1)}, f32[32,256]{1,0:T(8,128)S(1)}, u32[]{:S(2)}, u32[]{:S(2)}) collective-permute-start(f32[32,256]{1,0:T(8,128)S(1)} %shard_map.121.refs_0_), channel_id=1, source_target_pairs={{0,12},{1,13},{2,14},{3,15},{4,8},{5,9},{6,10},{7,11},{8,4},{9,5},... | collective-permute-start | bytes 98312 | tf_op jit(solution)/shard_map/ppermute | solution.py:34
  14.4 2.2 %collective-permute-start.5 = (f32[32,256]{1,0:T(8,128)S(1)}, f32[32,256]{1,0:T(8,128)S(1)}, u32[]{:S(2)}, u32[]{:S(2)}) collective-permute-start(f32[32,256]{1,0:T(8,128)S(1)} %shard_map.121.refs_0_), channel_id=1, source_target_pairs={{0,4},{4,0},{8,12},{12,8},{1,5},{5,1},{9,13},{13,9},{2,6},{6,2},{1... | collective-permute-start | bytes 98312 | tf_op jit(solution)/shard_map/ppermute | solution.py:24
  16.3 1.2 %collective-permute-start.6 = (f32[32,256]{1,0:T(8,128)S(1)}, f32[32,256]{1,0:T(8,128)S(1)}, u32[]{:S(2)}, u32[]{:S(2)}) collective-permute-start(f32[32,256]{1,0:T(8,128)S(1)} %collective-permute-done.4.refs_3_), channel_id=1, source_target_pairs={{0,4},{4,0},{8,12},{12,8},{1,5},{5,1},{9,13},{13,9},{2,6},{6,2},{1... | collective-permute-start | bytes 98312 | tf_op jit(solution)/shard_map/ppermute | solution.py:24
  17.8 4.3 %collective-permute-start.8 = (bf16[32,256]{1,0:T(8,128)(2,1)S(1)}, bf16[32,256]{1,0:T(8,128)(2,1)S(1)}, u32[]{:S(2)}, u32[]{:S(2)}) collective-permute-start(bf16[32,256]{1,0:T(8,128)(2,1)S(1)} %shard_map.123), channel_id=1, source_target_pairs={{0,4},{1,5},{2,6},{3,7},{4,0},{5,1},{6,2},{7,3},{8,12},{9,13},{10,... | collective-permute-start | bytes 49160 | tf_op jit(solution)/shard_map/ppermute | solution.py:34
  18.2 5.0 %collective-permute-start.7 = (bf16[32,256]{1,0:T(8,128)(2,1)S(1)}, bf16[32,256]{1,0:T(8,128)(2,1)S(1)}, u32[]{:S(2)}, u32[]{:S(2)}) collective-permute-start(bf16[32,256]{1,0:T(8,128)(2,1)S(1)} %shard_map.123), channel_id=1, source_target_pairs={{0,7},{1,6},{2,5},{3,4},{4,3},{5,2},{6,1},{7,0},{8,15},{9,14},{10,... | collective-permute-start | bytes 49160 | tf_op jit(solution)/shard_map/ppermute | solution.py:34
  20.4 3.7 %collective-permute-start.9 = (bf16[32,256]{1,0:T(8,128)(2,1)S(1)}, bf16[32,256]{1,0:T(8,128)(2,1)S(1)}, u32[]{:S(2)}, u32[]{:S(2)}) collective-permute-start(bf16[32,256]{1,0:T(8,128)(2,1)S(1)} %shard_map.123), channel_id=1, source_target_pairs={{0,5},{1,4},{2,7},{3,6},{4,1},{5,0},{6,3},{7,2},{8,13},{9,12},{10,... | collective-permute-start | bytes 49160 | tf_op jit(solution)/shard_map/ppermute | solution.py:34
  20.7 4.1 %collective-permute-start.10 = (bf16[32,256]{1,0:T(8,128)(2,1)S(1)}, bf16[32,256]{1,0:T(8,128)(2,1)S(1)}, u32[]{:S(2)}, u32[]{:S(2)}) collective-permute-start(bf16[32,256]{1,0:T(8,128)(2,1)S(1)} %shard_map.123), channel_id=1, source_target_pairs={{0,6},{1,7},{2,4},{3,5},{4,2},{5,3},{6,0},{7,1},{8,14},{9,15},{10,... | collective-permute-start | bytes 49160 | tf_op jit(solution)/shard_map/ppermute | solution.py:34
  22.1 2.7 %copy-start = (bf16[1,64,1024]{2,1,0:T(8,128)(2,1)S(1)}, bf16[1,64,1024]{2,1,0:T(8,128)(2,1)}, u32[]{:S(2)}) copy-start(bf16[1,64,1024]{2,1,0:T(8,128)(2,1)} %param.9) | copy-start | bytes 393220
  22.1 2.7 %copy-start.1 = (bf16[16,1024]{1,0:T(8,128)(2,1)S(1)}, bf16[16,1024]{1,0:T(8,128)(2,1)}, u32[]{:S(2)}) copy-start(bf16[16,1024]{1,0:T(8,128)(2,1)} %coef.3) | copy-start | bytes 98308
  26.3 1.7 %collective-permute-start.11 = (f32[48,512]{1,0:T(8,128)S(1)}, f32[48,512]{1,0:T(8,128)S(1)}, u32[]{:S(2)}, u32[]{:S(2)}) collective-permute-start(f32[48,512]{1,0:T(8,128)S(1)} %get-tuple-element.57), channel_id=1, source_target_pairs={{0,4},{4,0},{8,12},{12,8},{1,5},{5,1},{9,13},{13,9},{2,6},{6,2},{1... | collective-permute-start | bytes 294920 | tf_op jit(solution)/shard_map/ppermute | solution.py:24
  28.1 3.8 %collective-permute-start.12 = (bf16[48,512]{1,0:T(8,128)(2,1)S(1)}, bf16[48,512]{1,0:T(8,128)(2,1)S(1)}, u32[]{:S(2)}, u32[]{:S(2)}) collective-permute-start(bf16[48,512]{1,0:T(8,128)(2,1)S(1)} %add_convert_fusion.1), channel_id=1, source_target_pairs={{0,12},{1,13},{2,14},{3,15},{4,8},{5,9},{6,10},{7,11},{8,4},{9,5},... | collective-permute-start | bytes 147464 | tf_op jit(solution)/shard_map/ppermute | solution.py:34
  31.9 6.5 %collective-permute-start.15 = (bf16[48,512]{1,0:T(8,128)(2,1)S(1)}, bf16[48,512]{1,0:T(8,128)(2,1)S(1)}, u32[]{:S(2)}, u32[]{:S(2)}) collective-permute-start(bf16[48,512]{1,0:T(8,128)(2,1)S(1)} %add_convert_fusion), channel_id=1, source_target_pairs={{0,3},{1,2},{2,1},{3,0},{4,7},{5,6},{6,5},{7,4},{8,11},{9,10},{10,... | collective-permute-start | bytes 147464 | tf_op jit(solution)/shard_map/ppermute | solution.py:34
  33.7 6.1 %collective-permute-start.14 = (bf16[48,512]{1,0:T(8,128)(2,1)S(1)}, bf16[48,512]{1,0:T(8,128)(2,1)S(1)}, u32[]{:S(2)}, u32[]{:S(2)}) collective-permute-start(bf16[48,512]{1,0:T(8,128)(2,1)S(1)} %add_convert_fusion), channel_id=1, source_target_pairs={{0,6},{1,7},{2,4},{3,5},{4,2},{5,3},{6,0},{7,1},{8,14},{9,15},{10,... | collective-permute-start | bytes 147464 | tf_op jit(solution)/shard_map/ppermute | solution.py:34
  34.3 5.5 %collective-permute-start.13 = (bf16[48,512]{1,0:T(8,128)(2,1)S(1)}, bf16[48,512]{1,0:T(8,128)(2,1)S(1)}, u32[]{:S(2)}, u32[]{:S(2)}) collective-permute-start(bf16[48,512]{1,0:T(8,128)(2,1)S(1)} %add_convert_fusion), channel_id=1, source_target_pairs={{0,5},{1,4},{2,7},{3,6},{4,1},{5,0},{6,3},{7,2},{8,13},{9,12},{10,... | collective-permute-start | bytes 147464 | tf_op jit(solution)/shard_map/ppermute | solution.py:34
  39.9 1.4 %collective-permute-start.16 = (f32[48,512]{1,0:T(8,128)S(1)}, f32[48,512]{1,0:T(8,128)S(1)}, u32[]{:S(2)}, u32[]{:S(2)}) collective-permute-start(f32[48,512]{1,0:T(8,128)S(1)} %add_add_fusion.summed), channel_id=1, source_target_pairs={{0,4},{4,0},{8,12},{12,8},{1,5},{5,1},{9,13},{13,9},{2,6},{6,2},{1... | collective-permute-start | bytes 294920 | tf_op jit(solution)/shard_map/ppermute | solution.py:24
